TPU v7x, 128 devices: a whole 4x4x4 slice. The times are simulated.
128 devices in a mesh: gx: 8 (over x, y_lo), gy: 16 (over y_hi, z, core).
Axes of the slice: x: 4, y: 4 (y_hi: 2, y_lo: 2; y = y_hi * 2 + y_lo), z: 4, core: 2. Of those that a mesh axis runs over, the one named last changes fastest.
Arguments:
- coarse_velocity: float32 [3, 32, 256, 128], P(None, 'gx', 'gy'), may hold values from -6 to 6
- coarse_stress: float32 [6, 32, 256, 128], P(None, 'gx', 'gy'), may hold values from -6 to 6
- coarse_material: float32 [3, 32, 256, 128], P(None, 'gx', 'gy'), may hold values from 0.5 to 2
- fine_velocity: float32 [3, 96, 384, 256], P(None, 'gx', 'gy'), may hold values from -6 to 6
- fine_stress: float32 [6, 96, 384, 256], P(None, 'gx', 'gy'), may hold values from -6 to 6
- fine_material: float32 [3, 96, 384, 256], P(None, 'gx', 'gy'), may hold values from 0.5 to 2
- fault_slip: float32 [96, 384], P('gx', 'gy'), may hold values from 0 to 0.5
- initial_shear: float32 [96, 384], P('gx', 'gy'), may hold values from -6 to 6
- normal_stress: float32 [96, 384], P('gx', 'gy'), may hold values from 0.5 to 2.5
- fault_mask: int32 [96, 384], P('gx', 'gy'), may hold values 0 or 1
- zone_ids: int32 [96, 384], P('gx', 'gy'), may hold values from 0 to 3
- static_friction: float32 [4], replicated, may hold values from 0.5 to 0.8
- friction_drop: float32 [4], replicated, may hold values from 0.1 to 0.4
- weakening_distance: float32 [4], replicated, may hold values from 0.05 to 0.5
- owner_rows: int32 [2, 32, 128], P(None, 'gx'), may hold values from 85 to 171, as said below
Outputs:
- coarse_velocity_next: float32 [3, 32, 256, 128], P(None, 'gx', 'gy')
- coarse_stress_next: float32 [6, 32, 256, 128], P(None, 'gx', 'gy')
- fine_velocity_next: float32 [3, 96, 384, 256], P(None, 'gx', 'gy')
- fine_stress_next: float32 [6, 96, 384, 256], P(None, 'gx', 'gy')
- fault_slip_next: float32 [96, 384], P('gx', 'gy')
Inputs may be any that keep to these rules, and one draw needn't show every extreme that they name: owner_rows[0] lies within one row of 86 and owner_rows[1] within one row of 170; both ends of both ranges are taken.
All inputs are finite; a program needn't handle non-finite values. No bound on the sum of `fault_mask` on one device may be relied on, other than what follows from the above.
Results may differ from a plain program's by a relative error of at most 0.00002.
Values sent between devices are 32-bit elements; how exact they have to be, the bound alone decides.
No kernel may reach another device: no remote copies, remote signals or barrier semaphores. Data moves between devices by JAX's collectives and lax.ppermute only.
A program may use at most 128 MiB of HBM per device.

v0:
```python
import jax
import jax.numpy as jnp
from jax import lax
from jax.sharding import PartitionSpec as P

STEP_RATIO = 0.15


def from_behind(value, axis, steps):
    count = lax.axis_size(axis)
    first, last = (max(0, -steps), min(count, count - steps))
    return lax.ppermute(value, axis, [(source, source + steps) for source in range(first, last)])


def shifted(values, along, forward):
    length = values.shape[along]
    edge = jnp.zeros_like(lax.slice_in_dim(values, 0, 1, axis=along))
    if forward:
        return jnp.concatenate([lax.slice_in_dim(values, 1, length, axis=along), edge], axis=along)
    return jnp.concatenate([edge, lax.slice_in_dim(values, 0, length - 1, axis=along)], axis=along)


def back_diff(values, along):
    return values - shifted(values, along, False)


def fore_diff(values, along):
    return shifted(values, along, True) - values


def trimmed(stacked, margin):
    return stacked[:, margin:-margin, margin:-margin]


def velocity_step(velocity, source, material, directions, margin):
    along_x, along_y, along_z = directions
    force_x = (
        back_diff(source[0], along_x)
        + back_diff(source[3], along_y)
        + back_diff(source[4], along_z)
    )
    force_y = (
        back_diff(source[3], along_x)
        + back_diff(source[1], along_y)
        + back_diff(source[5], along_z)
    )
    force_z = (
        back_diff(source[4], along_x)
        + back_diff(source[5], along_y)
        + back_diff(source[2], along_z)
    )
    forces = trimmed(jnp.stack([force_x, force_y, force_z]), margin)
    return velocity + STEP_RATIO * material[0] * forces


def stress_step(stress, source, material, directions, margin):
    along_x, along_y, along_z = directions
    strain = jnp.stack(
        [
            fore_diff(source[0], along_x),
            fore_diff(source[1], along_y),
            fore_diff(source[2], along_z),
            fore_diff(source[0], along_y) + fore_diff(source[1], along_x),
            fore_diff(source[0], along_z) + fore_diff(source[2], along_x),
            fore_diff(source[1], along_z) + fore_diff(source[2], along_y),
        ]
    )
    strain = trimmed(strain, margin)
    dilation = strain[0] + strain[1] + strain[2]
    lame_first = material[1]
    shear_modulus = material[2]
    update = jnp.stack(
        [
            lame_first * dilation + 2.0 * shear_modulus * strain[0],
            lame_first * dilation + 2.0 * shear_modulus * strain[1],
            lame_first * dilation + 2.0 * shear_modulus * strain[2],
            shear_modulus * strain[3],
            shear_modulus * strain[4],
            shear_modulus * strain[5],
        ]
    )
    return stress + STEP_RATIO * update


def friction_step(stress, slip_state, settings):
    active, shear_start, normal_load, static_part, drop_part, inverse_distance = settings
    centre = stress.shape[3] // 2
    shear_plane = stress[3, :, :, centre]
    traction = shear_plane + shear_start
    weakened = jnp.minimum(slip_state * inverse_distance, 1.0)
    strength = normal_load * (static_part - drop_part * weakened)
    resisted = jnp.clip(traction, -strength, strength)
    slip_state = slip_state + active * STEP_RATIO * jnp.abs(traction - resisted)
    stress = stress.at[3, :, :, centre].set(shear_plane + active * (resisted - traction))
    return (stress, slip_state)


def with_bounds(velocity, bounds):
    velocity = velocity.at[:, :, :, 0].set(bounds[0])
    return velocity.at[:, :, :, -1].set(bounds[1])


def fault_settings(
    fault_mask,
    initial_shear,
    normal_stress,
    zone_ids,
    static_friction,
    friction_drop,
    weakening_distance,
):
    zone_count = static_friction.shape[0]
    onehot = (
        zone_ids[:, :, None] == jnp.arange(zone_count, dtype=jnp.int32)[None, None, :]
    ).astype(jnp.float32)
    static_part = jnp.sum(onehot * static_friction, axis=2)
    drop_part = jnp.sum(onehot * friction_drop, axis=2)
    inverse_distance = jnp.sum(onehot * (1.0 / weakening_distance), axis=2)
    return (
        fault_mask.astype(jnp.float32),
        initial_shear,
        normal_stress,
        static_part,
        drop_part,
        inverse_distance,
    )


def block_mean(velocity, start):
    face_cells = lax.slice_in_dim(velocity, start, start + 3, axis=3)
    grouped = face_cells.reshape(
        face_cells.shape[0], face_cells.shape[1] // 3, 3, face_cells.shape[2] // 3, 3, 3
    )
    return jnp.mean(grouped, axis=(2, 4, 5))


def restrict(velocity):
    across = velocity.shape[3]
    return jnp.stack([block_mean(velocity, 0), block_mean(velocity, across - 3)])


def inserted(velocity, selectors, restricted):
    for face in range(2):
        velocity = (
            velocity * (1.0 - selectors[face]) + selectors[face] * restricted[face][:, :, None, :]
        )
    return velocity


def low_framed(values, from_first, from_second, comps_first, comps_second):
    padded = jnp.pad(values, ((0, 0), (1, 1), (1, 1), (0, 0)))
    for member, comp in enumerate(comps_first):
        padded = padded.at[comp, 0:1, 1:-1].set(from_first[member])
    for member, comp in enumerate(comps_second):
        padded = padded.at[comp, 1:-1, 0:1].set(from_second[member])
    return padded


def high_framed(values, from_first, from_second):
    padded = jnp.pad(values, ((0, 0), (1, 1), (1, 1), (0, 0)))
    padded = padded.at[:, -1:, 1:-1].set(from_first)
    return padded.at[:, 1:-1, -1:].set(from_second)


def last_planes(values, comps, along):
    return jnp.stack(
        [
            lax.slice_in_dim(
                values[comp], values.shape[along + 1] - 1, values.shape[along + 1], axis=along
            )
            for comp in comps
        ]
    )


def body(
    coarse_velocity,
    coarse_stress,
    coarse_material,
    fine_velocity,
    fine_stress,
    fine_material,
    fault_slip,
    initial_shear,
    normal_stress,
    fault_mask,
    zone_ids,
    static_friction,
    friction_drop,
    weakening_distance,
    owner_rows,
):
    rows_here = coarse_velocity.shape[2]
    local_rows = lax.axis_index("gy") * rows_here + jnp.arange(rows_here, dtype=jnp.int32)
    selectors = (local_rows[None, None, :, None] == owner_rows[:, :, None, :]).astype(jnp.float32)
    coupling_plane = jnp.sum(selectors[:, None] * coarse_velocity[None], axis=3)
    shares = lax.psum_scatter(coupling_plane, "gy", scatter_dimension=3, tiled=True)
    bounds = jnp.repeat(jnp.repeat(shares, 3, axis=2), 3, axis=3)
    settings = fault_settings(
        fault_mask,
        initial_shear,
        normal_stress,
        zone_ids,
        static_friction,
        friction_drop,
        weakening_distance,
    )
    velocity = fine_velocity
    stress = fine_stress
    slip_state = fault_slip
    for substep in range(3):
        stress_strike = from_behind(last_planes(stress, (0, 3, 4), 0), "gx", 1)
        stress_depth = from_behind(last_planes(stress, (2, 4, 5), 1), "gy", 1)
        framed_stress = low_framed(stress, stress_strike, stress_depth, (0, 3, 4), (2, 4, 5))
        velocity = with_bounds(
            velocity_step(velocity, framed_stress, fine_material, (0, 2, 1), 1), bounds
        )
        moving_strike = from_behind(velocity[:, 0:1], "gx", -1)
        moving_depth = from_behind(velocity[:, :, 0:1], "gy", -1)
        framed_velocity = high_framed(velocity, moving_strike, moving_depth)
        stress = stress_step(stress, framed_velocity, fine_material, (0, 2, 1), 1)
        stress, slip_state = friction_step(stress, slip_state, settings)
    restricted = restrict(velocity)
    restricted_full = lax.all_gather(restricted, "gy", axis=3, tiled=True)
    coarse_strike = from_behind(last_planes(coarse_stress, (0, 3, 4), 0), "gx", 1)
    coarse_mapy = from_behind(last_planes(coarse_stress, (3, 1, 5), 1), "gy", 1)
    coarse_rim = low_framed(coarse_stress, coarse_strike, coarse_mapy, (0, 3, 4), (3, 1, 5))
    coarse_next = velocity_step(coarse_velocity, coarse_rim, coarse_material, (0, 1, 2), 1)
    coarse_next = inserted(coarse_next, selectors, restricted_full)
    next_strike = from_behind(coarse_next[:, 0:1], "gx", -1)
    next_mapy = from_behind(coarse_next[:, :, 0:1], "gy", -1)
    moving_rim = high_framed(coarse_next, next_strike, next_mapy)
    coarse_stress_next = stress_step(coarse_stress, moving_rim, coarse_material, (0, 1, 2), 1)
    return (coarse_next, coarse_stress_next, velocity, stress, slip_state)


def solution(mesh):
    return jax.shard_map(
        body,
        mesh=mesh,
        in_specs=(
            P(None, "gx", "gy", None),
            P(None, "gx", "gy", None),
            P(None, "gx", "gy", None),
            P(None, "gx", "gy", None),
            P(None, "gx", "gy", None),
            P(None, "gx", "gy", None),
            P("gx", "gy"),
            P("gx", "gy"),
            P("gx", "gy"),
            P("gx", "gy"),
            P("gx", "gy"),
            P(),
            P(),
            P(),
            P(None, "gx", None),
        ),
        out_specs=(
            P(None, "gx", "gy", None),
            P(None, "gx", "gy", None),
            P(None, "gx", "gy", None),
            P(None, "gx", "gy", None),
            P("gx", "gy"),
        ),
        check_vma=False,
    )
```

profile of v0, /device:TPU:31, one launch (start us, length us, event | category | flops | bytes accessed | tf_op | source)
XLA Modules:
  0.0 307.1 jit_solution(3842828616656935652)
XLA Ops:
  2.8 4.1 %collective-permute-start.3 = (f32[3,12,1,256]{3,0,1,2:T(4,128)}, f32[3,12,1,256]{3,0,1,2:T(4,128)}, u32[]{:S(2)}, u32[]{:S(2)}) collective-permute-start(f32[3,12,1,256]{3,0,1,2:T(4,128)} %pad_maximum_fusion.11), channel_id=1, source_target_pairs={{0,1},{1,2},{2,3},{3,4},{4,5},{5,6},{6,7},{7,8},{8,9},{9,10},{10,1... | collective-permute-start | bytes 110600 | tf_op jit(solution)/shard_map/ppermute | solution.py:12
  10.3 1.9 collective-permute-start.1
  17.2 62.7 %all-reduce.80 = f32[2,3,4,128]{3,2,1,0:T(4,128)S(1)} all-reduce(f32[2,3,4,128]{3,2,1,0:T(4,128)S(1)} %multiply_reduce_fusion), channel_id=2, replica_groups=mesh['gx'=8,'gy'=16] {'gy'}, use_global_device_ids=true, to_apply=%region_1.0.clone | all-reduce | flops 3072 | bytes 24576
  97.7 1.8 slice_bitcast_fusion.61
  109.6 3.6 %scatter.156 = f32[3,12,24,256]{3,2,1,0:T(8,128)S(1)} dynamic-update-slice(f32[3,12,24,256]{3,2,1,0:T(8,128)S(1)} %fusion.4, f32[3,12,24,1]{3,2,1,0:T(8,128)S(1)} %copy-done.12, s32[]{:T(128)} %constant.1057.clone.1, s32[]{:T(128)} %constant.1057.clone.1, s32[]{:T(128)} %constant.1057.clone.1, s32[]{:T(128)} %constant.1057.clone.1) | dynamic-update-slice | bytes 6916 | tf_op jit(solution)/shard_map/scatter | solution.py:99
  113.2 6.1 %scatter.159 = f32[3,12,24,256]{3,2,1,0:T(8,128)S(1)} dynamic-update-slice(f32[3,12,24,256]{3,2,1,0:T(8,128)S(1)} %scatter.156, f32[3,12,24,1]{3,2,1,0:T(8,128)S(1)} %copy-done.13, s32[]{:T(128)} %constant.1057.clone.1, s32[]{:T(128)} %constant.1057.clone.1, s32[]{:T(128)} %constant.1057.clone.1, s32[]{:T(128)} %constant.1066.clone.1) | dynamic-update-slice | bytes 6916 | tf_op jit(solution)/shard_map/scatter | solution.py:100
  119.3 4.9 %collective-permute-start.4 = (f32[3,1,24,256]{3,2,1,0:T(8,128)S(1)}, f32[3,1,24,256]{3,2,1,0:T(8,128)S(1)}, u32[]{:S(2)}, u32[]{:S(2)}) collective-permute-start(f32[3,1,24,256]{3,2,1,0:T(8,128)S(1)} %slice.2487), channel_id=1, source_target_pairs={{16,0},{32,16},{48,32},{64,48},{80,64},{96,80},{112,96},{17,1},{33... | collective-permute-start | bytes 221192 | tf_op jit(solution)/shard_map/ppermute | solution.py:12
  124.2 8.1 %collective-permute-start.5 = (f32[3,12,1,256]{3,2,1,0:T(1,128)S(1)}, f32[3,12,1,256]{3,2,1,0:T(1,128)S(1)}, u32[]{:S(2)}, u32[]{:S(2)}) collective-permute-start(f32[3,12,1,256]{3,2,1,0:T(1,128)S(1)} %slice.2488), channel_id=1, source_target_pairs={{1,0},{2,1},{3,2},{4,3},{5,4},{6,5},{7,6},{8,7},{9,8},{10,9},{11,1... | collective-permute-start | bytes 110600 | tf_op jit(solution)/shard_map/ppermute | solution.py:12
  142.2 1.9 collective-permute-start.7
  144.2 1.9 pad.255
  148.2 5.0 %collective-permute-done.6 = f32[3,1,24,256]{3,2,1,0:T(8,128)S(1)} collective-permute-done((f32[3,1,24,256]{3,2,1,0:T(8,128)S(1)}, f32[3,1,24,256]{3,2,1,0:T(8,128)S(1)}, u32[]{:S(2)}, u32[]{:S(2)}) %collective-permute-start.6) | collective-permute-done | bytes 73760 | tf_op jit(solution)/shard_map/ppermute | solution.py:12
  162.6 2.0 slice_bitcast_fusion.16
  167.3 2.3 scatter.175
  169.6 4.7 %scatter.176 = f32[3,12,24,256]{3,2,1,0:T(8,128)} dynamic-update-slice(f32[3,12,24,256]{3,2,1,0:T(8,128)} %scatter.175, f32[3,12,24,1]{3,2,1,0:T(8,128)} %copy.574, s32[]{:T(128)} %constant.1057.clone.1, s32[]{:T(128)} %constant.1057.clone.1, s32[]{:T(128)} %constant.1057.clone.1, s32[]{:T(128)} %constant.1066.clone.1) | dynamic-update-slice | bytes 6916 | tf_op jit(solution)/shard_map/scatter | solution.py:100
  176.9 4.4 %collective-permute-start.8 = (f32[3,1,24,256]{3,2,1,0:T(8,128)S(1)}, f32[3,1,24,256]{3,2,1,0:T(8,128)}, u32[]{:S(2)}, u32[]{:S(2)}) collective-permute-start(f32[3,1,24,256]{3,2,1,0:T(8,128)S(1)} %slice.2537), channel_id=1, source_target_pairs={{16,0},{32,16},{48,32},{64,48},{80,64},{96,80},{112,96},{17,1},{33... | collective-permute-start | bytes 221192 | tf_op jit(solution)/shard_map/ppermute | solution.py:12
  181.4 3.8 %collective-permute-start.9 = (f32[3,12,1,256]{3,2,1,0:T(1,128)}, f32[3,12,1,256]{3,2,1,0:T(1,128)}, u32[]{:S(2)}, u32[]{:S(2)}) collective-permute-start(f32[3,12,1,256]{3,2,1,0:T(1,128)} %slice.2538), channel_id=1, source_target_pairs={{1,0},{2,1},{3,2},{4,3},{5,4},{6,5},{7,6},{8,7},{9,8},{10,9},{11,1... | collective-permute-start | bytes 110600 | tf_op jit(solution)/shard_map/ppermute | solution.py:12
  185.3 1.7 fusion.35
  189.8 1.8 scatter.180
  201.4 1.9 collective-permute-start.11
  203.3 1.9 pad.257
  206.5 2.2 collective-permute-done.11
  208.6 1.6 collective-permute-done.10
  219.1 2.0 slice_bitcast_fusion.7
  223.2 3.2 %scatter.194 = f32[3,12,24,256]{3,2,1,0:T(8,128)S(1)} dynamic-update-slice(f32[3,12,24,256]{3,2,1,0:T(8,128)S(1)} %fusion.1, f32[3,12,24,1]{3,2,1,0:T(8,128)} %copy.571, s32[]{:T(128)} %constant.1057.clone.1, s32[]{:T(128)} %constant.1057.clone.1, s32[]{:T(128)} %constant.1057.clone.1, s32[]{:T(128)} %constant.1057.clone.1) | dynamic-update-slice | bytes 6916 | tf_op jit(solution)/shard_map/scatter | solution.py:99
  226.4 5.8 %scatter.195 = f32[3,12,24,256]{3,2,1,0:T(8,128)S(1)} dynamic-update-slice(f32[3,12,24,256]{3,2,1,0:T(8,128)S(1)} %scatter.194, f32[3,12,24,1]{3,2,1,0:T(8,128)} %copy.574, s32[]{:T(128)} %constant.1057.clone.1, s32[]{:T(128)} %constant.1057.clone.1, s32[]{:T(128)} %constant.1057.clone.1, s32[]{:T(128)} %constant.1066.clone.1) | dynamic-update-slice | bytes 6916 | tf_op jit(solution)/shard_map/scatter | solution.py:100
  244.1 29.0 %all_gather.3 = f32[2,3,4,128]{2,0,1,3:T(2,128)S(1)} all-gather(f32[2,3,4,8]{2,0,1,3:T(2,128)} %copy.587), channel_id=1, replica_groups=mesh['gx'=8,'gy'=16] {'gy'}, dimensions={3}, use_global_device_ids=true | all-gather | bytes 13056 | tf_op jit(solution)/shard_map/all_gather | solution.py:224
  274.1 1.6 copy.588
  278.4 2.2 collective-permute-start.12
  281.2 2.3 collective-permute-start.13
  286.1 2.9 collective-permute-start.14
  289.0 2.2 collective-permute-start.15
  296.7 1.8 scatter.201
  (348 shorter events, 120.7 us)
Async XLA Ops:
  0.6 80.6 %copy-start.56 = (u32[128]{0:T(128)S(1)}, u32[128]{0:T(128)}, u32[]{:S(2)}) copy-start(u32[128]{0:T(128)} %constant.1247) | copy-start | bytes 1540
  0.7 14.9 %copy-start = (f32[3,12,24,256]{3,2,1,0:T(8,128)S(1)}, f32[3,12,24,256]{3,2,1,0:T(8,128)}, u32[]{:S(2)}) copy-start(f32[3,12,24,256]{3,2,1,0:T(8,128)} %param.102) | copy-start | bytes 2654212
  0.7 15.7 %copy-start.52 = (s32[2,4,128]{2,1,0:T(4,128)S(1)}, s32[2,4,128]{2,1,0:T(4,128)}, u32[]{:S(2)}) copy-start(s32[2,4,128]{2,1,0:T(4,128)} %param.111) | copy-start | bytes 12292
  0.7 16.4 %copy-start.25 = (f32[3,4,16,128]{3,2,1,0:T(8,128)S(1)}, f32[3,4,16,128]{3,2,1,0:T(8,128)}, u32[]{:S(2)}) copy-start(f32[3,4,16,128]{3,2,1,0:T(8,128)} %param.97) | copy-start | bytes 294916
  0.7 79.2 %copy-start.55 = (f32[4]{0:T(128)S(1)}, f32[4]{0:T(128)}, u32[]{:S(2)}) copy-start(f32[4]{0:T(128)} %param.110) | copy-start | bytes 52
  0.7 81.8 %copy-start.51 = (s32[12,24]{1,0:T(8,128)S(1)}, s32[12,24]{1,0:T(8,128)}, u32[]{:S(2)}) copy-start(s32[12,24]{1,0:T(8,128)} %param.107) | copy-start | bytes 3460
  0.7 81.8 %copy-start.54 = (f32[4]{0:T(128)S(1)}, f32[4]{0:T(128)}, u32[]{:S(2)}) copy-start(f32[4]{0:T(128)} %param.108) | copy-start | bytes 52
  0.7 81.8 %copy-start.53 = (f32[4]{0:T(128)S(1)}, f32[4]{0:T(128)}, u32[]{:S(2)}) copy-start(f32[4]{0:T(128)} %param.109) | copy-start | bytes 52
  2.8 96.7 %collective-permute-start.3 = (f32[3,12,1,256]{3,0,1,2:T(4,128)}, f32[3,12,1,256]{3,0,1,2:T(4,128)}, u32[]{:S(2)}, u32[]{:S(2)}) collective-permute-start(f32[3,12,1,256]{3,0,1,2:T(4,128)} %pad_maximum_fusion.11), channel_id=1, source_target_pairs={{0,1},{1,2},{2,3},{3,4},{4,5},{5,6},{6,7},{7,8},{8,9},{9,10},{10,1... | collective-permute-start | bytes 110600 | tf_op jit(solution)/shard_map/ppermute | solution.py:12
  7.6 94.7 %collective-permute-start.2 = (f32[3,1,24,256]{3,2,1,0:T(8,128)}, f32[3,1,24,256]{3,2,1,0:T(8,128)}, u32[]{:S(2)}, u32[]{:S(2)}) collective-permute-start(f32[3,1,24,256]{3,2,1,0:T(8,128)} %pad_maximum_fusion.8), channel_id=1, source_target_pairs={{0,16},{16,32},{32,48},{48,64},{64,80},{80,96},{96,112},{1,17},{17... | collective-permute-start | bytes 221192 | tf_op jit(solution)/shard_map/ppermute | solution.py:12
  10.3 78.0 %collective-permute-start.1 = (f32[3,4,1,128]{3,2,1,0:T(1,128)}, f32[3,4,1,128]{3,2,1,0:T(1,128)}, u32[]{:S(2)}, u32[]{:S(2)}) collective-permute-start(f32[3,4,1,128]{3,2,1,0:T(1,128)} %pad_maximum_fusion.16), channel_id=1, source_target_pairs={{0,1},{1,2},{2,3},{3,4},{4,5},{5,6},{6,7},{7,8},{8,9},{9,10},{10,1... | collective-permute-start | bytes 18440 | tf_op jit(solution)/shard_map/ppermute | solution.py:12
  14.3 74.8 %collective-permute-start = (f32[3,1,16,128]{3,2,1,0:T(8,128)}, f32[3,1,16,128]{3,2,1,0:T(8,128)}, u32[]{:S(2)}, u32[]{:S(2)}) collective-permute-start(f32[3,1,16,128]{3,2,1,0:T(8,128)} %pad_maximum_fusion.14), channel_id=1, source_target_pairs={{0,16},{16,32},{32,48},{48,64},{64,80},{80,96},{96,112},{1,17},{17... | collective-permute-start | bytes 73736 | tf_op jit(solution)/shard_map/ppermute | solution.py:12
  119.3 14.8 %collective-permute-start.4 = (f32[3,1,24,256]{3,2,1,0:T(8,128)S(1)}, f32[3,1,24,256]{3,2,1,0:T(8,128)S(1)}, u32[]{:S(2)}, u32[]{:S(2)}) collective-permute-start(f32[3,1,24,256]{3,2,1,0:T(8,128)S(1)} %slice.2487), channel_id=1, source_target_pairs={{16,0},{32,16},{48,32},{64,48},{80,64},{96,80},{112,96},{17,1},{33... | collective-permute-start | bytes 221192 | tf_op jit(solution)/shard_map/ppermute | solution.py:12
  124.2 10.1 %collective-permute-start.5 = (f32[3,12,1,256]{3,2,1,0:T(1,128)S(1)}, f32[3,12,1,256]{3,2,1,0:T(1,128)S(1)}, u32[]{:S(2)}, u32[]{:S(2)}) collective-permute-start(f32[3,12,1,256]{3,2,1,0:T(1,128)S(1)} %slice.2488), channel_id=1, source_target_pairs={{1,0},{2,1},{3,2},{4,3},{5,4},{6,5},{7,6},{8,7},{9,8},{10,9},{11,1... | collective-permute-start | bytes 110600 | tf_op jit(solution)/shard_map/ppermute | solution.py:12
  142.2 5.3 %collective-permute-start.7 = (f32[3,12,1,256]{3,2,1,0:T(1,128)S(1)}, f32[3,12,1,256]{3,2,1,0:T(1,128)S(1)}, u32[]{:S(2)}, u32[]{:S(2)}) collective-permute-start(f32[3,12,1,256]{3,2,1,0:T(1,128)S(1)} %pad_maximum_fusion.12), channel_id=1, source_target_pairs={{0,1},{1,2},{2,3},{3,4},{4,5},{5,6},{6,7},{7,8},{8,9},{9,10},{10,1... | collective-permute-start | bytes 110600 | tf_op jit(solution)/shard_map/ppermute | solution.py:12
  146.1 7.0 %collective-permute-start.6 = (f32[3,1,24,256]{3,2,1,0:T(8,128)S(1)}, f32[3,1,24,256]{3,2,1,0:T(8,128)S(1)}, u32[]{:S(2)}, u32[]{:S(2)}) collective-permute-start(f32[3,1,24,256]{3,2,1,0:T(8,128)S(1)} %pad_maximum_fusion.9), channel_id=1, source_target_pairs={{0,16},{16,32},{32,48},{48,64},{64,80},{80,96},{96,112},{1,17},{17... | collective-permute-start | bytes 221192 | tf_op jit(solution)/shard_map/ppermute | solution.py:12
  167.3 17.9 %copy-start.17 = (f32[6,6,18,128]{3,2,1,0:T(8,128)S(1)}, f32[6,6,18,128]{3,2,1,0:T(8,128)}, u32[]{:S(2)}) copy-start(f32[6,6,18,128]{3,2,1,0:T(8,128)} %scatter.145) | copy-start | bytes 995332
  167.3 17.9 %copy-start.23 = (f32[6,18,128]{2,1,0:T(8,128)S(1)}, f32[6,18,128]{2,1,0:T(8,128)}, u32[]{:S(2)}) copy-start(f32[6,18,128]{2,1,0:T(8,128)} %get-tuple-element.621) | copy-start | bytes 165892
  167.3 17.9 %copy-start.26 = (f32[6,18,128]{2,1,0:T(8,128)S(1)}, f32[6,18,128]{2,1,0:T(8,128)}, u32[]{:S(2)}) copy-start(f32[6,18,128]{2,1,0:T(8,128)} %get-tuple-element.619) | copy-start | bytes 165892
  167.3 17.9 %copy-start.27 = (f32[6,18,128]{2,1,0:T(8,128)S(1)}, f32[6,18,128]{2,1,0:T(8,128)}, u32[]{:S(2)}) copy-start(f32[6,18,128]{2,1,0:T(8,128)} %get-tuple-element.620) | copy-start | bytes 165892
  167.3 17.9 %copy-start.28 = (f32[6,18,128]{2,1,0:T(8,128)S(1)}, f32[6,18,128]{2,1,0:T(8,128)}, u32[]{:S(2)}) copy-start(f32[6,18,128]{2,1,0:T(8,128)} %get-tuple-element.622) | copy-start | bytes 165892
  167.3 17.9 %copy-start.29 = (f32[6,18,128]{2,1,0:T(8,128)S(1)}, f32[6,18,128]{2,1,0:T(8,128)}, u32[]{:S(2)}) copy-start(f32[6,18,128]{2,1,0:T(8,128)} %get-tuple-element.623) | copy-start | bytes 165892
  167.3 17.9 %copy-start.30 = (f32[5,18,128]{2,1,0:T(8,128)S(1)}, f32[5,18,128]{2,1,0:T(8,128)}, u32[]{:S(2)}) copy-start(f32[5,18,128]{2,1,0:T(8,128)} %get-tuple-element.616) | copy-start | bytes 138244
  176.9 11.2 %collective-permute-start.8 = (f32[3,1,24,256]{3,2,1,0:T(8,128)S(1)}, f32[3,1,24,256]{3,2,1,0:T(8,128)}, u32[]{:S(2)}, u32[]{:S(2)}) collective-permute-start(f32[3,1,24,256]{3,2,1,0:T(8,128)S(1)} %slice.2537), channel_id=1, source_target_pairs={{16,0},{32,16},{48,32},{64,48},{80,64},{96,80},{112,96},{17,1},{33... | collective-permute-start | bytes 221192 | tf_op jit(solution)/shard_map/ppermute | solution.py:12
  181.4 8.4 %collective-permute-start.9 = (f32[3,12,1,256]{3,2,1,0:T(1,128)}, f32[3,12,1,256]{3,2,1,0:T(1,128)}, u32[]{:S(2)}, u32[]{:S(2)}) collective-permute-start(f32[3,12,1,256]{3,2,1,0:T(1,128)} %slice.2538), channel_id=1, source_target_pairs={{1,0},{2,1},{3,2},{4,3},{5,4},{6,5},{7,6},{8,7},{9,8},{10,9},{11,1... | collective-permute-start | bytes 110600 | tf_op jit(solution)/shard_map/ppermute | solution.py:12
  201.4 7.3 %collective-permute-start.11 = (f32[3,12,1,256]{3,2,1,0:T(1,128)S(1)}, f32[3,12,1,256]{3,2,1,0:T(1,128)S(1)}, u32[]{:S(2)}, u32[]{:S(2)}) collective-permute-start(f32[3,12,1,256]{3,2,1,0:T(1,128)S(1)} %pad_maximum_fusion.13), channel_id=1, source_target_pairs={{0,1},{1,2},{2,3},{3,4},{4,5},{5,6},{6,7},{7,8},{8,9},{9,10},{10,1... | collective-permute-start | bytes 110600 | tf_op jit(solution)/shard_map/ppermute | solution.py:12
  205.2 5.1 %collective-permute-start.10 = (f32[3,1,24,256]{3,2,1,0:T(8,128)S(1)}, f32[3,1,24,256]{3,2,1,0:T(8,128)S(1)}, u32[]{:S(2)}, u32[]{:S(2)}) collective-permute-start(f32[3,1,24,256]{3,2,1,0:T(8,128)S(1)} %pad_maximum_fusion.10), channel_id=1, source_target_pairs={{0,16},{16,32},{32,48},{48,64},{64,80},{80,96},{96,112},{1,17},{17... | collective-permute-start | bytes 221192 | tf_op jit(solution)/shard_map/ppermute | solution.py:12
  232.2 53.3 %copy-start.9 = (f32[3,12,24,256]{3,2,1,0:T(8,128)}, f32[3,12,24,256]{3,2,1,0:T(8,128)S(1)}, u32[]{:S(2)}) copy-start(f32[3,12,24,256]{3,2,1,0:T(8,128)S(1)} %scatter.195) | copy-start | bytes 2654212
  278.4 12.8 %collective-permute-start.12 = (f32[3,1,16,128]{3,2,1,0:T(8,128)S(1)}, f32[3,1,16,128]{3,2,1,0:T(8,128)}, u32[]{:S(2)}, u32[]{:S(2)}) collective-permute-start(f32[3,1,16,128]{3,2,1,0:T(8,128)S(1)} %slice.2592), channel_id=1, source_target_pairs={{16,0},{32,16},{48,32},{64,48},{80,64},{96,80},{112,96},{17,1},{33... | collective-permute-start | bytes 73736 | tf_op jit(solution)/shard_map/ppermute | solution.py:12
  281.2 10.9 %collective-permute-start.13 = (f32[3,4,1,128]{3,2,1,0:T(1,128)}, f32[3,4,1,128]{3,2,1,0:T(1,128)}, u32[]{:S(2)}, u32[]{:S(2)}) collective-permute-start(f32[3,4,1,128]{3,2,1,0:T(1,128)} %slice.2593), channel_id=1, source_target_pairs={{1,0},{2,1},{3,2},{4,3},{5,4},{6,5},{7,6},{8,7},{9,8},{10,9},{11,1... | collective-permute-start | bytes 18440 | tf_op jit(solution)/shard_map/ppermute | solution.py:12
  286.1 9.0 %collective-permute-start.14 = (f32[3,1,24,256]{3,2,1,0:T(8,128)}, f32[3,1,24,256]{3,2,1,0:T(8,128)S(1)}, u32[]{:S(2)}, u32[]{:S(2)}) collective-permute-start(f32[3,1,24,256]{3,2,1,0:T(8,128)} %slice.2612), channel_id=1, source_target_pairs={{16,0},{32,16},{48,32},{64,48},{80,64},{96,80},{112,96},{17,1},{33... | collective-permute-start | bytes 221192 | tf_op jit(solution)/shard_map/ppermute | solution.py:12
  289.0 7.7 %collective-permute-start.15 = (f32[3,12,1,256]{3,2,1,0:T(1,128)}, f32[3,12,1,256]{3,2,1,0:T(1,128)S(1)}, u32[]{:S(2)}, u32[]{:S(2)}) collective-permute-start(f32[3,12,1,256]{3,2,1,0:T(1,128)} %slice.2613), channel_id=1, source_target_pairs={{1,0},{2,1},{3,2},{4,3},{5,4},{6,5},{7,6},{8,7},{9,8},{10,9},{11,1... | collective-permute-start | bytes 110600 | tf_op jit(solution)/shard_map/ppermute | solution.py:12
  (41 other events, 99.8 us)
where the time goes:
time: 311 us; the launch traced here: 307 us
  local copies, waits for them, and re-layouts  129 us (41%)
  blocking collectives  91.7 us (29%)
  starting transfers between devices  46.1 us (15%)
  other arithmetic  28.5 us (9%)
  waiting for transfers between devices  8.78 us (3%)
    unnamed x1, blocking collectives  62.7 us
    ppermute x16, starting transfers between devices, from_behind(): lax.ppermute(value, axis, [(source, source + steps) for source in range(f...  46.1 us
    all_gather x1, blocking collectives, body(): restricted_full = lax.all_gather(restricted, 'gy', axis=3, tiled=True)  29 us
    scatter x3, local copies, waits for them, and re-layouts, with_bounds(): return velocity.at[:, :, :, -1].set(bounds[1])  16.6 us
    scatter x12, local copies, waits for them, and re-layouts, low_framed(): padded = padded.at[comp, 1:-1, 0:1].set(from_second[member])  16 us
    scatter x12, local copies, waits for them, and re-layouts, low_framed(): padded = padded.at[comp, 0:1, 1:-1].set(from_first[member])  12.6 us
    unnamed x117, local copies, waits for them, and re-layouts  10.7 us
    scatter x3, local copies, waits for them, and re-layouts, with_bounds(): velocity = velocity.at[:, :, :, 0].set(bounds[0])  9.1 us
  transfers between devices with their start and end apart: 16, of which 3 were waited for; matrix products, arithmetic and copies ran while one was open for 15% of the time, Pallas kernels for 0%

commit v1 on v0

v1 whole, which is shorter than its diff:
```python
import jax
import jax.numpy as jnp
from jax import lax
from jax.experimental import pallas as pl
from jax.experimental.pallas import tpu as pltpu
from jax.sharding import PartitionSpec as P

STEP_RATIO = 0.15
F32 = jnp.float32
FINE_S = (0, 2, 1, 4, 3, 5)
FINE_V = (0, 2, 1)
COARSE_S = (0, 1, 2, 3, 4, 5)
COARSE_V = (0, 1, 2)
VMEM = pl.BlockSpec(memory_space=pltpu.VMEM)
SMEM = pl.BlockSpec(memory_space=pltpu.SMEM)
PARAMS = pltpu.CompilerParams(vmem_limit_bytes=32 * 1024 * 1024)


def call(kernel, outs, specs, *args):
    return pl.pallas_call(
        kernel,
        out_shape=tuple(jax.ShapeDtypeStruct(shape, F32) for shape in outs),
        in_specs=list(specs),
        out_specs=tuple(VMEM for _ in outs),
        compiler_params=PARAMS,
    )(*args)


def ring(value, axis, steps):
    count = lax.axis_size(axis)
    return lax.ppermute(value, axis, [(i, (i + steps) % count) for i in range(count)])


def iota(shape, along):
    return lax.broadcasted_iota(jnp.int32, shape, along)


def behind(a, along, edge):
    return jnp.where(iota(a.shape, along) == 0, edge, pltpu.roll(a, 1, along))


def ahead(a, along, edge):
    last = a.shape[along] - 1
    return jnp.where(iota(a.shape, along) == last, edge, pltpu.roll(a, last, along))


def velocity_plane(v, s, s_prev, rows, buoyancy):
    xx, bb, ll, xb, xl, bl = s
    p_xx, p_xb, p_xl = s_prev
    r_xb, r_bb, r_bl = rows
    f_x = (xx - p_xx) + (xb - behind(xb, 0, r_xb)) + (xl - behind(xl, 1, 0.0))
    f_b = (xb - p_xb) + (bb - behind(bb, 0, r_bb)) + (bl - behind(bl, 1, 0.0))
    f_l = (xl - p_xl) + (bl - behind(bl, 0, r_bl)) + (ll - behind(ll, 1, 0.0))
    scale = STEP_RATIO * buoyancy
    return (v[0] + scale * f_x, v[1] + scale * f_b, v[2] + scale * f_l)


def stress_plane(s, v, v_next, rows, lame, shear):
    vx, vb, vl = v
    nx, nb, nl = v_next
    rx, rb, rl = rows
    e_x = nx - vx
    e_b = ahead(vb, 0, rb) - vb
    e_l = ahead(vl, 1, 0.0) - vl
    e_xb = (ahead(vx, 0, rx) - vx) + (nb - vb)
    e_xl = (ahead(vx, 1, 0.0) - vx) + (nl - vl)
    e_bl = (ahead(vl, 0, rl) - vl) + (ahead(vb, 1, 0.0) - vb)
    common = (STEP_RATIO * lame) * (e_x + e_b + e_l)
    one = STEP_RATIO * shear
    two = 2.0 * one
    return (
        s[0] + (common + two * e_x),
        s[1] + (common + two * e_b),
        s[2] + (common + two * e_l),
        s[3] + one * e_xb,
        s[4] + one * e_xl,
        s[5] + one * e_bl,
    )


def own_cells(place, depth):
    shape = (depth, 128)
    return iota(shape, 1) == place[1] * (depth // 3) + iota(shape, 0) // 3


def pack_kernel(fs, cs, cv, rows_ref, place, xsend, zsend, coupling):
    nx, nz, _ = fs.shape[1:]
    cx, cy, cz = cs.shape[1:]
    for k, c in enumerate((0, 4, 3)):
        xsend[k * nz : (k + 1) * nz, :] = fs[c, nx - 1]
    for k, c in enumerate((0, 3, 4)):
        at = 3 * nz + k * 8
        xsend[at : at + 8, 0:128] = cs[c, cx - 1, 0:8]
        xsend[at : at + 8, 128:256] = cs[c, cx - 1, 8:16]
    zsend[...] = jnp.zeros_like(zsend)
    for k, c in enumerate((4, 2, 5)):
        for x in range(nx):
            zsend[k * nx + x, :] = fs[c, x, nz - 1]
    for k, c in enumerate((3, 1, 5)):
        for x in range(cx):
            zsend[40 + k * cx + x, 0:128] = cs[c, x, cy - 1]
    for f in range(2):
        for x in range(cx):
            here = place[1] * cy + iota((cy, cz), 0) == rows_ref[f, x : x + 1, :]
            for c in range(3):
                row = jnp.sum(jnp.where(here, cv[c, x], 0.0), axis=0, keepdims=True)
                coupling[(f * 3 + c) * cx + x : (f * 3 + c) * cx + x + 1, :] = row


def fault_kernel(slip, shear, normal, mask, zone, static, drop, distance, out, buf):
    nx, nz = slip.shape
    buf[...] = jnp.zeros_like(buf)
    for k, ref in enumerate((slip, shear, normal, mask, zone)):
        buf[16 * k : 16 * k + nx, 0:nz] = ref[...].astype(F32)
    turned = buf[...].T[0:nz]
    parts = [turned] + [pltpu.roll(turned, 128 - 16 * k, 1) for k in range(1, 5)]
    zero = jnp.zeros_like(turned)
    static_part, drop_part, inverse = zero, zero, zero
    for k in range(4):
        hit = parts[4] == float(k)
        static_part = jnp.where(hit, static[k], static_part)
        drop_part = jnp.where(hit, drop[k], drop_part)
        inverse = jnp.where(hit, 1.0 / jnp.full_like(zero, distance[k]), inverse)
    for k, part in enumerate((parts[0], parts[1], parts[2], parts[3], static_part, drop_part, inverse)):
        out[k] = part


def fine_velocity_kernel(last, with_coarse, *refs):
    if with_coarse:
        v, s, m, xr, zr, bounds, place, cxs, czs, out, xsend, zsend = refs
    elif last:
        v, s, m, xr, zr, bounds, place, out, xsend, zsend, share = refs
    else:
        v, s, m, xr, zr, bounds, place, out, xsend, zsend = refs
    nx, nz, ny = v.shape[1:]
    lane = iota((nz, ny), 1)
    cells = own_cells(place, nz)
    has_x = place[0] > 0
    has_z = place[1] > 0

    def column(f, c, x):
        at = (f * 3 + c) * (nx // 3) + x
        return jnp.sum(jnp.where(cells, bounds[at : at + 1, :], 0.0), axis=1, keepdims=True)

    columns = [[[column(f, c, x) for x in range(nx // 3)] for c in range(3)] for f in range(2)]
    zsend[...] = jnp.zeros_like(zsend)
    sums = {}
    for x in range(nx):
        here = [s[c, x] for c in FINE_S]
        if x == 0:
            before = [jnp.where(has_x, xr[k * nz : (k + 1) * nz, :], 0.0) for k in range(3)]
        else:
            before = [s[c, x - 1] for c in (0, 4, 3)]
        rows = [jnp.where(has_z, zr[k * nx + x : k * nx + x + 1, :], 0.0) for k in range(3)]
        new = velocity_plane([v[c, x] for c in FINE_V], here, before, rows, m[0, x])
        for k, c in enumerate(FINE_V):
            val = jnp.where(lane == 0, columns[0][c][x // 3], new[k])
            val = jnp.where(lane == ny - 1, columns[1][c][x // 3], val)
            out[c, x] = val
            if x == 0:
                xsend[k * nz : (k + 1) * nz, :] = val
            zsend[k * nx + x : k * nx + x + 1, :] = val[0:1]
            if last:
                sums[c, x // 3] = val if x % 3 == 0 else sums[c, x // 3] + val
    if with_coarse:
        xsend[3 * nz :, :] = cxs[...]
        zsend[40:, :] = czs[...]
    if last:
        for f in range(2):
            face = lane < 3 if f == 0 else lane >= ny - 3
            for c in range(3):
                for x in range(nx // 3):
                    at = (f * 3 + c) * (nx // 3) + x
                    total = jnp.sum(jnp.where(face, sums[c, x], 0.0), axis=1, keepdims=True)
                    row = jnp.sum(jnp.where(cells, total, 0.0), axis=0, keepdims=True)
                    share[at : at + 1, :] = row * (1.0 / 27.0)


def fine_stress_kernel(last, s, v, m, xr, zr, settings, slip, place, out, slip_out, *sends):
    nx, nz, ny = s.shape[1:]
    has_x = place[0] < place[2] - 1
    has_z = place[1] < place[3] - 1
    for x in range(nx):
        here = [v[c, x] for c in FINE_V]
        if x == nx - 1:
            after = [jnp.where(has_x, xr[k * nz : (k + 1) * nz, :], 0.0) for k in range(3)]
        else:
            after = [v[c, x + 1] for c in FINE_V]
        rows = [jnp.where(has_z, zr[k * nx + x : k * nx + x + 1, :], 0.0) for k in range(3)]
        new = stress_plane([s[c, x] for c in FINE_S], here, after, rows, m[1, x], m[2, x])
        for k, c in enumerate(FINE_S):
            out[c, x] = new[k]
    lane = iota((nz, 128), 1)
    half = ny // 2
    planes = [out[3, x, :, half:] for x in range(nx)]
    shear_plane = jnp.zeros((nz, 128), F32)
    for x in range(nx):
        moved = planes[x] if x == 0 else pltpu.roll(planes[x], x, 1)
        shear_plane = jnp.where(lane == x, moved, shear_plane)
    old = slip[...]
    traction = shear_plane + settings[1]
    weakened = jnp.minimum(old * settings[6], 1.0)
    strength = settings[2] * (settings[4] - settings[5] * weakened)
    resisted = jnp.clip(traction, -strength, strength)
    active = settings[3]
    fresh = old + active * STEP_RATIO * jnp.abs(traction - resisted)
    fixed = shear_plane + active * (resisted - traction)
    for x in range(nx):
        moved = fixed if x == 0 else pltpu.roll(fixed, 128 - x, 1)
        out[3, x, :, half:] = jnp.where(lane == 0, moved, planes[x])
    if last:
        turned = jnp.concatenate([fresh, jnp.zeros((128 - nz, 128), F32)], axis=0).T
        slip_out[...] = turned[0:nx, 0:nz]
        return
    slip_out[...] = fresh
    xsend, zsend = sends
    for k, c in enumerate((0, 4, 3)):
        xsend[k * nz : (k + 1) * nz, :] = out[c, nx - 1]
    zsend[...] = jnp.zeros_like(zsend)
    for k, c in enumerate((4, 2, 5)):
        for x in range(nx):
            zsend[k * nx + x : k * nx + x + 1, :] = out[c, x, nz - 1 : nz]


def coarse_velocity_kernel(cv, cs, cm, xr, zr, rows_ref, place, out, xsend, zsend):
    nx, ny, nz = cv.shape[1:]
    nzf = xr.shape[0] - 24
    has_x = place[0] > 0
    has_y = place[1] > 0
    xsend[...] = jnp.zeros_like(xsend)
    zsend[...] = jnp.zeros_like(zsend)
    for x in range(nx):
        here = [cs[c, x] for c in COARSE_S]
        if x == 0:
            before = []
            for k in range(3):
                at = nzf + 8 * k
                plane = jnp.concatenate([xr[at : at + 8, 0:128], xr[at : at + 8, 128:256]], axis=0)
                before.append(jnp.where(has_x, plane, 0.0))
        else:
            before = [cs[c, x - 1] for c in (0, 3, 4)]
        rows = [jnp.where(has_y, zr[40 + k * nx + x : 41 + k * nx + x, 0:128], 0.0) for k in range(3)]
        new = velocity_plane([cv[c, x] for c in COARSE_V], here, before, rows, cm[0, x])
        for c in range(3):
            out[c, x] = new[c]
            zsend[c * nx + x : c * nx + x + 1, 0:128] = new[c][0:1]
            if x == 0:
                xsend[8 * c : 8 * c + 8, 0:128] = new[c][0:8]
                xsend[8 * c : 8 * c + 8, 128:256] = new[c][8:16]
    for f in range(2):
        xsend[24 + f : 25 + f, 0:128] = rows_ref[f, 0:1, :].astype(F32)


def coarse_stress_kernel(cv, cs, cm, xr, zr, rows_ref, rest, rest_next, place, v_out, s_out):
    nx, ny, nz = cv.shape[1:]
    base = xr.shape[0] - 32
    has_x = place[0] < place[2] - 1
    has_y = place[1] < place[3] - 1
    row_ids = place[1] * ny + iota((ny, nz), 0)

    def inserted(plane, c, x):
        for f in range(2):
            if x < nx:
                hit = row_ids == rows_ref[f, x : x + 1, :]
                at = (f * 3 + c) * nx + x
                value = rest[at : at + 1, :]
            else:
                hit = row_ids.astype(F32) == xr[base + 24 + f : base + 25 + f, 0:128]
                value = rest_next[f * 3 + c : f * 3 + c + 1, :]
            plane = jnp.where(hit, value, plane)
        return plane

    planes = [[inserted(cv[c, x], c, x) for c in range(3)] for x in range(nx)]
    edge = []
    for c in range(3):
        at = base + 8 * c
        plane = jnp.concatenate([xr[at : at + 8, 0:128], xr[at : at + 8, 128:256]], axis=0)
        edge.append(jnp.where(has_x, inserted(plane, c, nx), 0.0))
    planes.append(edge)
    for x in range(nx):
        for c in range(3):
            v_out[c, x] = planes[x][c]
        rows = [jnp.where(has_y, zr[40 + k * nx + x : 41 + k * nx + x, 0:128], 0.0) for k in range(3)]
        new = stress_plane([cs[c, x] for c in COARSE_S], planes[x], planes[x + 1], rows, cm[1, x], cm[2, x])
        for c in range(6):
            s_out[c, x] = new[c]


def spread(value):
    total = value + ring(value, "gy", 4) + ring(value, "gy", 8) + ring(value, "gy", 12)
    return total + ring(total, "gy", 1) + ring(total, "gy", 2) + ring(total, "gy", 3)


def body(
    coarse_velocity,
    coarse_stress,
    coarse_material,
    fine_velocity,
    fine_stress,
    fine_material,
    fault_slip,
    initial_shear,
    normal_stress,
    fault_mask,
    zone_ids,
    static_friction,
    friction_drop,
    weakening_distance,
    owner_rows,
):
    nx, nz, ny = fine_velocity.shape[1:]
    cx = coarse_velocity.shape[1]
    place = jnp.stack(
        [lax.axis_index("gx"), lax.axis_index("gy"), lax.axis_size("gx"), lax.axis_size("gy")]
    ).astype(jnp.int32)
    shares = (6 * cx, 128)
    xsize = 3 * nz
    xsend, zsend, coupling = call(
        pack_kernel,
        [(xsize + 24, 256), (56, 256), shares],
        [VMEM] * 4 + [SMEM],
        fine_stress, coarse_stress, coarse_velocity, owner_rows, place,
    )
    bounds = spread(coupling)
    xr, zr = ring(xsend, "gx", 1), ring(zsend, "gy", 1)
    settings = pl.pallas_call(
        fault_kernel,
        out_shape=jax.ShapeDtypeStruct((7, nz, 128), F32),
        in_specs=[VMEM] * 5 + [SMEM] * 3,
        out_specs=VMEM,
        scratch_shapes=[pltpu.VMEM((128, 128), F32)],
        compiler_params=PARAMS,
    )(fault_slip, initial_shear, normal_stress, fault_mask, zone_ids, static_friction, friction_drop, weakening_distance)
    slip = settings[0]
    coarse_moved, cxs, czs = call(
        coarse_velocity_kernel,
        [coarse_velocity.shape, (32, 256), (16, 256)],
        [VMEM] * 6 + [SMEM],
        coarse_velocity, coarse_stress, coarse_material, xr, zr, owner_rows, place,
    )
    velocity, stress = fine_velocity, fine_stress
    for step in range(3):
        last, coarse_too = step == 2, step == 1
        args = [velocity, stress, fine_material, xr, zr, bounds, place]
        outs = [velocity.shape, (xsize + 32 * coarse_too, 256), (40 + 16 * coarse_too, 256)]
        specs = [VMEM] * 6 + [SMEM]
        if coarse_too:
            args += [cxs, czs]
            specs += [VMEM] * 2
        if last:
            outs.append(shares)
        velocity, xsend, zsend, *more = call(
            lambda *refs, last=last, coarse_too=coarse_too: fine_velocity_kernel(last, coarse_too, *refs),
            outs, specs, *args,
        )
        if last:
            restricted = spread(more[0])
            first = jnp.concatenate([restricted[cx * k : cx * k + 1] for k in range(6)], axis=0)
            restricted_next = ring(first, "gx", -1)
        xr, zr = ring(xsend, "gx", -1), ring(zsend, "gy", -1)
        if coarse_too:
            coarse_xr, coarse_zr = xr, zr
        outs = [stress.shape]
        outs += [fault_slip.shape] if last else [(nz, 128), (xsize, 256), (40, 256)]
        stress, slip, *sends = call(
            lambda *refs, last=last: fine_stress_kernel(last, *refs),
            outs, [VMEM] * 7 + [SMEM],
            stress, velocity, fine_material, xr, zr, settings, slip, place,
        )
        if not last:
            xr, zr = ring(sends[0], "gx", 1), ring(sends[1], "gy", 1)
    coarse_next, coarse_stress_next = call(
        coarse_stress_kernel,
        [coarse_velocity.shape, coarse_stress.shape],
        [VMEM] * 8 + [SMEM],
        coarse_moved, coarse_stress, coarse_material, coarse_xr, coarse_zr, owner_rows, restricted, restricted_next, place,
    )
    return (coarse_next, coarse_stress_next, velocity, stress, slip)


def solution(mesh):
    grid = P(None, "gx", "gy", None)
    plane = P("gx", "gy")
    return jax.shard_map(
        body,
        mesh=mesh,
        in_specs=(grid,) * 6 + (plane,) * 5 + (P(),) * 3 + (P(None, "gx", None),),
        out_specs=(grid,) * 4 + (plane,),
        check_vma=False,
    )
```

time: 311 us -> 99.1 us (0.32)
  local copies, waits for them, and re-layouts: 129 us -> 6.78 us
  blocking collectives: 91.7 us -> 0 us
  other arithmetic: 28.5 us -> 0.1 us
  Pallas kernels: 0 us -> 12.5 us
  waiting for transfers between devices: 8.78 us -> 21 us
  starting transfers between devices: 46.1 us -> 56 us
    scatter x41 -> x0, local copies, waits for them, and re-layouts: 67.4 us -> none  [the longest x3 16.6 us: with_bounds(): return velocity.at[:, :, :, -1].set(bounds[1])]
    unnamed x1 -> x0, blocking collectives: 62.7 us -> none
    all_gather x1 -> x0, blocking collectives: 29 us -> none  [body(): restricted_full = lax.all_gather(restricted, 'gy', axis=3, tiled=True)]
    slice x78 -> x1, local copies, waits for them, and re-layouts: 22.4 us -> 0.01 us  [body(): restricted[cx * k:cx * k + 1]]
    pallas_call x0 -> x10, Pallas kernels: none -> 12.5 us  [the longest x9 11.8 us: call(): pl.pallas_call(kernel, out_shape=tuple((jax.ShapeDtypeStruct(shape, F32)...]
    ppermute x16 -> x25, waiting for transfers between devices: 8.78 us -> 21 us  [ring(): lax.ppermute(value, axis, [(i, (i + steps) % count) for i in range(count)])]
    another operation x24 -> x1, other arithmetic: 11.8 us -> 0.08 us  [body(): jnp.stack([lax.axis_index('gx'), lax.axis_index('gy'), lax.axis_size('gx'...]
    squeeze x12 -> x1, local copies, waits for them, and re-layouts: 11.6 us -> 0.01 us  [body(): slip = settings[0]]
  transfers between devices with their start and end apart: 16 -> 25, of which waited for: 3 -> 14; matrix products, arithmetic and copies ran while one was open for 15% -> 0% of each run, Pallas kernels for 0% -> 3%
where the time goes in v1:
time: 99.1 us; the launch traced here: 97.3 us
  starting transfers between devices  56 us (57%)
  waiting for transfers between devices  21 us (21%)
  Pallas kernels  12.5 us (13%)
  local copies, waits for them, and re-layouts  6.78 us (7%)
    ppermute x25, starting transfers between devices, ring(): lax.ppermute(value, axis, [(i, (i + steps) % count) for i in range(count)])  56 us
    ppermute x25, waiting for transfers between devices, ring(): lax.ppermute(value, axis, [(i, (i + steps) % count) for i in range(count)])  21 us
    pallas_call x9, Pallas kernels, call(): pl.pallas_call(kernel, out_shape=tuple((jax.ShapeDtypeStruct(shape, F32)...  11.8 us
    unnamed x38, local copies, waits for them, and re-layouts  6.75 us
  transfers between devices with their start and end apart: 25, of which 14 were waited for; matrix products, arithmetic and copies ran while one was open for 0% of the time, Pallas kernels for 3%

profile of v1, /device:TPU:31, one launch (start us, length us, event | category | flops | bytes accessed | tf_op | source)
XLA Modules:
  0.0 97.3 jit_solution(12980155242027302667)
XLA Ops:
  0.7 1.5 %copy-done.1 = f32[6,12,24,256]{3,2,1,0:T(8,128)S(1)} copy-done((f32[6,12,24,256]{3,2,1,0:T(8,128)S(1)}, f32[6,12,24,256]{3,2,1,0:T(8,128)}, u32[]{:S(2)}) %copy-start.1) | copy-done | bytes 1769496
  5.5 3.7 %collective-permute-start.2 = (f32[24,128]{1,0:T(8,128)S(1)}, f32[24,128]{1,0:T(8,128)S(1)}, u32[]{:S(2)}, u32[]{:S(2)}) collective-permute-start(f32[24,128]{1,0:T(8,128)S(1)} %get-tuple-element.36), channel_id=1, source_target_pairs={{0,4},{1,5},{2,6},{3,7},{4,8},{5,9},{6,10},{7,11},{8,12},{9,13},{1... | collective-permute-start | bytes 36872 | tf_op jit(solution)/shard_map/ppermute | solution.py:31
  10.1 1.8 %collective-permute-start.4 = (f32[24,128]{1,0:T(8,128)S(1)}, f32[24,128]{1,0:T(8,128)S(1)}, u32[]{:S(2)}, u32[]{:S(2)}) collective-permute-start(f32[24,128]{1,0:T(8,128)S(1)} %get-tuple-element.36), channel_id=1, source_target_pairs={{0,12},{1,13},{2,14},{3,15},{4,0},{5,1},{6,2},{7,3},{8,4},{9,5},{1... | collective-permute-start | bytes 36872 | tf_op jit(solution)/shard_map/ppermute | solution.py:31
  12.0 1.4 %collective-permute-done.3 = f32[24,128]{1,0:T(8,128)S(1)} collective-permute-done((f32[24,128]{1,0:T(8,128)S(1)}, f32[24,128]{1,0:T(8,128)S(1)}, u32[]{:S(2)}, u32[]{:S(2)}) %collective-permute-start.3) | collective-permute-done | bytes 12320 | tf_op jit(solution)/shard_map/ppermute | solution.py:31
  14.1 3.0 %collective-permute-start.5 = (f32[24,128]{1,0:T(8,128)S(1)}, f32[24,128]{1,0:T(8,128)S(1)}, u32[]{:S(2)}, u32[]{:S(2)}) collective-permute-start(f32[24,128]{1,0:T(8,128)S(1)} %add_add_fusion.3), channel_id=1, source_target_pairs={{0,1},{1,2},{2,3},{3,4},{4,5},{5,6},{6,7},{7,8},{8,9},{9,10},{10,1... | collective-permute-start | bytes 36872 | tf_op jit(solution)/shard_map/ppermute | solution.py:31
  17.1 2.4 %collective-permute-start.6 = (f32[24,128]{1,0:T(8,128)S(1)}, f32[24,128]{1,0:T(8,128)S(1)}, u32[]{:S(2)}, u32[]{:S(2)}) collective-permute-start(f32[24,128]{1,0:T(8,128)S(1)} %add_add_fusion.3), channel_id=1, source_target_pairs={{0,2},{1,3},{2,4},{3,5},{4,6},{5,7},{6,8},{7,9},{8,10},{9,11},{10,... | collective-permute-start | bytes 36872 | tf_op jit(solution)/shard_map/ppermute | solution.py:31
  19.6 2.9 %collective-permute-start.7 = (f32[24,128]{1,0:T(8,128)S(1)}, f32[24,128]{1,0:T(8,128)S(1)}, u32[]{:S(2)}, u32[]{:S(2)}) collective-permute-start(f32[24,128]{1,0:T(8,128)S(1)} %add_add_fusion.3), channel_id=1, source_target_pairs={{0,3},{1,4},{2,5},{3,6},{4,7},{5,8},{6,9},{7,10},{8,11},{9,12},{10... | collective-permute-start | bytes 36872 | tf_op jit(solution)/shard_map/ppermute | solution.py:31
  23.7 2.6 %collective-permute-done.7 = f32[24,128]{1,0:T(8,128)S(1)} collective-permute-done((f32[24,128]{1,0:T(8,128)S(1)}, f32[24,128]{1,0:T(8,128)S(1)}, u32[]{:S(2)}, u32[]{:S(2)}) %collective-permute-start.7) | collective-permute-done | bytes 12320 | tf_op jit(solution)/shard_map/ppermute | solution.py:31
  27.2 1.5 %copy-done.2 = f32[6,12,24,256]{3,2,1,0:T(8,128)S(1)} copy-done((f32[6,12,24,256]{3,2,1,0:T(8,128)S(1)}, f32[6,12,24,256]{3,2,1,0:T(8,128)}, u32[]{:S(2)}) %copy-start.2) | copy-done | bytes 1769496
  28.6 1.1 %shard_map.184 = (f32[3,12,24,256]{3,2,1,0:T(8,128)S(1)}, f32[72,256]{1,0:T(8,128)S(1)}, f32[40,256]{1,0:T(8,128)S(1)}) custom-call(f32[3,12,24,256]{3,2,1,0:T(8,128)S(1)} %copy-done.5, f32[6,12,24,256]{3,2,1,0:T(8,128)S(1)} %copy-done.2, f32[3,12,24,256]{3,2,1,0:T(8,128)S(1)} %copy-done, f32[96,256]{1,0:T(8,128)S(1)} %collective-permute-done.xr.refs_3_, ...), custom_call_target="tpu_custom_call" | custom-call | tf_op jit(solution)/shard_map/pallas_call | solution.py:20
  29.8 1.4 %collective-permute-start.8 = (f32[72,256]{1,0:T(8,128)S(1)}, f32[72,256]{1,0:T(8,128)S(1)}, u32[]{:S(2)}, u32[]{:S(2)}) collective-permute-start(f32[72,256]{1,0:T(8,128)S(1)} %get-tuple-element.38), channel_id=1, source_target_pairs={{0,112},{16,0},{32,16},{48,32},{64,48},{80,64},{96,80},{112,96},{1... | collective-permute-start | bytes 221192 | tf_op jit(solution)/shard_map/ppermute | solution.py:31
  31.2 3.0 %collective-permute-start.9 = (f32[40,256]{1,0:T(8,128)S(1)}, f32[40,256]{1,0:T(8,128)S(1)}, u32[]{:S(2)}, u32[]{:S(2)}) collective-permute-start(f32[40,256]{1,0:T(8,128)S(1)} %get-tuple-element.39), channel_id=1, source_target_pairs={{0,15},{1,0},{2,1},{3,2},{4,3},{5,4},{6,5},{7,6},{8,7},{9,8},{10,9... | collective-permute-start | bytes 122888 | tf_op jit(solution)/shard_map/ppermute | solution.py:31
  35.2 1.2 %shard_map.186 = (f32[6,12,24,256]{3,2,1,0:T(8,128)S(1)}, f32[24,128]{1,0:T(8,128)S(1)}, f32[72,256]{1,0:T(8,128)S(1)}, f32[40,256]{1,0:T(8,128)S(1)}) custom-call(f32[6,12,24,256]{3,2,1,0:T(8,128)S(1)} %copy-done.2, f32[3,12,24,256]{3,2,1,0:T(8,128)S(1)} %get-tuple-element.37.refs_1_.refs_0_, f32[3,12,24,256]{3,2,1,0:T(8,128)S(1)} %copy-done, ...), custom_call_target="tpu_custom_call" | custom-call | tf_op jit(solution)/shard_map/pallas_call | solution.py:20
  36.4 3.4 %collective-permute-start.10 = (f32[72,256]{1,0:T(8,128)S(1)}, f32[72,256]{1,0:T(8,128)S(1)}, u32[]{:S(2)}, u32[]{:S(2)}) collective-permute-start(f32[72,256]{1,0:T(8,128)S(1)} %get-tuple-element.41), channel_id=1, source_target_pairs={{0,16},{16,32},{32,48},{48,64},{64,80},{80,96},{96,112},{112,0},{1... | collective-permute-start | bytes 221192 | tf_op jit(solution)/shard_map/ppermute | solution.py:31
  40.5 1.9 %collective-permute-done.11.refs_4_ = f32[40,256]{1,0:T(8,128)S(1)} collective-permute-done((f32[40,256]{1,0:T(8,128)S(1)}, f32[40,256]{1,0:T(8,128)S(1)}, u32[]{:S(2)}, u32[]{:S(2)}) %collective-permute-start.11) | collective-permute-done | bytes 40992 | tf_op jit(solution)/shard_map/ppermute | solution.py:31
  43.5 1.7 %collective-permute-start.12 = (f32[104,256]{1,0:T(8,128)S(1)}, f32[104,256]{1,0:T(8,128)S(1)}, u32[]{:S(2)}, u32[]{:S(2)}) collective-permute-start(f32[104,256]{1,0:T(8,128)S(1)} %get-tuple-element.45), channel_id=1, source_target_pairs={{0,112},{16,0},{32,16},{48,32},{64,48},{80,64},{96,80},{112,96},{1... | collective-permute-start | bytes 319496 | tf_op jit(solution)/shard_map/ppermute | solution.py:31
  45.2 6.6 %collective-permute-start.13 = (f32[56,256]{1,0:T(8,128)S(1)}, f32[56,256]{1,0:T(8,128)S(1)}, u32[]{:S(2)}, u32[]{:S(2)}) collective-permute-start(f32[56,256]{1,0:T(8,128)S(1)} %get-tuple-element.46), channel_id=1, source_target_pairs={{0,15},{1,0},{2,1},{3,2},{4,3},{5,4},{6,5},{7,6},{8,7},{9,8},{10,9... | collective-permute-start | bytes 172040 | tf_op jit(solution)/shard_map/ppermute | solution.py:31
  52.7 1.2 %shard_map.188 = (f32[6,12,24,256]{3,2,1,0:T(8,128)S(1)}, f32[24,128]{1,0:T(8,128)S(1)}, f32[72,256]{1,0:T(8,128)S(1)}, f32[40,256]{1,0:T(8,128)S(1)}) custom-call(f32[6,12,24,256]{3,2,1,0:T(8,128)S(1)} %get-tuple-element.40.refs_1_.refs_0_, f32[3,12,24,256]{3,2,1,0:T(8,128)S(1)} %get-tuple-element.47.refs_1_.refs_0_, f32[3,12,24,256]{3,2,1,0:T(8,128)S(1)} %copy-done, ...), custom_call_target="tpu_custom_call" | custom-call | tf_op jit(solution)/shard_map/pallas_call | solution.py:20
  54.0 2.2 %collective-permute-start.14 = (f32[72,256]{1,0:T(8,128)S(1)}, f32[72,256]{1,0:T(8,128)S(1)}, u32[]{:S(2)}, u32[]{:S(2)}) collective-permute-start(f32[72,256]{1,0:T(8,128)S(1)} %get-tuple-element.50), channel_id=1, source_target_pairs={{0,16},{16,32},{32,48},{48,64},{64,80},{80,96},{96,112},{112,0},{1... | collective-permute-start | bytes 221192 | tf_op jit(solution)/shard_map/ppermute | solution.py:31
  56.2 2.9 %collective-permute-done.15.refs_4_ = f32[40,256]{1,0:T(8,128)S(1)} collective-permute-done((f32[40,256]{1,0:T(8,128)S(1)}, f32[40,256]{1,0:T(8,128)S(1)}, u32[]{:S(2)}, u32[]{:S(2)}) %collective-permute-start.15) | collective-permute-done | bytes 40992 | tf_op jit(solution)/shard_map/ppermute | solution.py:31
  59.1 2.1 %shard_map.189 = (f32[3,12,24,256]{3,2,1,0:T(8,128)}, f32[72,256]{1,0:T(8,128)S(1)}, f32[40,256]{1,0:T(8,128)}, f32[24,128]{1,0:T(8,128)S(1)}) custom-call(f32[3,12,24,256]{3,2,1,0:T(8,128)S(1)} %get-tuple-element.47.refs_1_.refs_0_, f32[6,12,24,256]{3,2,1,0:T(8,128)S(1)} %get-tuple-element.49.refs_1_.refs_0_, f32[3,12,24,256]{3,2,1,0:T(8,128)S(1)} %copy-done, ...), custom_call_target="tpu_custom_call" | custom-call | tf_op jit(solution)/shard_map/pallas_call | solution.py:20
  61.1 2.1 %collective-permute-start.17 = (f32[24,128]{1,0:T(8,128)S(1)}, f32[24,128]{1,0:T(8,128)S(1)}, u32[]{:S(2)}, u32[]{:S(2)}) collective-permute-start(f32[24,128]{1,0:T(8,128)S(1)} %get-tuple-element.52), channel_id=1, source_target_pairs={{0,8},{1,9},{2,10},{3,11},{4,12},{5,13},{6,14},{7,15},{8,0},{9,1},... | collective-permute-start | bytes 36872 | tf_op jit(solution)/shard_map/ppermute | solution.py:31
  63.2 3.3 %collective-permute-start.18 = (f32[24,128]{1,0:T(8,128)S(1)}, f32[24,128]{1,0:T(8,128)S(1)}, u32[]{:S(2)}, u32[]{:S(2)}) collective-permute-start(f32[24,128]{1,0:T(8,128)S(1)} %get-tuple-element.52), channel_id=1, source_target_pairs={{0,12},{1,13},{2,14},{3,15},{4,0},{5,1},{6,2},{7,3},{8,4},{9,5},{1... | collective-permute-start | bytes 36872 | tf_op jit(solution)/shard_map/ppermute | solution.py:31
  67.9 4.8 %collective-permute-start.19 = (f32[24,128]{1,0:T(8,128)S(1)}, f32[24,128]{1,0:T(8,128)S(1)}, u32[]{:S(2)}, u32[]{:S(2)}) collective-permute-start(f32[24,128]{1,0:T(8,128)S(1)} %add_add_fusion.1), channel_id=1, source_target_pairs={{0,1},{1,2},{2,3},{3,4},{4,5},{5,6},{6,7},{7,8},{8,9},{9,10},{10,1... | collective-permute-start | bytes 36872 | tf_op jit(solution)/shard_map/ppermute | solution.py:31
  72.7 8.1 %collective-permute-start.20 = (f32[24,128]{1,0:T(8,128)S(1)}, f32[24,128]{1,0:T(8,128)S(1)}, u32[]{:S(2)}, u32[]{:S(2)}) collective-permute-start(f32[24,128]{1,0:T(8,128)S(1)} %add_add_fusion.1), channel_id=1, source_target_pairs={{0,2},{1,3},{2,4},{3,5},{4,6},{5,7},{6,8},{7,9},{8,10},{9,11},{10,... | collective-permute-start | bytes 36872 | tf_op jit(solution)/shard_map/ppermute | solution.py:31
  81.3 1.7 %collective-permute-start.23 = (f32[72,256]{1,0:T(8,128)S(1)}, f32[72,256]{1,0:T(8,128)S(1)}, u32[]{:S(2)}, u32[]{:S(2)}) collective-permute-start(f32[72,256]{1,0:T(8,128)S(1)} %get-tuple-element.56), channel_id=1, source_target_pairs={{0,112},{16,0},{32,16},{48,32},{64,48},{80,64},{96,80},{112,96},{1... | collective-permute-start | bytes 221192 | tf_op jit(solution)/shard_map/ppermute | solution.py:31
  83.2 4.4 %collective-permute-done.21 = f32[24,128]{1,0:T(8,128)S(1)} collective-permute-done((f32[24,128]{1,0:T(8,128)S(1)}, f32[24,128]{1,0:T(8,128)S(1)}, u32[]{:S(2)}, u32[]{:S(2)}) %collective-permute-start.21) | collective-permute-done | bytes 12320 | tf_op jit(solution)/shard_map/ppermute | solution.py:31
  87.6 1.7 %collective-permute-start.22 = (f32[6,128]{1,0:T(8,128)S(1)}, f32[6,128]{1,0:T(8,128)S(1)}, u32[]{:S(2)}, u32[]{:S(2)}) collective-permute-start(f32[6,128]{1,0:T(8,128)S(1)} %concatenate.3), channel_id=1, source_target_pairs={{0,112},{16,0},{32,16},{48,32},{64,48},{80,64},{96,80},{112,96},{1... | collective-permute-start | bytes 9224 | tf_op jit(solution)/shard_map/ppermute | solution.py:31
  89.4 2.9 %collective-permute-done.22.rest_next = f32[6,128]{1,0:T(8,128)S(1)} collective-permute-done((f32[6,128]{1,0:T(8,128)S(1)}, f32[6,128]{1,0:T(8,128)S(1)}, u32[]{:S(2)}, u32[]{:S(2)}) %collective-permute-start.22) | collective-permute-done | bytes 3104 | tf_op jit(solution)/shard_map/ppermute | solution.py:31
  92.3 1.3 %shard_map.190 = (f32[3,4,16,128]{3,2,1,0:T(8,128)}, f32[6,4,16,128]{3,2,1,0:T(8,128)}) custom-call(f32[3,4,16,128]{3,2,1,0:T(8,128)S(1)} %get-tuple-element.35.cv, f32[6,4,16,128]{3,2,1,0:T(8,128)S(1)} %copy-done.4, f32[3,4,16,128]{3,2,1,0:T(8,128)S(1)} %copy-done.8, f32[104,256]{1,0:T(8,128)S(1)} %collective-permute-done.12.refs_3_.xr, ...), custom_call_target="tpu_custom_call" | custom-call | tf_op jit(solution)/shard_map/pallas_call | solution.py:20
  93.6 1.2 %copy-done.6 = f32[3,12,24,256]{3,2,1,0:T(8,128)S(1)} copy-done((f32[3,12,24,256]{3,2,1,0:T(8,128)S(1)}, f32[3,12,24,256]{3,2,1,0:T(8,128)}, u32[]{:S(2)}) %copy-start.6) | copy-done | bytes 884760
  94.8 2.5 %shard_map.191 = (f32[6,12,24,256]{3,2,1,0:T(8,128)}, f32[12,24]{1,0:T(8,128)}) custom-call(f32[6,12,24,256]{3,2,1,0:T(8,128)S(1)} %get-tuple-element.49.refs_1_.refs_0_, f32[3,12,24,256]{3,2,1,0:T(8,128)S(1)} %copy-done.6, f32[3,12,24,256]{3,2,1,0:T(8,128)S(1)} %copy-done, f32[72,256]{1,0:T(8,128)S(1)} %collective-permute-done.23.refs_3_, ...), custom_call_target="tpu_custom_call" | custom-call | tf_op jit(solution)/shard_map/pallas_call | solution.py:20
  (74 shorter events, 12.7 us)
Async XLA Ops:
  0.6 26.5 %copy-start = (f32[3,12,24,256]{3,2,1,0:T(8,128)S(1)}, f32[3,12,24,256]{3,2,1,0:T(8,128)}, u32[]{:S(2)}) copy-start(f32[3,12,24,256]{3,2,1,0:T(8,128)} %refs_2_.11) | copy-start | bytes 2654212
  4.8 18.1 %copy-start.14 = (s32[12,24]{1,0:T(8,128)S(1)}, s32[12,24]{1,0:T(8,128)}, u32[]{:S(2)}) copy-start(s32[12,24]{1,0:T(8,128)} %mask.1) | copy-start | bytes 3460
  4.8 18.1 %copy-start.15 = (s32[12,24]{1,0:T(8,128)S(1)}, s32[12,24]{1,0:T(8,128)}, u32[]{:S(2)}) copy-start(s32[12,24]{1,0:T(8,128)} %zone.1) | copy-start | bytes 3460
  4.8 18.1 %copy-start.16 = (f32[4]{0:T(128)S(1)}, f32[4]{0:T(128)}, u32[]{:S(2)}) copy-start(f32[4]{0:T(128)} %static.1) | copy-start | bytes 52
  4.8 18.1 %copy-start.17 = (f32[4]{0:T(128)S(1)}, f32[4]{0:T(128)}, u32[]{:S(2)}) copy-start(f32[4]{0:T(128)} %drop.1) | copy-start | bytes 52
  4.8 22.3 %copy-start.5 = (f32[3,12,24,256]{3,2,1,0:T(8,128)S(1)}, f32[3,12,24,256]{3,2,1,0:T(8,128)}, u32[]{:S(2)}) copy-start(f32[3,12,24,256]{3,2,1,0:T(8,128)} %refs_0_.2) | copy-start | bytes 2654212
  5.5 6.5 %collective-permute-start.2 = (f32[24,128]{1,0:T(8,128)S(1)}, f32[24,128]{1,0:T(8,128)S(1)}, u32[]{:S(2)}, u32[]{:S(2)}) collective-permute-start(f32[24,128]{1,0:T(8,128)S(1)} %get-tuple-element.36), channel_id=1, source_target_pairs={{0,4},{1,5},{2,6},{3,7},{4,8},{5,9},{6,10},{7,11},{8,12},{9,13},{1... | collective-permute-start | bytes 36872 | tf_op jit(solution)/shard_map/ppermute | solution.py:31
  9.1 4.3 %collective-permute-start.3 = (f32[24,128]{1,0:T(8,128)S(1)}, f32[24,128]{1,0:T(8,128)S(1)}, u32[]{:S(2)}, u32[]{:S(2)}) collective-permute-start(f32[24,128]{1,0:T(8,128)S(1)} %get-tuple-element.36), channel_id=1, source_target_pairs={{0,8},{1,9},{2,10},{3,11},{4,12},{5,13},{6,14},{7,15},{8,0},{9,1},... | collective-permute-start | bytes 36872 | tf_op jit(solution)/shard_map/ppermute | solution.py:31
  10.1 4.0 %collective-permute-start.4 = (f32[24,128]{1,0:T(8,128)S(1)}, f32[24,128]{1,0:T(8,128)S(1)}, u32[]{:S(2)}, u32[]{:S(2)}) collective-permute-start(f32[24,128]{1,0:T(8,128)S(1)} %get-tuple-element.36), channel_id=1, source_target_pairs={{0,12},{1,13},{2,14},{3,15},{4,0},{5,1},{6,2},{7,3},{8,4},{9,5},{1... | collective-permute-start | bytes 36872 | tf_op jit(solution)/shard_map/ppermute | solution.py:31
  14.1 9.5 %collective-permute-start.5 = (f32[24,128]{1,0:T(8,128)S(1)}, f32[24,128]{1,0:T(8,128)S(1)}, u32[]{:S(2)}, u32[]{:S(2)}) collective-permute-start(f32[24,128]{1,0:T(8,128)S(1)} %add_add_fusion.3), channel_id=1, source_target_pairs={{0,1},{1,2},{2,3},{3,4},{4,5},{5,6},{6,7},{7,8},{8,9},{9,10},{10,1... | collective-permute-start | bytes 36872 | tf_op jit(solution)/shard_map/ppermute | solution.py:31
  17.1 6.5 %collective-permute-start.6 = (f32[24,128]{1,0:T(8,128)S(1)}, f32[24,128]{1,0:T(8,128)S(1)}, u32[]{:S(2)}, u32[]{:S(2)}) collective-permute-start(f32[24,128]{1,0:T(8,128)S(1)} %add_add_fusion.3), channel_id=1, source_target_pairs={{0,2},{1,3},{2,4},{3,5},{4,6},{5,7},{6,8},{7,9},{8,10},{9,11},{10,... | collective-permute-start | bytes 36872 | tf_op jit(solution)/shard_map/ppermute | solution.py:31
  19.6 6.7 %collective-permute-start.7 = (f32[24,128]{1,0:T(8,128)S(1)}, f32[24,128]{1,0:T(8,128)S(1)}, u32[]{:S(2)}, u32[]{:S(2)}) collective-permute-start(f32[24,128]{1,0:T(8,128)S(1)} %add_add_fusion.3), channel_id=1, source_target_pairs={{0,3},{1,4},{2,5},{3,6},{4,7},{5,8},{6,9},{7,10},{8,11},{9,12},{10... | collective-permute-start | bytes 36872 | tf_op jit(solution)/shard_map/ppermute | solution.py:31
  22.5 4.6 %collective-permute-start = (f32[96,256]{1,0:T(8,128)S(1)}, f32[96,256]{1,0:T(8,128)S(1)}, u32[]{:S(2)}, u32[]{:S(2)}) collective-permute-start(f32[96,256]{1,0:T(8,128)S(1)} %get-tuple-element.33), channel_id=1, source_target_pairs={{0,16},{16,32},{32,48},{48,64},{64,80},{80,96},{96,112},{112,0},{1... | collective-permute-start | bytes 294920 | tf_op jit(solution)/shard_map/ppermute | solution.py:31
  22.9 3.4 %collective-permute-start.1 = (f32[56,256]{1,0:T(8,128)S(1)}, f32[56,256]{1,0:T(8,128)S(1)}, u32[]{:S(2)}, u32[]{:S(2)}) collective-permute-start(f32[56,256]{1,0:T(8,128)S(1)} %get-tuple-element.34), channel_id=1, source_target_pairs={{0,1},{1,2},{2,3},{3,4},{4,5},{5,6},{6,7},{7,8},{8,9},{9,10},{10,1... | collective-permute-start | bytes 172040 | tf_op jit(solution)/shard_map/ppermute | solution.py:31
  29.8 5.4 %collective-permute-start.8 = (f32[72,256]{1,0:T(8,128)S(1)}, f32[72,256]{1,0:T(8,128)S(1)}, u32[]{:S(2)}, u32[]{:S(2)}) collective-permute-start(f32[72,256]{1,0:T(8,128)S(1)} %get-tuple-element.38), channel_id=1, source_target_pairs={{0,112},{16,0},{32,16},{48,32},{64,48},{80,64},{96,80},{112,96},{1... | collective-permute-start | bytes 221192 | tf_op jit(solution)/shard_map/ppermute | solution.py:31
  31.2 3.8 %collective-permute-start.9 = (f32[40,256]{1,0:T(8,128)S(1)}, f32[40,256]{1,0:T(8,128)S(1)}, u32[]{:S(2)}, u32[]{:S(2)}) collective-permute-start(f32[40,256]{1,0:T(8,128)S(1)} %get-tuple-element.39), channel_id=1, source_target_pairs={{0,15},{1,0},{2,1},{3,2},{4,3},{5,4},{6,5},{7,6},{8,7},{9,8},{10,9... | collective-permute-start | bytes 122888 | tf_op jit(solution)/shard_map/ppermute | solution.py:31
  36.4 6.0 %collective-permute-start.10 = (f32[72,256]{1,0:T(8,128)S(1)}, f32[72,256]{1,0:T(8,128)S(1)}, u32[]{:S(2)}, u32[]{:S(2)}) collective-permute-start(f32[72,256]{1,0:T(8,128)S(1)} %get-tuple-element.41), channel_id=1, source_target_pairs={{0,16},{16,32},{32,48},{48,64},{64,80},{80,96},{96,112},{112,0},{1... | collective-permute-start | bytes 221192 | tf_op jit(solution)/shard_map/ppermute | solution.py:31
  39.8 2.6 %collective-permute-start.11 = (f32[40,256]{1,0:T(8,128)S(1)}, f32[40,256]{1,0:T(8,128)S(1)}, u32[]{:S(2)}, u32[]{:S(2)}) collective-permute-start(f32[40,256]{1,0:T(8,128)S(1)} %get-tuple-element.42), channel_id=1, source_target_pairs={{0,1},{1,2},{2,3},{3,4},{4,5},{5,6},{6,7},{7,8},{8,9},{9,10},{10,1... | collective-permute-start | bytes 122888 | tf_op jit(solution)/shard_map/ppermute | solution.py:31
  43.5 9.2 %collective-permute-start.12 = (f32[104,256]{1,0:T(8,128)S(1)}, f32[104,256]{1,0:T(8,128)S(1)}, u32[]{:S(2)}, u32[]{:S(2)}) collective-permute-start(f32[104,256]{1,0:T(8,128)S(1)} %get-tuple-element.45), channel_id=1, source_target_pairs={{0,112},{16,0},{32,16},{48,32},{64,48},{80,64},{96,80},{112,96},{1... | collective-permute-start | bytes 319496 | tf_op jit(solution)/shard_map/ppermute | solution.py:31
  45.2 7.5 %collective-permute-start.13 = (f32[56,256]{1,0:T(8,128)S(1)}, f32[56,256]{1,0:T(8,128)S(1)}, u32[]{:S(2)}, u32[]{:S(2)}) collective-permute-start(f32[56,256]{1,0:T(8,128)S(1)} %get-tuple-element.46), channel_id=1, source_target_pairs={{0,15},{1,0},{2,1},{3,2},{4,3},{5,4},{6,5},{7,6},{8,7},{9,8},{10,9... | collective-permute-start | bytes 172040 | tf_op jit(solution)/shard_map/ppermute | solution.py:31
  54.0 5.1 %collective-permute-start.14 = (f32[72,256]{1,0:T(8,128)S(1)}, f32[72,256]{1,0:T(8,128)S(1)}, u32[]{:S(2)}, u32[]{:S(2)}) collective-permute-start(f32[72,256]{1,0:T(8,128)S(1)} %get-tuple-element.50), channel_id=1, source_target_pairs={{0,16},{16,32},{32,48},{48,64},{64,80},{80,96},{96,112},{112,0},{1... | collective-permute-start | bytes 221192 | tf_op jit(solution)/shard_map/ppermute | solution.py:31
  56.2 2.9 %collective-permute-start.15 = (f32[40,256]{1,0:T(8,128)S(1)}, f32[40,256]{1,0:T(8,128)S(1)}, u32[]{:S(2)}, u32[]{:S(2)}) collective-permute-start(f32[40,256]{1,0:T(8,128)S(1)} %get-tuple-element.51), channel_id=1, source_target_pairs={{0,1},{1,2},{2,3},{3,4},{4,5},{5,6},{6,7},{7,8},{8,9},{9,10},{10,1... | collective-permute-start | bytes 122888 | tf_op jit(solution)/shard_map/ppermute | solution.py:31
  59.1 33.2 %copy-start.10 = (s32[2,4,128]{2,1,0:T(4,128)S(1)}, s32[2,4,128]{2,1,0:T(4,128)}, u32[]{:S(2)}) copy-start(s32[2,4,128]{2,1,0:T(4,128)} %rows_ref.5) | copy-start | bytes 12292
  61.1 6.5 %collective-permute-start.16 = (f32[24,128]{1,0:T(8,128)S(1)}, f32[24,128]{1,0:T(8,128)S(1)}, u32[]{:S(2)}, u32[]{:S(2)}) collective-permute-start(f32[24,128]{1,0:T(8,128)S(1)} %get-tuple-element.52), channel_id=1, source_target_pairs={{0,4},{1,5},{2,6},{3,7},{4,8},{5,9},{6,10},{7,11},{8,12},{9,13},{1... | collective-permute-start | bytes 36872 | tf_op jit(solution)/shard_map/ppermute | solution.py:31
  61.1 6.5 %collective-permute-start.17 = (f32[24,128]{1,0:T(8,128)S(1)}, f32[24,128]{1,0:T(8,128)S(1)}, u32[]{:S(2)}, u32[]{:S(2)}) collective-permute-start(f32[24,128]{1,0:T(8,128)S(1)} %get-tuple-element.52), channel_id=1, source_target_pairs={{0,8},{1,9},{2,10},{3,11},{4,12},{5,13},{6,14},{7,15},{8,0},{9,1},... | collective-permute-start | bytes 36872 | tf_op jit(solution)/shard_map/ppermute | solution.py:31
  63.2 4.7 %collective-permute-start.18 = (f32[24,128]{1,0:T(8,128)S(1)}, f32[24,128]{1,0:T(8,128)S(1)}, u32[]{:S(2)}, u32[]{:S(2)}) collective-permute-start(f32[24,128]{1,0:T(8,128)S(1)} %get-tuple-element.52), channel_id=1, source_target_pairs={{0,12},{1,13},{2,14},{3,15},{4,0},{5,1},{6,2},{7,3},{8,4},{9,5},{1... | collective-permute-start | bytes 36872 | tf_op jit(solution)/shard_map/ppermute | solution.py:31
  67.9 15.3 %collective-permute-start.19 = (f32[24,128]{1,0:T(8,128)S(1)}, f32[24,128]{1,0:T(8,128)S(1)}, u32[]{:S(2)}, u32[]{:S(2)}) collective-permute-start(f32[24,128]{1,0:T(8,128)S(1)} %add_add_fusion.1), channel_id=1, source_target_pairs={{0,1},{1,2},{2,3},{3,4},{4,5},{5,6},{6,7},{7,8},{8,9},{9,10},{10,1... | collective-permute-start | bytes 36872 | tf_op jit(solution)/shard_map/ppermute | solution.py:31
  72.7 10.5 %collective-permute-start.20 = (f32[24,128]{1,0:T(8,128)S(1)}, f32[24,128]{1,0:T(8,128)S(1)}, u32[]{:S(2)}, u32[]{:S(2)}) collective-permute-start(f32[24,128]{1,0:T(8,128)S(1)} %add_add_fusion.1), channel_id=1, source_target_pairs={{0,2},{1,3},{2,4},{3,5},{4,6},{5,7},{6,8},{7,9},{8,10},{9,11},{10,... | collective-permute-start | bytes 36872 | tf_op jit(solution)/shard_map/ppermute | solution.py:31
  80.9 6.7 %collective-permute-start.21 = (f32[24,128]{1,0:T(8,128)S(1)}, f32[24,128]{1,0:T(8,128)S(1)}, u32[]{:S(2)}, u32[]{:S(2)}) collective-permute-start(f32[24,128]{1,0:T(8,128)S(1)} %add_add_fusion.1), channel_id=1, source_target_pairs={{0,3},{1,4},{2,5},{3,6},{4,7},{5,8},{6,9},{7,10},{8,11},{9,12},{10... | collective-permute-start | bytes 36872 | tf_op jit(solution)/shard_map/ppermute | solution.py:31
  81.3 12.3 %collective-permute-start.23 = (f32[72,256]{1,0:T(8,128)S(1)}, f32[72,256]{1,0:T(8,128)S(1)}, u32[]{:S(2)}, u32[]{:S(2)}) collective-permute-start(f32[72,256]{1,0:T(8,128)S(1)} %get-tuple-element.56), channel_id=1, source_target_pairs={{0,112},{16,0},{32,16},{48,32},{64,48},{80,64},{96,80},{112,96},{1... | collective-permute-start | bytes 221192 | tf_op jit(solution)/shard_map/ppermute | solution.py:31
  83.0 10.6 %collective-permute-start.24 = (f32[40,256]{1,0:T(8,128)}, f32[40,256]{1,0:T(8,128)S(1)}, u32[]{:S(2)}, u32[]{:S(2)}) collective-permute-start(f32[40,256]{1,0:T(8,128)} %get-tuple-element.57), channel_id=1, source_target_pairs={{0,15},{1,0},{2,1},{3,2},{4,3},{5,4},{6,5},{7,6},{8,7},{9,8},{10,9... | collective-permute-start | bytes 122888 | tf_op jit(solution)/shard_map/ppermute | solution.py:31
  87.6 4.6 %collective-permute-start.22 = (f32[6,128]{1,0:T(8,128)S(1)}, f32[6,128]{1,0:T(8,128)S(1)}, u32[]{:S(2)}, u32[]{:S(2)}) collective-permute-start(f32[6,128]{1,0:T(8,128)S(1)} %concatenate.3), channel_id=1, source_target_pairs={{0,112},{16,0},{32,16},{48,32},{64,48},{80,64},{96,80},{112,96},{1... | collective-permute-start | bytes 9224 | tf_op jit(solution)/shard_map/ppermute | solution.py:31
  (12 other events, 88.6 us)

commit v2 on v1

v2 whole, which is shorter than its diff:
```python
import jax
import jax.numpy as jnp
from jax import lax
from jax.experimental import pallas as pl
from jax.experimental.pallas import tpu as pltpu
from jax.sharding import PartitionSpec as P

STEP_RATIO = 0.15
F32 = jnp.float32
FINE_S = (0, 2, 1, 4, 3, 5)
FINE_V = (0, 2, 1)
COARSE_S = (0, 1, 2, 3, 4, 5)
COARSE_V = (0, 1, 2)
VMEM = pl.BlockSpec(memory_space=pltpu.VMEM)
SMEM = pl.BlockSpec(memory_space=pltpu.SMEM)
HBM = pl.BlockSpec(memory_space=pltpu.HBM)
PARAMS = pltpu.CompilerParams(vmem_limit_bytes=32 * 1024 * 1024)


def call(kernel, outs, specs, *args):
    return pl.pallas_call(
        kernel,
        out_shape=tuple(jax.ShapeDtypeStruct(shape, F32) for shape in outs),
        in_specs=list(specs),
        out_specs=tuple(VMEM for _ in outs),
        compiler_params=PARAMS,
    )(*args)


def ring(value, axis, steps):
    count = lax.axis_size(axis)
    return lax.ppermute(value, axis, [(i, (i + steps) % count) for i in range(count)])


def iota(shape, along):
    return lax.broadcasted_iota(jnp.int32, shape, along)


def b_behind(a, edge):
    return jnp.where(iota(a.shape, 0) == 0, edge, pltpu.roll(a, 1, 0))


def b_ahead(a, edge):
    last = a.shape[0] - 1
    return jnp.where(iota(a.shape, 0) == last, edge, pltpu.roll(a, last, 0))


def l_behind(a):
    return jnp.where(iota(a.shape, 1) == 0, 0.0, pltpu.roll(a, 1, 1))


def l_ahead(a):
    last = a.shape[1] - 1
    return jnp.where(iota(a.shape, 1) == last, 0.0, pltpu.roll(a, last, 1))


def velocity_plane(v, s, s_prev, rows, buoyancy, b_back=b_behind, l_back=l_behind):
    xx, bb, ll, xb, xl, bl = s
    p_xx, p_xb, p_xl = s_prev
    r_xb, r_bb, r_bl = rows
    f_x = (xx - p_xx) + (xb - b_back(xb, r_xb)) + (xl - l_back(xl))
    f_b = (xb - p_xb) + (bb - b_back(bb, r_bb)) + (bl - l_back(bl))
    f_l = (xl - p_xl) + (bl - b_back(bl, r_bl)) + (ll - l_back(ll))
    scale = STEP_RATIO * buoyancy
    return (v[0] + scale * f_x, v[1] + scale * f_b, v[2] + scale * f_l)


def stress_plane(s, v, v_next, rows, lame, shear, b_fore=b_ahead, l_fore=l_ahead):
    vx, vb, vl = v
    nx, nb, nl = v_next
    rx, rb, rl = rows
    e_x = nx - vx
    e_b = b_fore(vb, rb) - vb
    e_l = l_fore(vl) - vl
    e_xb = (b_fore(vx, rx) - vx) + (nb - vb)
    e_xl = (l_fore(vx) - vx) + (nl - vl)
    e_bl = (b_fore(vl, rl) - vl) + (l_fore(vb) - vb)
    common = (STEP_RATIO * lame) * (e_x + e_b + e_l)
    one = STEP_RATIO * shear
    two = 2.0 * one
    return (
        s[0] + (common + two * e_x),
        s[1] + (common + two * e_b),
        s[2] + (common + two * e_l),
        s[3] + one * e_xb,
        s[4] + one * e_xl,
        s[5] + one * e_bl,
    )


BEFORE_X, AFTER_X, BEFORE_Z, AFTER_Z, FIRST_CELL, FIRST_ROW = range(6)


def make_flags(cells, rows):
    gx, gy = lax.axis_index("gx"), lax.axis_index("gy")
    last_x, last_y = lax.axis_size("gx") - 1, lax.axis_size("gy") - 1
    values = (gx > 0, gx < last_x, gy > 0, gy < last_y, gy * cells, gy * rows, gx, gy)
    values = jnp.stack([jnp.asarray(v).astype(F32) for v in values])
    return jnp.broadcast_to(values[:, None], (8, 256))


def has(flags, which):
    return flags[which : which + 1, :] > 0.5


def own_cells(flags, depth):
    shape = (depth, 128)
    row = iota(shape, 0)
    cell = iota(shape, 1) - jnp.where(row < 27, row // 3, -1)
    return cell.astype(F32) == flags[FIRST_CELL : FIRST_CELL + 1, 0:128]


def own_rows(flags, shape):
    return iota(shape, 0).astype(F32) + flags[FIRST_ROW : FIRST_ROW + 1, 0:128]


RIM = 8


def part_of(field, refs):
    if field < 3:
        return refs[0], field
    if field < 9:
        return refs[1], field - 3
    return refs[2], field - 9


def pack_kernel(
    fv, fs, fm, cs, cv, cm, slip, shear, normal, mask, zone, rows_hbm, flags,
    up, down, coupling, raw,
    top_v, top_s, top_m, low_v, low_s, low_m, cz_buf, cv_buf, cs_low, cm_low, rows_ref, slip_buf, shear_buf, normal_buf, mask_buf, zone_buf, turn, sem,
):
    nx, nz, ny = fv.shape[1:]
    cx, cy, cz = cs.shape[1:]
    fault = (slip_buf, shear_buf, normal_buf, mask_buf, zone_buf)
    moves = [(cv, cv_buf), (rows_hbm, rows_ref)]
    moves += list(zip((slip, shear, normal, mask, zone), fault))
    for k, c in enumerate((3, 1, 5)):
        moves.append((cs.at[c, :, cy - 8 : cy, :], cz_buf.at[k]))
    moves.append((cs.at[:, :, 0:8, :], cs_low))
    moves.append((cm.at[0, :, 0:8, :], cm_low))
    early = len(moves)
    for src, top, low in ((fv, top_v, low_v), (fs, top_s, low_s), (fm, top_m, low_m)):
        moves.append((src.at[:, :, nz - 8 : nz, :], top))
        moves.append((src.at[:, :, 0:8, :], low))
    copies = [pltpu.make_async_copy(src, dst, sem.at[i]) for i, (src, dst) in enumerate(moves)]
    for copy in copies:
        copy.start()
    for copy in copies[:early]:
        copy.wait()
    for f in range(2):
        for x in range(cx):
            here = own_rows(flags, (cy, cz)) == rows_ref[f, x : x + 1, :].astype(F32)
            for c in range(3):
                row = jnp.sum(jnp.where(here, cv_buf[c, x], 0.0), axis=0, keepdims=True)
                at = (f * 3 + c) * cx + x
                coupling[at : at + 1, :] = row
    turn[...] = jnp.zeros_like(turn)
    for k, ref in enumerate(fault):
        turn[16 * k : 16 * k + nx, 0:nz] = ref[...].astype(F32)
    turned = turn[...].T[0:nz]
    raw[...] = turned
    at = nx * 32
    up[at:, :] = jnp.zeros((24, ny), F32)
    for k in range(3):
        for x in range(cx):
            up[at + k * cx + x : at + k * cx + x + 1, 0:128] = cz_buf[k, x, 7:8]
    up[at + 16 : at + 24, 0:128] = turned[nz - 8 :]
    down[nx * 40 :, :] = jnp.zeros((48, ny), F32)
    down[nx * 40 : nx * 40 + 8, 0:128] = turned[0:8]
    for c in range(10):
        for x in range(cx):
            if c < 3:
                row = cv_buf[c, x, 0:1]
            elif c < 9:
                row = cs_low[c - 3, x, 0:1]
            else:
                row = cm_low[x, 0:1]
            at = nx * 40 + 8 + c * cx + x
            down[at : at + 1, 0:128] = row
    for copy in copies[early:]:
        copy.wait()
    tops, lows = (top_v, top_s, top_m), (low_v, low_s, low_m)
    sub = iota((RIM, ny), 0)

    def rolled(tile, by):
        return pltpu.roll(tile, by % RIM, 0) if by % RIM else tile

    def step(x, _):
        def take(refs, field):
            ref, c = part_of(field, refs)
            return ref[c, x]

        for t in range(3):
            tile = rolled(take(tops, 4 * t), -6)
            for i in range(1, 4):
                tile = jnp.where(sub // 2 == i, rolled(take(tops, 4 * t + i), 2 * i - 6), tile)
            up[pl.ds(x * 32 + 8 * t, 8), :] = tile
        tile = rolled(take(tops, 3 + 2), -5)
        tile = jnp.where(sub == 1, rolled(take(tops, 3 + 4), -4), tile)
        tile = jnp.where(sub == 2, rolled(take(tops, 3 + 5), -3), tile)
        up[pl.ds(x * 32 + 24, 8), :] = tile
        for t in range(5):
            tile = jnp.where(sub < 3, take(lows, 2 * t), rolled(take(lows, 2 * t + 1), 3))
            if t < 2:
                tile = jnp.where(sub < 6, tile, rolled(take(lows, 10 + t), 6))
            down[pl.ds(x * 40 + 8 * t, 8), :] = tile
        return 0

    lax.fori_loop(0, nx, step, 0)


def rim_kernel(from_below, from_above, fs, cs, raw, parts_of, flags, left, right, rim, xsend, settings, total):
    total[...] = left[...] + right[...]
    nx, nz, ny = fs.shape[1:]
    cx = cs.shape[1]
    has_below, has_above = has(flags, BEFORE_Z), has(flags, AFTER_Z)
    sub = iota((RIM, ny), 0)

    def rolled(tile, by):
        return pltpu.roll(tile, by % RIM, 0) if by % RIM else tile

    def step(x, _):
        last = jnp.where(has_below, from_below[pl.ds(x * 32 + 24, 8), :], 0.0)
        for t in range(3):
            tile = jnp.where(has_below, from_below[pl.ds(x * 32 + 8 * t, 8), :], 0.0)
            for i in range(4):
                field = 4 * t + i
                below = rolled(tile, 6 - 2 * i)
                extra = {5: 5, 7: 4, 8: 3}.get(field)
                if extra is not None:
                    below = jnp.where(sub == 5, rolled(last, extra), below)
                t2, i2 = divmod(field, 2)
                if field < 10:
                    above = from_above[pl.ds(x * 40 + 8 * t2, 8), :]
                    above = rolled(above, -3 * i2)
                else:
                    above = rolled(from_above[pl.ds(x * 40 + 8 * (field - 10), 8), :], 2)
                above = jnp.where(has_above, above, 0.0)
                rim[field, x] = jnp.where(sub < 4, above, below)
        return 0

    lax.fori_loop(0, nx, step, 0)
    for k, c in enumerate((0, 4, 3)):
        xsend[32 * k : 32 * k + nz, :] = fs[c, nx - 1]
        xsend[32 * k + nz : 32 * k + 32, :] = rim[3 + c, nx - 1]
    for k, c in enumerate((0, 3, 4)):
        xsend[96 + 8 * k : 104 + 8 * k, 0:128] = cs[c, cx - 1, 0:8]
        xsend[96 + 8 * k : 104 + 8 * k, 128:256] = cs[c, cx - 1, 8:16]
    xsend[120:, :] = jnp.zeros((8, ny), F32)
    for k, c in enumerate((0, 3, 4)):
        at = nx * 40 + 8 + (3 + c) * cx + cx - 1
        xsend[120 + k : 121 + k, 0:128] = jnp.where(has_above[:, 0:128], from_above[at : at + 1, 0:128], 0.0)
    below = jnp.where(has_below[:, 0:128], from_below[nx * 32 + 16 :, 0:128], 0.0)
    above = jnp.where(has_above[:, 0:128], from_above[nx * 40 : nx * 40 + 8, 0:128], 0.0)
    turned = jnp.concatenate([raw[...], jnp.where(iota((RIM, 128), 0) < 4, above, below)], axis=0)
    settings[0] = turned
    for k in (1, 2, 3):
        settings[k] = pltpu.roll(turned, 128 - 16 * k, 1)
    zones = pltpu.roll(turned, 128 - 64, 1)
    for k in range(3):
        value = jnp.zeros_like(turned)
        for zone in range(4):
            value = jnp.where(zones == float(zone), parts_of[4 * k + zone : 4 * k + zone + 1, :], value)
        settings[4 + k] = value


def ring_back(a, _):
    return pltpu.roll(a, 1, 0)


def ring_fore(a, _):
    return pltpu.roll(a, a.shape[0] - 1, 0)


def reader(ref, rim, first):
    if ref.shape[2] == 32:
        return lambda c, x: ref[c, x]
    return lambda c, x: jnp.concatenate([ref[c, x], rim[first + c, x]], axis=0)


def held_column(bounds, cells, face, c, x):
    at = (face * 3 + c) * (bounds.shape[0] // 6) + x
    return jnp.sum(jnp.where(cells, bounds[at : at + 1, :], 0.0), axis=1, keepdims=True)


def held(value, columns):
    lane = iota(value.shape, 1)
    value = jnp.where(lane == 0, columns[0], value)
    return jnp.where(lane == value.shape[1] - 1, columns[1], value)


def merged(a):
    return jnp.where(iota((a.shape[0], 128), 1) < 64, a[:, 0:128], a[:, a.shape[1] - 128 :])


def fine_velocity_kernel(step, v_ref, s_ref, m_ref, rim, xr, bounds_a, bounds_b, flags, *refs):
    refs = list(refs)
    if step == 1:
        cxs = refs.pop(0)
    if step == 2:
        left, right = refs.pop(0), refs.pop(0)
        refs.pop()[...] = left[...] + right[...]
    out, xsend = refs
    bounds = bounds_a[...] + bounds_b[...]
    v, s, m = reader(v_ref, rim, 0), reader(s_ref, rim, 3), reader(m_ref, rim, 9)
    nx, nz, ny = v_ref.shape[1], 32, v_ref.shape[3]
    cells = own_cells(flags, nz)
    has_x = has(flags, BEFORE_X)
    for x in range(nx):
        here = [s(c, x) for c in FINE_S]
        if x % 3 == 0:
            columns = [[held_column(bounds, cells, f, c, x // 3) for f in range(2)] for c in range(3)]
        if x == 0:
            before = [jnp.where(has_x, xr[k * nz : (k + 1) * nz, :], 0.0) for k in range(3)]
        else:
            before = [s(c, x - 1) for c in (0, 4, 3)]
        old = [v(c, x) for c in FINE_V]
        buoyancy = m(0, x)
        new = velocity_plane(old, here, before, (0.0,) * 3, buoyancy, ring_back)
        for k, c in enumerate(FINE_V):
            val = held(new[k], columns[c])
            out[c, x] = val
            if x == 0:
                xsend[k * nz : (k + 1) * nz, :] = val
        if step == 0 and x == 0:
            xsend[3 * nz :, :] = jnp.zeros_like(xsend[3 * nz :, :])
            xsend[3 * nz :, 0:128] = merged(buoyancy)[0:16]
            xsend[3 * nz : 3 * nz + 8, 128:256] = merged(buoyancy)[16:24]
    if step == 1:
        xsend[3 * nz :, :] = cxs[...]


def share_kernel(v, s, m, xr, bounds_a, bounds_b, flags, share):
    nx, nz, ny = v.shape[1:]
    cx, own = nx // 3, nz - RIM
    bounds = bounds_a[...] + bounds_b[...]
    lane = iota((own, 128), 1)
    cells = own_cells(flags, own)

    def l_back(a):
        return pltpu.roll(a, 1, 1)

    columns = [[[held_column(bounds, cells, f, c, x) for f in range(2)] for c in range(3)] for x in range(cx)]
    sums = {}
    before = [jnp.zeros((own, 128), F32)] * 3
    for x in range(nx):
        here = [merged(s[c, x]) for c in FINE_S]
        old = [merged(v[c, x, 0:own, :]) for c in FINE_V]
        rows = [here[k][nz - 1 : nz] for k in (3, 1, 5)]
        here = [a[0:own] for a in here]
        new = velocity_plane(old, here, before, rows, merged(m[0, x]), b_behind, l_back)
        before = [here[0], here[3], here[4]]
        for k, c in enumerate(FINE_V):
            val = held(new[k], columns[x // 3][c])
            sums[c, x // 3] = val if x % 3 == 0 else sums[c, x // 3] + val
    buoyancy = jnp.concatenate([xr[96:112, 0:128], xr[96:104, 128:256]], axis=0)
    ahead = [-STEP_RATIO * buoyancy * plane for plane in before]
    for f in range(2):
        face = lane < 3 if f == 0 else lane >= 125
        free = (lane == 1) | (lane == 2) if f == 0 else (lane == 125) | (lane == 126)
        for k, c in enumerate(FINE_V):
            at = f * 3 + c
            for x in range(cx):
                total = jnp.sum(jnp.where(face, sums[c, x], 0.0), axis=1, keepdims=True)
                row = jnp.sum(jnp.where(cells, total, 0.0), axis=0, keepdims=True)
                share[at * cx + x : at * cx + x + 1, :] = row * (1.0 / 27.0)
            total = jnp.sum(jnp.where(free, ahead[k], 0.0), axis=1, keepdims=True)
            row = jnp.sum(jnp.where(cells, total, 0.0), axis=0, keepdims=True)
            share[6 * cx + at : 6 * cx + at + 1, :] = row * (1.0 / 27.0)
    share[6 * cx + 6 :, :] = jnp.zeros_like(share[6 * cx + 6 :, :])


def fine_stress_kernel(step, s_ref, v_ref, m_ref, rim, xr, settings, slip, flags, *refs):
    last = step == 2
    copies = []
    nx, nz, ny = s_ref.shape[1], 32, s_ref.shape[3]
    own = nz - RIM
    if last:
        final, v_final, slip_out, out, sem = refs
        copies.append(pltpu.make_async_copy(v_ref.at[:, :, 0:own, :], v_final, sem.at[0]))
        copies[0].start()
    else:
        out, slip_out, xsend = refs
    v, s, m = reader(v_ref, rim, 0), reader(s_ref, rim, 3), reader(m_ref, rim, 9)
    has_x = has(flags, AFTER_X)
    half = ny // 2
    lane = iota((nz, 128), 1)
    shear_plane = jnp.zeros((nz, 128), F32)
    for x in range(nx):
        here = [v(c, x) for c in FINE_V]
        if x == nx - 1:
            after = [jnp.where(has_x, xr[k * nz : (k + 1) * nz, :], 0.0) for k in range(3)]
        else:
            after = [v(c, x + 1) for c in FINE_V]
        old = [s(c, x) for c in FINE_S]
        new = stress_plane(old, here, after, (0.0,) * 3, m(1, x), m(2, x), ring_fore)
        for k, c in enumerate(FINE_S):
            out[c, x] = new[k]
            if c == 3:
                moved = new[k][:, half:]
                moved = moved if x == 0 else pltpu.roll(moved, x, 1)
                shear_plane = jnp.where(lane == x, moved, shear_plane)
        if last:
            for first, end in ((0, 3), (4, 6)):
                at = len(copies)
                copies.append(
                    pltpu.make_async_copy(
                        out.at[first:end, x, 0:own, :], final.at[first:end, x], sem.at[at]
                    )
                )
                copies[at].start()
    old = slip[...]
    traction = shear_plane + settings[1]
    weakened = jnp.minimum(old * settings[6], 1.0)
    strength = settings[2] * (settings[4] - settings[5] * weakened)
    resisted = jnp.clip(traction, -strength, strength)
    active = settings[3]
    fresh = old + active * STEP_RATIO * jnp.abs(traction - resisted)
    fixed = shear_plane + active * (resisted - traction)
    for x in range(nx):
        moved = fixed if x == 0 else pltpu.roll(fixed, 128 - x, 1)
        out[3, x, :, half : half + 128] = jnp.where(lane == 0, moved, out[3, x, :, half : half + 128])
    if last:
        copies.append(pltpu.make_async_copy(out.at[3, :, 0:own, :], final.at[3], sem.at[len(copies)]))
        copies[-1].start()
        turned = jnp.concatenate([fresh, jnp.zeros((128 - nz, 128), F32)], axis=0).T
        slip_out[...] = turned[0:nx, 0:own]
        for copy in copies:
            copy.wait()
        return
    slip_out[...] = fresh
    for k, c in enumerate((0, 4, 3)):
        xsend[k * nz : (k + 1) * nz, :] = out[c, nx - 1]


def coarse_velocity_kernel(cv, cs, cm, xr, below, above, rows_ref, flags, out, xsend, next_rows, cs_near, cm_near):
    nx, ny, nz = cv.shape[1:]
    has_x, has_y = has(flags, BEFORE_X)[:, 0:128], has(flags, BEFORE_Z)[:, 0:128]
    more = has(flags, AFTER_Z)[:, 0:128]
    low, high = below.shape[0] - 24, above.shape[0] - 40
    cs_near[...] = cs[...]
    cm_near[...] = cm[...]
    xsend[...] = jnp.zeros_like(xsend)
    next_rows[3 * nx :, :] = jnp.zeros_like(next_rows[3 * nx :, :])

    def ahead(field, x):
        at = high + field * nx + x
        return jnp.where(more, above[at : at + 1, 0:128], 0.0)

    for x in range(nx):
        here = [cs[c, x] for c in COARSE_S]
        here_row = [ahead(3 + c, x) for c in COARSE_S]
        if x == 0:
            before, before_row = [], []
            for k in range(3):
                at = 96 + 8 * k
                plane = jnp.concatenate([xr[at : at + 8, 0:128], xr[at : at + 8, 128:256]], axis=0)
                before.append(jnp.where(has_x, plane, 0.0))
                before_row.append(jnp.where(has_x, xr[120 + k : 121 + k, 0:128], 0.0))
        else:
            before = [cs[c, x - 1] for c in (0, 3, 4)]
            before_row = [ahead(3 + c, x - 1) for c in (0, 3, 4)]
        rows = [jnp.where(has_y, below[low + k * nx + x : low + k * nx + x + 1, 0:128], 0.0) for k in range(3)]
        new = velocity_plane([cv[c, x] for c in COARSE_V], here, before, rows, cm[0, x])
        last = [here[k][ny - 1 : ny] for k in (3, 1, 5)]
        old_row = [ahead(c, x) for c in COARSE_V]
        new_row = velocity_plane(old_row, here_row, before_row, last, ahead(9, x), lambda a, edge: edge)
        for c in range(3):
            out[c, x] = new[c]
            next_rows[c * nx + x : c * nx + x + 1, :] = new_row[c]
            if x == 0:
                xsend[8 * c : 8 * c + 8, 0:128] = new[c][0:8]
                xsend[8 * c : 8 * c + 8, 128:256] = new[c][8:16]
    for f in range(2):
        xsend[24 + f : 25 + f, 0:128] = rows_ref[f, 0:1, :].astype(F32)


def coarse_stress_kernel(cv, cs, cm, xr, zr, rows_ref, rest, rest_next, rest_before, flags, _, v_out, s_out):
    nx, ny, nz = cv.shape[1:]
    base = xr.shape[0] - 32
    has_x, has_y = has(flags, AFTER_X)[:, 0:128], has(flags, AFTER_Z)[:, 0:128]
    row_ids = own_rows(flags, (ny, nz))

    before_x = has(flags, BEFORE_X)[:, 0:128]

    def inserted(plane, c, x):
        for f in range(2):
            if x < nx:
                hit = row_ids == rows_ref[f, x : x + 1, :].astype(F32)
            else:
                hit = row_ids == xr[base + 24 + f : base + 25 + f, 0:128]
            at = (f * 3 + c) * nx + x % nx
            more = 6 * nx + f * 3 + c
            if x == 0:
                from_before = jnp.where(before_x, rest_before[more : more + 1, :], 0.0)
                value = rest[at : at + 1, :] + from_before
            elif x < nx:
                value = rest[at : at + 1, :]
            else:
                value = rest_next[at : at + 1, :] + rest[more : more + 1, :]
            plane = jnp.where(hit, value, plane)
        return plane

    planes = [[inserted(cv[c, x], c, x) for c in range(3)] for x in range(nx)]
    edge = []
    for c in range(3):
        at = base + 8 * c
        plane = jnp.concatenate([xr[at : at + 8, 0:128], xr[at : at + 8, 128:256]], axis=0)
        edge.append(jnp.where(has_x, inserted(plane, c, nx), 0.0))
    planes.append(edge)
    for x in range(nx):
        for c in range(3):
            v_out[c, x] = planes[x][c]
        rows = [jnp.where(has_y, zr[k * nx + x : k * nx + x + 1, :], 0.0) for k in range(3)]
        new = stress_plane([cs[c, x] for c in COARSE_S], planes[x], planes[x + 1], rows, cm[1, x], cm[2, x])
        for c in range(6):
            s_out[c, x] = new[c]


def swap(value, axis, bit):
    count = lax.axis_size(axis)
    return lax.ppermute(value, axis, [(i, i ^ bit) for i in range(count)])


def spread(value, turns):
    for bits in turns:
        value = value + swap(value, "gy", bits)
    return value


def body(
    coarse_velocity,
    coarse_stress,
    coarse_material,
    fine_velocity,
    fine_stress,
    fine_material,
    fault_slip,
    initial_shear,
    normal_stress,
    fault_mask,
    zone_ids,
    static_friction,
    friction_drop,
    weakening_distance,
    owner_rows,
):
    nx, nz, ny = fine_velocity.shape[1:]
    cx, cy, cz = coarse_velocity.shape[1:]
    flags = make_flags(nz // 3, cy)
    shares = (6 * cx, cz)
    fault = (fault_slip, initial_shear, normal_stress, fault_mask, zone_ids)
    fields = (fine_velocity, fine_stress, fine_material)
    given = [
        pltpu.with_memory_space_constraint(a, pltpu.HBM)
        for a in fields + (coarse_stress, coarse_velocity, coarse_material) + fault + (owner_rows,)
    ]
    up, down, coupling, raw = pl.pallas_call(
        pack_kernel,
        out_shape=[
            jax.ShapeDtypeStruct(shape, F32)
            for shape in ((nx * 32 + 24, ny), (nx * 40 + 48, ny), shares, (nz, 128))
        ],
        in_specs=[HBM] * len(given) + [VMEM],
        out_specs=[VMEM] * 4,
        scratch_shapes=[pltpu.VMEM((a.shape[0], nx, 8, ny), F32) for a in fields * 2]
        + [pltpu.VMEM((3, cx, 8, cz), F32), pltpu.VMEM(coarse_velocity.shape, F32)]
        + [pltpu.VMEM((6, cx, 8, cz), F32), pltpu.VMEM((cx, 8, cz), F32)]
        + [pltpu.VMEM(owner_rows.shape, jnp.int32)]
        + [pltpu.VMEM(a.shape, a.dtype) for a in fault]
        + [pltpu.VMEM((128, 128), F32), pltpu.SemaphoreType.DMA((18,))],
        compiler_params=PARAMS,
    )(*given, flags)
    from_below, from_above = ring(up, "gy", 1), ring(down, "gy", -1)
    coupling = spread(coupling, (1, 2))
    parts_of = jnp.concatenate([static_friction, friction_drop, 1.0 / weakening_distance, jnp.zeros(4, F32)])
    parts_of = jnp.broadcast_to(parts_of[:, None], (16, 128))
    rim, xsend, settings, bounds = call(
        rim_kernel,
        [(12, nx, RIM, ny), (128, ny), (7, 32, 128), shares],
        [VMEM] * 9,
        from_below, from_above, fine_stress, coarse_stress, raw, parts_of, flags, coupling, swap(coupling, "gy", 6),
    )
    slip = settings[0]
    xr = ring(xsend, "gx", 1)
    bounds = (bounds, swap(bounds, "gy", 8))
    coarse_moved, cxs, coarse_zr, coarse_stress, coarse_material = call(
        coarse_velocity_kernel,
        [coarse_velocity.shape, (32, ny), (16, cz), coarse_stress.shape, coarse_material.shape],
        [VMEM] * 8,
        coarse_velocity, coarse_stress, coarse_material, xr, from_below, from_above, owner_rows, flags,
    )
    velocity, stress = fine_velocity, fine_stress

    def velocity_half(step, xr, *more):
        outs = [(3, nx, 32, ny), (96 + (16, 32, 0)[step], ny)]
        if step == 2:
            outs.append(more[0].shape)
        return call(
            lambda *refs: fine_velocity_kernel(step, *refs),
            outs, [VMEM] * (8 + len(more)),
            velocity, stress, fine_material, rim, xr, *bounds, flags, *more,
        )

    def stress_half(step, xr):
        return call(
            lambda *refs: fine_stress_kernel(step, *refs),
            [(6, nx, 32, ny), (32, 128), (96, ny)], [VMEM] * 8,
            stress, velocity, fine_material, rim, xr, settings, slip, flags,
        )

    velocity, xsend = velocity_half(0, xr)
    next_x = ring(xsend, "gx", -1)
    stress, slip, xsend = stress_half(0, next_x)
    velocity, xsend = velocity_half(1, ring(xsend, "gx", 1), cxs)
    coarse_xr = ring(xsend, "gx", -1)
    stress, slip, xsend = stress_half(1, coarse_xr)
    (share,) = call(share_kernel, [(32, cz)], [VMEM] * 7, velocity, stress, fine_material, next_x, *bounds, flags)
    share, xsend = lax.optimization_barrier((share, xsend))
    share = spread(share, (1,))
    velocity, xsend, share = velocity_half(2, ring(xsend, "gx", 1), share, swap(share, "gy", 2))
    restricted = spread(share, (6, 8))
    restricted_next, restricted_before = ring(restricted, "gx", -1), ring(restricted, "gx", 1)
    xr = ring(xsend, "gx", -1)
    stress, velocity, slip = pl.pallas_call(
        lambda *refs: fine_stress_kernel(2, *refs),
        out_shape=[jax.ShapeDtypeStruct(a.shape, F32) for a in (fine_stress, fine_velocity, fault_slip)],
        in_specs=[VMEM] * 8,
        out_specs=[pl.BlockSpec(memory_space=pl.ANY)] * 2 + [VMEM],
        scratch_shapes=[pltpu.VMEM((6, nx, 32, ny), F32), pltpu.SemaphoreType.DMA((2 * nx + 2,))],
        compiler_params=PARAMS,
    )(stress, velocity, fine_material, rim, xr, settings, slip, flags)
    coarse_next, coarse_stress_next = call(
        coarse_stress_kernel,
        [coarse_velocity.shape, coarse_stress.shape],
        [VMEM] * 11,
        coarse_moved, coarse_stress, coarse_material, coarse_xr, coarse_zr, owner_rows, restricted, restricted_next,
        restricted_before, flags, slip,
    )
    return (coarse_next, coarse_stress_next, velocity, stress, slip)


def solution(mesh):
    grid = P(None, "gx", "gy", None)
    plane = P("gx", "gy")
    return jax.shard_map(
        body,
        mesh=mesh,
        in_specs=(grid,) * 6 + (plane,) * 5 + (P(),) * 3 + (P(None, "gx", None),),
        out_specs=(grid,) * 4 + (plane,),
        check_vma=False,
    )
```

time: 99.1 us -> 79.8 us (0.81)
  the two profiles are of different devices: /device:TPU:31 before, /device:TPU:16 now
where the time goes in v2:
time: 79.8 us; the launch traced here: 79.6 us
  waiting for transfers between devices  40.1 us (50%)
  starting transfers between devices  26.1 us (33%)
  Pallas kernels  11.5 us (14%)
  local copies, waits for them, and re-layouts  0.97 us (1%)
    ppermute x8, waiting for transfers between devices, swap(): return lax.ppermute(value, axis, [(i, i ^ bit) for i in range(count)])  25.3 us
    ppermute x10, starting transfers between devices, ring(): lax.ppermute(value, axis, [(i, (i + steps) % count) for i in range(count)])  18.9 us
    ppermute x10, waiting for transfers between devices, ring(): lax.ppermute(value, axis, [(i, (i + steps) % count) for i in range(count)])  14.8 us
    ppermute x8, starting transfers between devices, swap(): return lax.ppermute(value, axis, [(i, i ^ bit) for i in range(count)])  7.22 us
    pallas_call x9, Pallas kernels, call(): pl.pallas_call(kernel, out_shape=tuple((jax.ShapeDtypeStruct(shape, F32)...  6.41 us
    pallas_call x1, Pallas kernels, body(): pl.pallas_call(lambda *refs: fine_stress_kernel(2, *refs), out_shape=[jax...  2.79 us
    pallas_call x1, Pallas kernels, body(): pl.pallas_call(pack_kernel, out_shape=[jax.ShapeDtypeStruct(shape, F32) f...  2.28 us
  transfers between devices with their start and end apart: 18, of which 14 were waited for; matrix products, arithmetic and copies ran while one was open for 0% of the time, Pallas kernels for 4%

profile of v2, /device:TPU:16, one launch (start us, length us, event | category | flops | bytes accessed | tf_op | source)
XLA Modules:
  0.0 79.6 jit_solution(10177687053217776444)
XLA Ops:
  0.8 2.3 %shard_map.182 = (f32[408,256]{1,0:T(8,128)S(1)}, f32[528,256]{1,0:T(8,128)S(1)}, f32[24,128]{1,0:T(8,128)S(1)}, f32[24,128]{1,0:T(8,128)S(1)}) custom-call(f32[3,12,24,256]{3,2,1,0:T(8,128)} %refs_0_.2, f32[6,12,24,256]{3,2,1,0:T(8,128)} %refs_0_.3, f32[3,12,24,256]{3,2,1,0:T(8,128)} %refs_2_.11, f32[6,4,16,128]{3,2,1,0:T(8,128)} %cs.5, ...), custom_call_target="tpu_custom_call" | custom-call | tf_op jit(solution)/shard_map/pallas_call | solution.py:559
  3.1 3.3 %collective-permute-start.1 = (f32[528,256]{1,0:T(8,128)S(1)}, f32[528,256]{1,0:T(8,128)S(1)}, u32[]{:S(2)}, u32[]{:S(2)}) collective-permute-start(f32[528,256]{1,0:T(8,128)S(1)} %get-tuple-element.39), channel_id=1, source_target_pairs={{0,15},{1,0},{2,1},{3,2},{4,3},{5,4},{6,5},{7,6},{8,7},{9,8},{10,9... | collective-permute-start | bytes 1622024 | tf_op jit(solution)/shard_map/ppermute | solution.py:32
  6.5 1.4 %collective-permute-done.2 = f32[24,128]{1,0:T(8,128)S(1)} collective-permute-done((f32[24,128]{1,0:T(8,128)S(1)}, f32[24,128]{1,0:T(8,128)S(1)}, u32[]{:S(2)}, u32[]{:S(2)}) %collective-permute-start.2) | collective-permute-done | bytes 12320 | tf_op jit(solution)/shard_map/ppermute | solution.py:523
  8.1 4.6 %collective-permute-done.3 = f32[24,128]{1,0:T(8,128)S(1)} collective-permute-done((f32[24,128]{1,0:T(8,128)S(1)}, f32[24,128]{1,0:T(8,128)S(1)}, u32[]{:S(2)}, u32[]{:S(2)}) %collective-permute-start.3) | collective-permute-done | bytes 12320 | tf_op jit(solution)/shard_map/ppermute | solution.py:523
  12.7 4.2 %collective-permute-start.4 = (f32[24,128]{1,0:T(8,128)S(1)}, f32[24,128]{1,0:T(8,128)S(1)}, u32[]{:S(2)}, u32[]{:S(2)}) collective-permute-start(f32[24,128]{1,0:T(8,128)S(1)} %add.16.left), channel_id=1, source_target_pairs={{0,6},{1,7},{2,4},{3,5},{4,2},{5,3},{6,0},{7,1},{8,14},{9,15},{10,... | collective-permute-start | bytes 36872 | tf_op jit(solution)/shard_map/ppermute | solution.py:523
  17.1 1.6 %collective-permute-done.4.right = f32[24,128]{1,0:T(8,128)S(1)} collective-permute-done((f32[24,128]{1,0:T(8,128)S(1)}, f32[24,128]{1,0:T(8,128)S(1)}, u32[]{:S(2)}, u32[]{:S(2)}) %collective-permute-start.4) | collective-permute-done | bytes 12320 | tf_op jit(solution)/shard_map/ppermute | solution.py:523
  19.0 1.4 %collective-permute-start.5 = (f32[128,256]{1,0:T(8,128)S(1)}, f32[128,256]{1,0:T(8,128)S(1)}, u32[]{:S(2)}, u32[]{:S(2)}) collective-permute-start(f32[128,256]{1,0:T(8,128)S(1)} %get-tuple-element.42), channel_id=1, source_target_pairs={{0,16},{16,32},{32,48},{48,64},{64,80},{80,96},{96,112},{112,0},{1... | collective-permute-start | bytes 393224 | tf_op jit(solution)/shard_map/ppermute | solution.py:32
  20.4 1.7 %collective-permute-start.6 = (f32[24,128]{1,0:T(8,128)S(1)}, f32[24,128]{1,0:T(8,128)S(1)}, u32[]{:S(2)}, u32[]{:S(2)}) collective-permute-start(f32[24,128]{1,0:T(8,128)S(1)} %get-tuple-element.47.refs_5_.bounds_a), channel_id=1, source_target_pairs={{0,8},{1,9},{2,10},{3,11},{4,12},{5,13},{6,14},{7,15},{8,0},{9,1},... | collective-permute-start | bytes 36872 | tf_op jit(solution)/shard_map/ppermute | solution.py:523
  22.1 3.7 %collective-permute-done.6.refs_6_.bounds_b = f32[24,128]{1,0:T(8,128)S(1)} collective-permute-done((f32[24,128]{1,0:T(8,128)S(1)}, f32[24,128]{1,0:T(8,128)S(1)}, u32[]{:S(2)}, u32[]{:S(2)}) %collective-permute-start.6) | collective-permute-done | bytes 12320 | tf_op jit(solution)/shard_map/ppermute | solution.py:523
  26.4 0.8 shard_map.185
  27.2 4.4 %collective-permute-start.7 = (f32[112,256]{1,0:T(8,128)S(1)}, f32[112,256]{1,0:T(8,128)S(1)}, u32[]{:S(2)}, u32[]{:S(2)}) collective-permute-start(f32[112,256]{1,0:T(8,128)S(1)} %get-tuple-element.49), channel_id=1, source_target_pairs={{0,112},{16,0},{32,16},{48,32},{64,48},{80,64},{96,80},{112,96},{1... | collective-permute-start | bytes 344072 | tf_op jit(solution)/shard_map/ppermute | solution.py:32
  31.6 2.4 %collective-permute-done.7.refs_4_.xr = f32[112,256]{1,0:T(8,128)S(1)} collective-permute-done((f32[112,256]{1,0:T(8,128)S(1)}, f32[112,256]{1,0:T(8,128)S(1)}, u32[]{:S(2)}, u32[]{:S(2)}) %collective-permute-start.7) | collective-permute-done | bytes 114720 | tf_op jit(solution)/shard_map/ppermute | solution.py:32
  34.0 1.1 %shard_map.186 = (f32[6,12,32,256]{3,2,1,0:T(8,128)S(1)}, f32[32,128]{1,0:T(8,128)S(1)}, f32[96,256]{1,0:T(8,128)S(1)}) custom-call(f32[6,12,24,256]{3,2,1,0:T(8,128)S(1)} %copy-done.1, f32[3,12,32,256]{3,2,1,0:T(8,128)S(1)} %get-tuple-element.48.refs_1_.refs_0_, f32[3,12,24,256]{3,2,1,0:T(8,128)S(1)} %copy-done, ...), custom_call_target="tpu_custom_call" | custom-call | tf_op jit(solution)/shard_map/pallas_call | solution.py:21
  35.1 2.5 %collective-permute-start.8 = (f32[96,256]{1,0:T(8,128)S(1)}, f32[96,256]{1,0:T(8,128)S(1)}, u32[]{:S(2)}, u32[]{:S(2)}) collective-permute-start(f32[96,256]{1,0:T(8,128)S(1)} %get-tuple-element.52), channel_id=1, source_target_pairs={{0,16},{16,32},{32,48},{48,64},{64,80},{80,96},{96,112},{112,0},{1... | collective-permute-start | bytes 294920 | tf_op jit(solution)/shard_map/ppermute | solution.py:32
  37.8 4.7 %collective-permute-done.8.refs_4_ = f32[96,256]{1,0:T(8,128)S(1)} collective-permute-done((f32[96,256]{1,0:T(8,128)S(1)}, f32[96,256]{1,0:T(8,128)S(1)}, u32[]{:S(2)}, u32[]{:S(2)}) %collective-permute-start.8) | collective-permute-done | bytes 98336 | tf_op jit(solution)/shard_map/ppermute | solution.py:32
  42.5 0.8 shard_map.187
  43.3 2.0 %collective-permute-start.9 = (f32[128,256]{1,0:T(8,128)S(1)}, f32[128,256]{1,0:T(8,128)S(1)}, u32[]{:S(2)}, u32[]{:S(2)}) collective-permute-start(f32[128,256]{1,0:T(8,128)S(1)} %get-tuple-element.54), channel_id=1, source_target_pairs={{0,112},{16,0},{32,16},{48,32},{64,48},{80,64},{96,80},{112,96},{1... | collective-permute-start | bytes 393224 | tf_op jit(solution)/shard_map/ppermute | solution.py:32
  45.3 3.1 %collective-permute-done.9.refs_4_.xr = f32[128,256]{1,0:T(8,128)S(1)} collective-permute-done((f32[128,256]{1,0:T(8,128)S(1)}, f32[128,256]{1,0:T(8,128)S(1)}, u32[]{:S(2)}, u32[]{:S(2)}) %collective-permute-start.9) | collective-permute-done | bytes 131104 | tf_op jit(solution)/shard_map/ppermute | solution.py:32
  48.3 1.2 %shard_map.188 = (f32[6,12,32,256]{3,2,1,0:T(8,128)S(1)}, f32[32,128]{1,0:T(8,128)S(1)}, f32[96,256]{1,0:T(8,128)S(1)}) custom-call(f32[6,12,32,256]{3,2,1,0:T(8,128)S(1)} %get-tuple-element.51.refs_1_.refs_0_, f32[3,12,32,256]{3,2,1,0:T(8,128)S(1)} %get-tuple-element.56.refs_1_.v.refs_0_, f32[3,12,24,256]{3,2,1,0:T(8,128)S(1)} %copy-done, ...), custom_call_target="tpu_custom_call" | custom-call | tf_op jit(solution)/shard_map/pallas_call | solution.py:21
  50.0 0.8 collective-permute-start.10
  50.8 1.2 %collective-permute-done.11 = f32[32,128]{1,0:T(8,128)S(1)} collective-permute-done((f32[32,128]{1,0:T(8,128)S(1)}, f32[32,128]{1,0:T(8,128)S(1)}, u32[]{:S(2)}, u32[]{:S(2)}) %collective-permute-start.11) | collective-permute-done | bytes 16416 | tf_op jit(solution)/shard_map/ppermute | solution.py:523
  52.0 3.7 %collective-permute-done.12.refs_9_ = f32[32,128]{1,0:T(8,128)S(1)} collective-permute-done((f32[32,128]{1,0:T(8,128)S(1)}, f32[32,128]{1,0:T(8,128)S(1)}, u32[]{:S(2)}, u32[]{:S(2)}) %collective-permute-start.12) | collective-permute-done | bytes 16416 | tf_op jit(solution)/shard_map/ppermute | solution.py:523
  55.8 1.1 %collective-permute-done.10.refs_4_ = f32[96,256]{1,0:T(8,128)S(1)} collective-permute-done((f32[96,256]{1,0:T(8,128)S(1)}, f32[96,256]{1,0:T(8,128)S(1)}, u32[]{:S(2)}, u32[]{:S(2)}) %collective-permute-start.10) | collective-permute-done | bytes 98336 | tf_op jit(solution)/shard_map/ppermute | solution.py:32
  56.8 0.8 shard_map.190
  57.6 2.5 %collective-permute-start.17 = (f32[96,256]{1,0:T(8,128)S(1)}, f32[96,256]{1,0:T(8,128)S(1)}, u32[]{:S(2)}, u32[]{:S(2)}) collective-permute-start(f32[96,256]{1,0:T(8,128)S(1)} %get-tuple-element.64), channel_id=1, source_target_pairs={{0,112},{16,0},{32,16},{48,32},{64,48},{80,64},{96,80},{112,96},{1... | collective-permute-start | bytes 294920 | tf_op jit(solution)/shard_map/ppermute | solution.py:32
  60.1 1.0 %collective-permute-start.13 = (f32[32,128]{1,0:T(8,128)S(1)}, f32[32,128]{1,0:T(8,128)S(1)}, u32[]{:S(2)}, u32[]{:S(2)}) collective-permute-start(f32[32,128]{1,0:T(8,128)S(1)} %get-tuple-element.62), channel_id=1, source_target_pairs={{0,6},{1,7},{2,4},{3,5},{4,2},{5,3},{6,0},{7,1},{8,14},{9,15},{10,... | collective-permute-start | bytes 49160 | tf_op jit(solution)/shard_map/ppermute | solution.py:523
  61.1 4.0 %collective-permute-done.13 = f32[32,128]{1,0:T(8,128)S(1)} collective-permute-done((f32[32,128]{1,0:T(8,128)S(1)}, f32[32,128]{1,0:T(8,128)S(1)}, u32[]{:S(2)}, u32[]{:S(2)}) %collective-permute-start.13) | collective-permute-done | bytes 16416 | tf_op jit(solution)/shard_map/ppermute | solution.py:523
  65.2 5.1 %collective-permute-done.14 = f32[32,128]{1,0:T(8,128)S(1)} collective-permute-done((f32[32,128]{1,0:T(8,128)S(1)}, f32[32,128]{1,0:T(8,128)S(1)}, u32[]{:S(2)}, u32[]{:S(2)}) %collective-permute-start.14) | collective-permute-done | bytes 16416 | tf_op jit(solution)/shard_map/ppermute | solution.py:523
  70.3 1.9 %collective-permute-start.15 = (f32[32,128]{1,0:T(8,128)S(1)}, f32[32,128]{1,0:T(8,128)S(1)}, u32[]{:S(2)}, u32[]{:S(2)}) collective-permute-start(f32[32,128]{1,0:T(8,128)S(1)} %add.19.rest), channel_id=1, source_target_pairs={{0,112},{16,0},{32,16},{48,32},{64,48},{80,64},{96,80},{112,96},{1... | collective-permute-start | bytes 49160 | tf_op jit(solution)/shard_map/ppermute | solution.py:32
  72.4 2.8 %shard_map.191 = (f32[6,12,24,256]{3,2,1,0:T(8,128)}, f32[3,12,24,256]{3,2,1,0:T(8,128)}, f32[12,24]{1,0:T(8,128)}) custom-call(f32[6,12,32,256]{3,2,1,0:T(8,128)S(1)} %get-tuple-element.58.s.refs_1_.refs_0_, f32[3,12,32,256]{3,2,1,0:T(8,128)S(1)} %get-tuple-element.63.refs_1_, f32[3,12,24,256]{3,2,1,0:T(8,128)S(1)} %copy-done, ...), custom_call_target="tpu_custom_call" | custom-call | tf_op jit(solution)/shard_map/pallas_call | solution.py:626
  75.2 2.9 %collective-permute-done.16.rest_before = f32[32,128]{1,0:T(8,128)S(1)} collective-permute-done((f32[32,128]{1,0:T(8,128)S(1)}, f32[32,128]{1,0:T(8,128)S(1)}, u32[]{:S(2)}, u32[]{:S(2)}) %collective-permute-start.16) | collective-permute-done | bytes 16416 | tf_op jit(solution)/shard_map/ppermute | solution.py:32
  78.8 0.8 shard_map.192
  (49 shorter events, 3.1 us)
Async XLA Ops:
  0.8 7.3 %copy-start.10 = (f32[4]{0:T(128)S(1)}, f32[4]{0:T(128)}, u32[]{:S(2)}) copy-start(f32[4]{0:T(128)} %param.28) | copy-start | bytes 52
  0.8 16.2 %copy-start.8 = (f32[4]{0:T(128)S(1)}, f32[4]{0:T(128)}, u32[]{:S(2)}) copy-start(f32[4]{0:T(128)} %param.27) | copy-start | bytes 52
  0.8 16.2 %copy-start.9 = (f32[4]{0:T(128)S(1)}, f32[4]{0:T(128)}, u32[]{:S(2)}) copy-start(f32[4]{0:T(128)} %param.26) | copy-start | bytes 52
  0.8 17.9 %copy-start.1 = (f32[6,12,24,256]{3,2,1,0:T(8,128)S(1)}, f32[6,12,24,256]{3,2,1,0:T(8,128)}, u32[]{:S(2)}) copy-start(f32[6,12,24,256]{3,2,1,0:T(8,128)} %refs_0_.3) | copy-start | bytes 5308420
  0.8 17.9 %copy-start.3 = (f32[6,4,16,128]{3,2,1,0:T(8,128)S(1)}, f32[6,4,16,128]{3,2,1,0:T(8,128)}, u32[]{:S(2)}) copy-start(f32[6,4,16,128]{3,2,1,0:T(8,128)} %cs.5) | copy-start | bytes 589828
  3.1 23.3 %copy-start = (f32[3,12,24,256]{3,2,1,0:T(8,128)S(1)}, f32[3,12,24,256]{3,2,1,0:T(8,128)}, u32[]{:S(2)}) copy-start(f32[3,12,24,256]{3,2,1,0:T(8,128)} %refs_2_.11) | copy-start | bytes 2654212
  3.1 23.3 %copy-start.2 = (f32[3,12,24,256]{3,2,1,0:T(8,128)S(1)}, f32[3,12,24,256]{3,2,1,0:T(8,128)}, u32[]{:S(2)}) copy-start(f32[3,12,24,256]{3,2,1,0:T(8,128)} %refs_0_.2) | copy-start | bytes 2654212
  3.1 15.5 %collective-permute-start.1 = (f32[528,256]{1,0:T(8,128)S(1)}, f32[528,256]{1,0:T(8,128)S(1)}, u32[]{:S(2)}, u32[]{:S(2)}) collective-permute-start(f32[528,256]{1,0:T(8,128)S(1)} %get-tuple-element.39), channel_id=1, source_target_pairs={{0,15},{1,0},{2,1},{3,2},{4,3},{5,4},{6,5},{7,6},{8,7},{9,8},{10,9... | collective-permute-start | bytes 1622024 | tf_op jit(solution)/shard_map/ppermute | solution.py:32
  6.5 12.2 %collective-permute-start = (f32[408,256]{1,0:T(8,128)S(1)}, f32[408,256]{1,0:T(8,128)S(1)}, u32[]{:S(2)}, u32[]{:S(2)}) collective-permute-start(f32[408,256]{1,0:T(8,128)S(1)} %get-tuple-element.38), channel_id=1, source_target_pairs={{0,1},{1,2},{2,3},{3,4},{4,5},{5,6},{6,7},{7,8},{8,9},{9,10},{10,1... | collective-permute-start | bytes 1253384 | tf_op jit(solution)/shard_map/ppermute | solution.py:32
  6.5 1.4 %collective-permute-start.2 = (f32[24,128]{1,0:T(8,128)S(1)}, f32[24,128]{1,0:T(8,128)S(1)}, u32[]{:S(2)}, u32[]{:S(2)}) collective-permute-start(f32[24,128]{1,0:T(8,128)S(1)} %get-tuple-element.41), channel_id=1, source_target_pairs={{0,1},{1,0},{2,3},{3,2},{4,5},{5,4},{6,7},{7,6},{8,9},{9,8},{10,11... | collective-permute-start | bytes 36872 | tf_op jit(solution)/shard_map/ppermute | solution.py:523
  7.9 4.9 %collective-permute-start.3 = (f32[24,128]{1,0:T(8,128)S(1)}, f32[24,128]{1,0:T(8,128)S(1)}, u32[]{:S(2)}, u32[]{:S(2)}) collective-permute-start(f32[24,128]{1,0:T(8,128)S(1)} %add.15), channel_id=1, source_target_pairs={{0,2},{1,3},{2,0},{3,1},{4,6},{5,7},{6,4},{7,5},{8,10},{9,11},{10,... | collective-permute-start | bytes 36872 | tf_op jit(solution)/shard_map/ppermute | solution.py:523
  12.7 5.9 %collective-permute-start.4 = (f32[24,128]{1,0:T(8,128)S(1)}, f32[24,128]{1,0:T(8,128)S(1)}, u32[]{:S(2)}, u32[]{:S(2)}) collective-permute-start(f32[24,128]{1,0:T(8,128)S(1)} %add.16.left), channel_id=1, source_target_pairs={{0,6},{1,7},{2,4},{3,5},{4,2},{5,3},{6,0},{7,1},{8,14},{9,15},{10,... | collective-permute-start | bytes 36872 | tf_op jit(solution)/shard_map/ppermute | solution.py:523
  19.0 7.4 %collective-permute-start.5 = (f32[128,256]{1,0:T(8,128)S(1)}, f32[128,256]{1,0:T(8,128)S(1)}, u32[]{:S(2)}, u32[]{:S(2)}) collective-permute-start(f32[128,256]{1,0:T(8,128)S(1)} %get-tuple-element.42), channel_id=1, source_target_pairs={{0,16},{16,32},{32,48},{48,64},{64,80},{80,96},{96,112},{112,0},{1... | collective-permute-start | bytes 393224 | tf_op jit(solution)/shard_map/ppermute | solution.py:32
  20.4 5.3 %collective-permute-start.6 = (f32[24,128]{1,0:T(8,128)S(1)}, f32[24,128]{1,0:T(8,128)S(1)}, u32[]{:S(2)}, u32[]{:S(2)}) collective-permute-start(f32[24,128]{1,0:T(8,128)S(1)} %get-tuple-element.47.refs_5_.bounds_a), channel_id=1, source_target_pairs={{0,8},{1,9},{2,10},{3,11},{4,12},{5,13},{6,14},{7,15},{8,0},{9,1},... | collective-permute-start | bytes 36872 | tf_op jit(solution)/shard_map/ppermute | solution.py:523
  27.2 6.7 %collective-permute-start.7 = (f32[112,256]{1,0:T(8,128)S(1)}, f32[112,256]{1,0:T(8,128)S(1)}, u32[]{:S(2)}, u32[]{:S(2)}) collective-permute-start(f32[112,256]{1,0:T(8,128)S(1)} %get-tuple-element.49), channel_id=1, source_target_pairs={{0,112},{16,0},{32,16},{48,32},{64,48},{80,64},{96,80},{112,96},{1... | collective-permute-start | bytes 344072 | tf_op jit(solution)/shard_map/ppermute | solution.py:32
  33.9 3.7 %copy-start.4 = (f32[3,4,16,128]{3,2,1,0:T(8,128)S(1)}, f32[3,4,16,128]{3,2,1,0:T(8,128)}, u32[]{:S(2)}) copy-start(f32[3,4,16,128]{3,2,1,0:T(8,128)} %cv.3) | copy-start | bytes 294916
  33.9 3.7 %copy-start.5 = (f32[3,4,16,128]{3,2,1,0:T(8,128)S(1)}, f32[3,4,16,128]{3,2,1,0:T(8,128)}, u32[]{:S(2)}) copy-start(f32[3,4,16,128]{3,2,1,0:T(8,128)} %cm.3) | copy-start | bytes 294916
  33.9 3.7 %copy-start.6 = (s32[2,4,128]{2,1,0:T(4,128)S(1)}, s32[2,4,128]{2,1,0:T(4,128)}, u32[]{:S(2)}) copy-start(s32[2,4,128]{2,1,0:T(4,128)} %rows_ref.3) | copy-start | bytes 12292
  35.1 7.4 %collective-permute-start.8 = (f32[96,256]{1,0:T(8,128)S(1)}, f32[96,256]{1,0:T(8,128)S(1)}, u32[]{:S(2)}, u32[]{:S(2)}) collective-permute-start(f32[96,256]{1,0:T(8,128)S(1)} %get-tuple-element.52), channel_id=1, source_target_pairs={{0,16},{16,32},{32,48},{48,64},{64,80},{80,96},{96,112},{112,0},{1... | collective-permute-start | bytes 294920 | tf_op jit(solution)/shard_map/ppermute | solution.py:32
  43.3 5.0 %collective-permute-start.9 = (f32[128,256]{1,0:T(8,128)S(1)}, f32[128,256]{1,0:T(8,128)S(1)}, u32[]{:S(2)}, u32[]{:S(2)}) collective-permute-start(f32[128,256]{1,0:T(8,128)S(1)} %get-tuple-element.54), channel_id=1, source_target_pairs={{0,112},{16,0},{32,16},{48,32},{64,48},{80,64},{96,80},{112,96},{1... | collective-permute-start | bytes 393224 | tf_op jit(solution)/shard_map/ppermute | solution.py:32
  50.0 6.8 %collective-permute-start.10 = (f32[96,256]{1,0:T(8,128)S(1)}, f32[96,256]{1,0:T(8,128)S(1)}, u32[]{:S(2)}, u32[]{:S(2)}) collective-permute-start(f32[96,256]{1,0:T(8,128)S(1)} %get-tuple-element.60), channel_id=1, source_target_pairs={{0,16},{16,32},{32,48},{48,64},{64,80},{80,96},{96,112},{112,0},{1... | collective-permute-start | bytes 294920 | tf_op jit(solution)/shard_map/ppermute | solution.py:32
  50.8 1.2 %collective-permute-start.11 = (f32[32,128]{1,0:T(8,128)S(1)}, f32[32,128]{1,0:T(8,128)S(1)}, u32[]{:S(2)}, u32[]{:S(2)}) collective-permute-start(f32[32,128]{1,0:T(8,128)S(1)} %shard_map.189), channel_id=1, source_target_pairs={{0,1},{1,0},{2,3},{3,2},{4,5},{5,4},{6,7},{7,6},{8,9},{9,8},{10,11... | collective-permute-start | bytes 49160 | tf_op jit(solution)/shard_map/ppermute | solution.py:523
  52.0 3.7 %collective-permute-start.12 = (f32[32,128]{1,0:T(8,128)S(1)}, f32[32,128]{1,0:T(8,128)S(1)}, u32[]{:S(2)}, u32[]{:S(2)}) collective-permute-start(f32[32,128]{1,0:T(8,128)S(1)} %add.17.refs_8_), channel_id=1, source_target_pairs={{0,2},{1,3},{2,0},{3,1},{4,6},{5,7},{6,4},{7,5},{8,10},{9,11},{10,... | collective-permute-start | bytes 49160 | tf_op jit(solution)/shard_map/ppermute | solution.py:523
  57.6 14.7 %collective-permute-start.17 = (f32[96,256]{1,0:T(8,128)S(1)}, f32[96,256]{1,0:T(8,128)S(1)}, u32[]{:S(2)}, u32[]{:S(2)}) collective-permute-start(f32[96,256]{1,0:T(8,128)S(1)} %get-tuple-element.64), channel_id=1, source_target_pairs={{0,112},{16,0},{32,16},{48,32},{64,48},{80,64},{96,80},{112,96},{1... | collective-permute-start | bytes 294920 | tf_op jit(solution)/shard_map/ppermute | solution.py:32
  60.1 4.9 %collective-permute-start.13 = (f32[32,128]{1,0:T(8,128)S(1)}, f32[32,128]{1,0:T(8,128)S(1)}, u32[]{:S(2)}, u32[]{:S(2)}) collective-permute-start(f32[32,128]{1,0:T(8,128)S(1)} %get-tuple-element.62), channel_id=1, source_target_pairs={{0,6},{1,7},{2,4},{3,5},{4,2},{5,3},{6,0},{7,1},{8,14},{9,15},{10,... | collective-permute-start | bytes 49160 | tf_op jit(solution)/shard_map/ppermute | solution.py:523
  65.1 5.2 %collective-permute-start.14 = (f32[32,128]{1,0:T(8,128)S(1)}, f32[32,128]{1,0:T(8,128)S(1)}, u32[]{:S(2)}, u32[]{:S(2)}) collective-permute-start(f32[32,128]{1,0:T(8,128)S(1)} %add.18), channel_id=1, source_target_pairs={{0,8},{1,9},{2,10},{3,11},{4,12},{5,13},{6,14},{7,15},{8,0},{9,1},... | collective-permute-start | bytes 49160 | tf_op jit(solution)/shard_map/ppermute | solution.py:523
  70.3 4.8 %collective-permute-start.15 = (f32[32,128]{1,0:T(8,128)S(1)}, f32[32,128]{1,0:T(8,128)S(1)}, u32[]{:S(2)}, u32[]{:S(2)}) collective-permute-start(f32[32,128]{1,0:T(8,128)S(1)} %add.19.rest), channel_id=1, source_target_pairs={{0,112},{16,0},{32,16},{48,32},{64,48},{80,64},{96,80},{112,96},{1... | collective-permute-start | bytes 49160 | tf_op jit(solution)/shard_map/ppermute | solution.py:32
  72.3 5.8 %collective-permute-start.16 = (f32[32,128]{1,0:T(8,128)S(1)}, f32[32,128]{1,0:T(8,128)S(1)}, u32[]{:S(2)}, u32[]{:S(2)}) collective-permute-start(f32[32,128]{1,0:T(8,128)S(1)} %add.19.rest), channel_id=1, source_target_pairs={{0,16},{16,32},{32,48},{48,64},{64,80},{80,96},{96,112},{112,0},{1... | collective-permute-start | bytes 49160 | tf_op jit(solution)/shard_map/ppermute | solution.py:32
  78.1 0.7 copy-start.7

commit v3 on v2

--- a/solution.py
+++ b/solution.py
@@ -14,7 +14,7 @@
 VMEM = pl.BlockSpec(memory_space=pltpu.VMEM)
 SMEM = pl.BlockSpec(memory_space=pltpu.SMEM)
 HBM = pl.BlockSpec(memory_space=pltpu.HBM)
-PARAMS = pltpu.CompilerParams(vmem_limit_bytes=32 * 1024 * 1024)
+PARAMS = pltpu.CompilerParams(vmem_limit_bytes=8 * 1024 * 1024)
 
 
 def call(kernel, outs, specs, *args):
@@ -125,16 +125,35 @@
     return refs[2], field - 9
 
 
+def coupling_kernel(cv, rows_hbm, flags, _, coupling, cv_buf, rows_ref, sem):
+    cx, cy, cz = cv.shape[1:]
+    moves = ((cv, cv_buf), (rows_hbm, rows_ref))
+    copies = [pltpu.make_async_copy(src, dst, sem.at[i]) for i, (src, dst) in enumerate(moves)]
+    for copy in copies:
+        copy.start()
+    for copy in copies:
+        copy.wait()
+    ids = own_rows(flags, (cy, cz))
+    for f in range(2):
+        for x in range(cx):
+            here = ids == rows_ref[f, x : x + 1, :].astype(F32)
+            for c in range(3):
+                row = jnp.sum(jnp.where(here, cv_buf[c, x], 0.0), axis=0, keepdims=True)
+                at = (f * 3 + c) * cx + x
+                coupling[at : at + 1, :] = row
+
+
 def pack_kernel(
-    fv, fs, fm, cs, cv, cm, slip, shear, normal, mask, zone, rows_hbm, flags,
-    up, down, coupling, raw,
-    top_v, top_s, top_m, low_v, low_s, low_m, cz_buf, cv_buf, cs_low, cm_low, rows_ref, slip_buf, shear_buf, normal_buf, mask_buf, zone_buf, turn, sem,
+    fv, fs, fm, cs, cv, cm, slip, shear, normal, mask, zone, static, drop, distance, _,
+    up, down, raw,
+    top_v, top_s, top_m, low_v, low_s, low_m, cz_buf, cv_low, cs_low, cm_low, static_buf, drop_buf, distance_buf, slip_buf, shear_buf, normal_buf, mask_buf, zone_buf, turn, sem,
 ):
     nx, nz, ny = fv.shape[1:]
     cx, cy, cz = cs.shape[1:]
     fault = (slip_buf, shear_buf, normal_buf, mask_buf, zone_buf)
-    moves = [(cv, cv_buf), (rows_hbm, rows_ref)]
-    moves += list(zip((slip, shear, normal, mask, zone), fault))
+    zoned = (static_buf, drop_buf, distance_buf)
+    moves = list(zip((slip, shear, normal, mask, zone, static, drop, distance), fault + zoned))
+    moves.append((cv.at[:, :, 0:8, :], cv_low))
     for k, c in enumerate((3, 1, 5)):
         moves.append((cs.at[c, :, cy - 8 : cy, :], cz_buf.at[k]))
     moves.append((cs.at[:, :, 0:8, :], cs_low))
@@ -148,17 +167,20 @@
         copy.start()
     for copy in copies[:early]:
         copy.wait()
-    for f in range(2):
-        for x in range(cx):
-            here = own_rows(flags, (cy, cz)) == rows_ref[f, x : x + 1, :].astype(F32)
-            for c in range(3):
-                row = jnp.sum(jnp.where(here, cv_buf[c, x], 0.0), axis=0, keepdims=True)
-                at = (f * 3 + c) * cx + x
-                coupling[at : at + 1, :] = row
     turn[...] = jnp.zeros_like(turn)
     for k, ref in enumerate(fault):
         turn[16 * k : 16 * k + nx, 0:nz] = ref[...].astype(F32)
     turned = turn[...].T[0:nz]
+    zones = pltpu.roll(turned, 128 - 64, 1)
+    group = iota(turned.shape, 1) // 16
+    for k in range(3):
+        value = jnp.zeros_like(turned)
+        for zone_id in range(4):
+            part = zoned[k][zone_id]
+            if k == 2:
+                part = 1.0 / jnp.full(turned.shape, part)
+            value = jnp.where(zones == float(zone_id), part, value)
+        turned = jnp.where(group == 5 + k, pltpu.roll(value, 16 * (5 + k), 1), turned)
     raw[...] = turned
     at = nx * 32
     up[at:, :] = jnp.zeros((24, ny), F32)
@@ -171,7 +193,7 @@
     for c in range(10):
         for x in range(cx):
             if c < 3:
-                row = cv_buf[c, x, 0:1]
+                row = cv_low[c, x, 0:1]
             elif c < 9:
                 row = cs_low[c - 3, x, 0:1]
             else:
@@ -210,8 +232,18 @@
     lax.fori_loop(0, nx, step, 0)
 
 
-def rim_kernel(from_below, from_above, fs, cs, raw, parts_of, flags, left, right, rim, xsend, settings, total):
-    total[...] = left[...] + right[...]
+def add_up(parts):
+    total = parts[0][...]
+    for part in parts[1:]:
+        total = total + part[...]
+    return total
+
+
+def fault_settings(turned):
+    return [turned] + [pltpu.roll(turned, 128 - 16 * k, 1) for k in (1, 2, 3, 5, 6, 7)]
+
+
+def rim_kernel(from_below, from_above, fs, fm, cs, raw, flags, rim, xsend, settings):
     nx, nz, ny = fs.shape[1:]
     cx = cs.shape[1]
     has_below, has_above = has(flags, BEFORE_Z), has(flags, AFTER_Z)
@@ -247,22 +279,21 @@
     for k, c in enumerate((0, 3, 4)):
         xsend[96 + 8 * k : 104 + 8 * k, 0:128] = cs[c, cx - 1, 0:8]
         xsend[96 + 8 * k : 104 + 8 * k, 128:256] = cs[c, cx - 1, 8:16]
-    xsend[120:, :] = jnp.zeros((8, ny), F32)
+    xsend[120:128, :] = jnp.zeros((8, ny), F32)
     for k, c in enumerate((0, 3, 4)):
         at = nx * 40 + 8 + (3 + c) * cx + cx - 1
         xsend[120 + k : 121 + k, 0:128] = jnp.where(has_above[:, 0:128], from_above[at : at + 1, 0:128], 0.0)
     below = jnp.where(has_below[:, 0:128], from_below[nx * 32 + 16 :, 0:128], 0.0)
     above = jnp.where(has_above[:, 0:128], from_above[nx * 40 : nx * 40 + 8, 0:128], 0.0)
     turned = jnp.concatenate([raw[...], jnp.where(iota((RIM, 128), 0) < 4, above, below)], axis=0)
-    settings[0] = turned
-    for k in (1, 2, 3):
-        settings[k] = pltpu.roll(turned, 128 - 16 * k, 1)
-    zones = pltpu.roll(turned, 128 - 64, 1)
-    for k in range(3):
-        value = jnp.zeros_like(turned)
-        for zone in range(4):
-            value = jnp.where(zones == float(zone), parts_of[4 * k + zone : 4 * k + zone + 1, :], value)
-        settings[4 + k] = value
+    for k in (1, 2):
+        at = 96 + 32 * k
+        xsend[at : at + nz, :] = fm[k, nx - 1]
+        xsend[at + nz : at + 32, :] = rim[9 + k, nx - 1]
+    xsend[192:208, 0:128] = turned[0:16]
+    xsend[192:208, 128:256] = turned[16:32]
+    for k, part in enumerate(fault_settings(turned)):
+        settings[k] = part
 
 
 def ring_back(a, _):
@@ -294,44 +325,50 @@
     return jnp.where(iota((a.shape[0], 128), 1) < 64, a[:, 0:128], a[:, a.shape[1] - 128 :])
 
 
-def fine_velocity_kernel(step, v_ref, s_ref, m_ref, rim, xr, bounds_a, bounds_b, flags, *refs):
-    refs = list(refs)
-    if step == 1:
-        cxs = refs.pop(0)
-    if step == 2:
-        left, right = refs.pop(0), refs.pop(0)
-        refs.pop()[...] = left[...] + right[...]
-    out, xsend = refs
+def velocity_planes(planes, v_ref, s_ref, m_ref, rim, behind, bounds_a, bounds_b, flags, put):
     bounds = bounds_a[...] + bounds_b[...]
     v, s, m = reader(v_ref, rim, 0), reader(s_ref, rim, 3), reader(m_ref, rim, 9)
-    nx, nz, ny = v_ref.shape[1], 32, v_ref.shape[3]
+    nz = 32
     cells = own_cells(flags, nz)
     has_x = has(flags, BEFORE_X)
-    for x in range(nx):
+    columns = {}
+    for x in planes:
         here = [s(c, x) for c in FINE_S]
-        if x % 3 == 0:
-            columns = [[held_column(bounds, cells, f, c, x // 3) for f in range(2)] for c in range(3)]
+        if x // 3 not in columns:
+            columns[x // 3] = [[held_column(bounds, cells, f, c, x // 3) for f in range(2)] for c in range(3)]
         if x == 0:
-            before = [jnp.where(has_x, xr[k * nz : (k + 1) * nz, :], 0.0) for k in range(3)]
+            before = [jnp.where(has_x, behind[k * nz : (k + 1) * nz, :], 0.0) for k in range(3)]
         else:
             before = [s(c, x - 1) for c in (0, 4, 3)]
         old = [v(c, x) for c in FINE_V]
-        buoyancy = m(0, x)
-        new = velocity_plane(old, here, before, (0.0,) * 3, buoyancy, ring_back)
+        new = velocity_plane(old, here, before, (0.0,) * 3, m(0, x), ring_back)
+        put(x, [held(new[k], columns[x // 3][c]) for k, c in enumerate(FINE_V)])
+
+
+def velocity_edge_kernel(step, v, s, m, rim, behind, bounds_a, bounds_b, flags, *refs):
+    refs = list(refs)
+    more = [refs.pop(0)] if step == 1 else []
+    nz = 32 if step < 2 else 24
+
+    def put(x, new):
+        for k in range(3):
+            refs[0 if x == 0 else 1][k * nz : (k + 1) * nz, :] = new[k][0:nz]
+
+    planes = [0] if step == 2 else [0, v.shape[1] - 1]
+    velocity_planes(planes, v, s, m, rim, behind, bounds_a, bounds_b, flags, put)
+    if step == 1:
+        refs[0][3 * nz :, :] = more[0][...]
+
+
+def fine_velocity_kernel(v, s, m, rim, behind, bounds_a, bounds_b, flags, out):
+    def put(x, new):
         for k, c in enumerate(FINE_V):
-            val = held(new[k], columns[c])
-            out[c, x] = val
-            if x == 0:
-                xsend[k * nz : (k + 1) * nz, :] = val
-        if step == 0 and x == 0:
-            xsend[3 * nz :, :] = jnp.zeros_like(xsend[3 * nz :, :])
-            xsend[3 * nz :, 0:128] = merged(buoyancy)[0:16]
-            xsend[3 * nz : 3 * nz + 8, 128:256] = merged(buoyancy)[16:24]
-    if step == 1:
-        xsend[3 * nz :, :] = cxs[...]
-
-
-def share_kernel(v, s, m, xr, bounds_a, bounds_b, flags, share):
+            out[c, x] = new[k]
+
+    velocity_planes(range(v.shape[1]), v, s, m, rim, behind, bounds_a, bounds_b, flags, put)
+
+
+def share_kernel(v, s, m, behind, bounds_a, bounds_b, flags, share):
     nx, nz, ny = v.shape[1:]
     cx, own = nx // 3, nz - RIM
     bounds = bounds_a[...] + bounds_b[...]
@@ -343,7 +380,7 @@
 
     columns = [[[held_column(bounds, cells, f, c, x) for f in range(2)] for c in range(3)] for x in range(cx)]
     sums = {}
-    before = [jnp.zeros((own, 128), F32)] * 3
+    before = [merged(behind[k * nz : k * nz + own, :]) for k in range(3)]
     for x in range(nx):
         here = [merged(s[c, x]) for c in FINE_S]
         old = [merged(v[c, x, 0:own, :]) for c in FINE_V]
@@ -354,73 +391,112 @@
         for k, c in enumerate(FINE_V):
             val = held(new[k], columns[x // 3][c])
             sums[c, x // 3] = val if x % 3 == 0 else sums[c, x // 3] + val
-    buoyancy = jnp.concatenate([xr[96:112, 0:128], xr[96:104, 128:256]], axis=0)
-    ahead = [-STEP_RATIO * buoyancy * plane for plane in before]
     for f in range(2):
         face = lane < 3 if f == 0 else lane >= 125
-        free = (lane == 1) | (lane == 2) if f == 0 else (lane == 125) | (lane == 126)
-        for k, c in enumerate(FINE_V):
-            at = f * 3 + c
+        for c in range(3):
             for x in range(cx):
+                at = (f * 3 + c) * cx + x
                 total = jnp.sum(jnp.where(face, sums[c, x], 0.0), axis=1, keepdims=True)
                 row = jnp.sum(jnp.where(cells, total, 0.0), axis=0, keepdims=True)
-                share[at * cx + x : at * cx + x + 1, :] = row * (1.0 / 27.0)
-            total = jnp.sum(jnp.where(free, ahead[k], 0.0), axis=1, keepdims=True)
-            row = jnp.sum(jnp.where(cells, total, 0.0), axis=0, keepdims=True)
-            share[6 * cx + at : 6 * cx + at + 1, :] = row * (1.0 / 27.0)
-    share[6 * cx + 6 :, :] = jnp.zeros_like(share[6 * cx + 6 :, :])
-
-
-def fine_stress_kernel(step, s_ref, v_ref, m_ref, rim, xr, settings, slip, flags, *refs):
-    last = step == 2
-    copies = []
-    nx, nz, ny = s_ref.shape[1], 32, s_ref.shape[3]
-    own = nz - RIM
-    if last:
-        final, v_final, slip_out, out, sem = refs
-        copies.append(pltpu.make_async_copy(v_ref.at[:, :, 0:own, :], v_final, sem.at[0]))
-        copies[0].start()
-    else:
-        out, slip_out, xsend = refs
+                share[at : at + 1, :] = row * (1.0 / 27.0)
+
+
+def stress_planes(planes, s_ref, v_ref, m_ref, rim, xr, flags, put):
     v, s, m = reader(v_ref, rim, 0), reader(s_ref, rim, 3), reader(m_ref, rim, 9)
+    nx, nz, half = s_ref.shape[1], 32, s_ref.shape[3] // 2
     has_x = has(flags, AFTER_X)
-    half = ny // 2
     lane = iota((nz, 128), 1)
     shear_plane = jnp.zeros((nz, 128), F32)
-    for x in range(nx):
+    for x in planes:
         here = [v(c, x) for c in FINE_V]
         if x == nx - 1:
-            after = [jnp.where(has_x, xr[k * nz : (k + 1) * nz, :], 0.0) for k in range(3)]
+            rows = nz if xr.shape[0] >= 3 * nz else nz - RIM
+            after = [jnp.where(has_x, xr[k * rows : (k + 1) * rows, :], 0.0) for k in range(3)]
+            if rows < nz:
+                rest = jnp.zeros((nz - rows, xr.shape[1]), F32)
+                after = [jnp.concatenate([plane, rest], axis=0) for plane in after]
         else:
             after = [v(c, x + 1) for c in FINE_V]
         old = [s(c, x) for c in FINE_S]
         new = stress_plane(old, here, after, (0.0,) * 3, m(1, x), m(2, x), ring_fore)
-        for k, c in enumerate(FINE_S):
-            out[c, x] = new[k]
-            if c == 3:
-                moved = new[k][:, half:]
-                moved = moved if x == 0 else pltpu.roll(moved, x, 1)
-                shear_plane = jnp.where(lane == x, moved, shear_plane)
-        if last:
-            for first, end in ((0, 3), (4, 6)):
-                at = len(copies)
-                copies.append(
-                    pltpu.make_async_copy(
-                        out.at[first:end, x, 0:own, :], final.at[first:end, x], sem.at[at]
-                    )
-                )
-                copies[at].start()
-    old = slip[...]
+        put(x, new)
+        moved = new[4][:, half : half + 128]
+        moved = moved if x == 0 else pltpu.roll(moved, x, 1)
+        shear_plane = jnp.where(lane == x, moved, shear_plane)
+    return shear_plane
+
+
+def friction(shear_plane, settings, old):
     traction = shear_plane + settings[1]
     weakened = jnp.minimum(old * settings[6], 1.0)
     strength = settings[2] * (settings[4] - settings[5] * weakened)
     resisted = jnp.clip(traction, -strength, strength)
     active = settings[3]
     fresh = old + active * STEP_RATIO * jnp.abs(traction - resisted)
-    fixed = shear_plane + active * (resisted - traction)
+    return fresh, shear_plane + active * (resisted - traction)
+
+
+def with_fault(upper, fixed, x):
+    moved = fixed if x == 0 else pltpu.roll(fixed, 128 - x, 1)
+    return jnp.where(iota(upper.shape, 1) == 0, moved, upper)
+
+
+def stress_behind(old, v_behind, v_first, given, slip, flags, out, slip_out):
+    nz, half = 32, v_behind.shape[1] // 2
+    has_x = has(flags, BEFORE_X)
+    here = [v_behind[k * nz : (k + 1) * nz, :] for k in range(3)]
+    xx, xb, xl = (old[k * nz : (k + 1) * nz, :] for k in range(3))
+    lame, shear = given[128:160, :], given[160:192, :]
+    new = stress_plane((xx, xx, xx, xb, xl, xl), here, v_first, (0.0,) * 3, lame, shear, ring_fore)
+    turned = jnp.concatenate([given[192:208, 0:128], given[192:208, 128:256]], axis=0)
+    settings = fault_settings(turned)
+    last = 11
+    xl = new[4]
+    before = settings[0] if slip is None else slip[...]
+    fresh, fixed = friction(pltpu.roll(xl[:, half : half + 128], last, 1), settings, before)
+    if slip_out is not None:
+        slip_out[...] = fresh
+    xl = jnp.concatenate([xl[:, 0:half], with_fault(xl[:, half:], fixed, last)], axis=1)
+    for k, value in enumerate((new[0], new[3], xl)):
+        out[k * nz : (k + 1) * nz, :] = jnp.where(has_x, value, 0.0)
+
+
+def fine_stress_kernel(step, s, v, m, rim, xr, settings, slip, flags, *refs):
+    last = step == 2
+    copies = []
+    nx, nz, half = s.shape[1], 32, s.shape[3] // 2
+    own = nz - RIM
+    if last:
+        final, v_final, slip_out, mark, out, sem = refs
+        mark[...] = jnp.zeros_like(mark)
+        copies.append(pltpu.make_async_copy(v.at[:, :, 0:own, :], v_final, sem.at[0]))
+        copies[0].start()
+    else:
+        if step == 0:
+            v_behind, given, out, slip_out, behind, slip_behind = refs
+            old, slip_before = given, None
+        else:
+            v_behind, given, old, slip_before, out, slip_out, behind = refs
+            slip_behind = None
+        stress_behind(
+            old, v_behind, [v[c, 0] for c in FINE_V], given, slip_before, flags, behind, slip_behind
+        )
+
+    def put(x, new):
+        for k, c in enumerate(FINE_S):
+            out[c, x] = new[k]
+        if last:
+            for first, end in ((0, 3), (4, 6)):
+                at = len(copies)
+                copies.append(
+                    pltpu.make_async_copy(out.at[first:end, x, 0:own, :], final.at[first:end, x], sem.at[at])
+                )
+                copies[at].start()
+
+    shear_plane = stress_planes(range(nx), s, v, m, rim, xr, flags, put)
+    fresh, fixed = friction(shear_plane, settings, slip[...])
     for x in range(nx):
-        moved = fixed if x == 0 else pltpu.roll(fixed, 128 - x, 1)
-        out[3, x, :, half : half + 128] = jnp.where(lane == 0, moved, out[3, x, :, half : half + 128])
+        out[3, x, :, half:] = with_fault(out[3, x, :, half:], fixed, x)
     if last:
         copies.append(pltpu.make_async_copy(out.at[3, :, 0:own, :], final.at[3], sem.at[len(copies)]))
         copies[-1].start()
@@ -428,10 +504,8 @@
         slip_out[...] = turned[0:nx, 0:own]
         for copy in copies:
             copy.wait()
-        return
-    slip_out[...] = fresh
-    for k, c in enumerate((0, 4, 3)):
-        xsend[k * nz : (k + 1) * nz, :] = out[c, nx - 1]
+    else:
+        slip_out[...] = fresh
 
 
 def coarse_velocity_kernel(cv, cs, cm, xr, below, above, rows_ref, flags, out, xsend, next_rows, cs_near, cm_near):
@@ -476,13 +550,11 @@
         xsend[24 + f : 25 + f, 0:128] = rows_ref[f, 0:1, :].astype(F32)
 
 
-def coarse_stress_kernel(cv, cs, cm, xr, zr, rows_ref, rest, rest_next, rest_before, flags, _, v_out, s_out):
+def coarse_stress_kernel(cv, cs, cm, xr, zr, rows_ref, rest, rest_next, flags, _, v_out, s_out):
     nx, ny, nz = cv.shape[1:]
     base = xr.shape[0] - 32
     has_x, has_y = has(flags, AFTER_X)[:, 0:128], has(flags, AFTER_Z)[:, 0:128]
     row_ids = own_rows(flags, (ny, nz))
-
-    before_x = has(flags, BEFORE_X)[:, 0:128]
 
     def inserted(plane, c, x):
         for f in range(2):
@@ -491,14 +563,7 @@
             else:
                 hit = row_ids == xr[base + 24 + f : base + 25 + f, 0:128]
             at = (f * 3 + c) * nx + x % nx
-            more = 6 * nx + f * 3 + c
-            if x == 0:
-                from_before = jnp.where(before_x, rest_before[more : more + 1, :], 0.0)
-                value = rest[at : at + 1, :] + from_before
-            elif x < nx:
-                value = rest[at : at + 1, :]
-            else:
-                value = rest_next[at : at + 1, :] + rest[more : more + 1, :]
+            value = rest[at : at + 1, :] if x < nx else rest_next[at : at + 1, :]
             plane = jnp.where(hit, value, plane)
         return plane
 
@@ -523,10 +588,20 @@
     return lax.ppermute(value, axis, [(i, i ^ bit) for i in range(count)])
 
 
-def spread(value, turns):
-    for bits in turns:
-        value = value + swap(value, "gy", bits)
-    return value
+PARTNERS = ((2, (1, 3, 0, 4), (6, 5, 7)), (5, (4, 6, 7, 3), (2, 0, 1)))
+
+
+def far(value, out):
+    parts = []
+    for turn in range(4):
+        pairs = []
+        for home, *lists in PARTNERS:
+            for core, chips in enumerate(lists):
+                if turn < len(chips):
+                    pair = (2 * home + core, 2 * chips[turn] + core)
+                    pairs.append(pair if out else pair[::-1])
+        parts.append(lax.ppermute(value, "gy", pairs))
+    return parts
 
 
 def body(
@@ -552,39 +627,50 @@
     shares = (6 * cx, cz)
     fault = (fault_slip, initial_shear, normal_stress, fault_mask, zone_ids)
     fields = (fine_velocity, fine_stress, fine_material)
+    zoned = (static_friction, friction_drop, weakening_distance)
     given = [
         pltpu.with_memory_space_constraint(a, pltpu.HBM)
-        for a in fields + (coarse_stress, coarse_velocity, coarse_material) + fault + (owner_rows,)
+        for a in fields + (coarse_stress, coarse_velocity, coarse_material) + fault + zoned + (owner_rows,)
     ]
-    up, down, coupling, raw = pl.pallas_call(
+    up, down, raw = pl.pallas_call(
         pack_kernel,
         out_shape=[
-            jax.ShapeDtypeStruct(shape, F32)
-            for shape in ((nx * 32 + 24, ny), (nx * 40 + 48, ny), shares, (nz, 128))
+            jax.ShapeDtypeStruct(shape, F32) for shape in ((nx * 32 + 24, ny), (nx * 40 + 48, ny), (nz, 128))
         ],
-        in_specs=[HBM] * len(given) + [VMEM],
-        out_specs=[VMEM] * 4,
+        in_specs=[HBM] * 14 + [VMEM],
+        out_specs=[VMEM] * 3,
         scratch_shapes=[pltpu.VMEM((a.shape[0], nx, 8, ny), F32) for a in fields * 2]
-        + [pltpu.VMEM((3, cx, 8, cz), F32), pltpu.VMEM(coarse_velocity.shape, F32)]
-        + [pltpu.VMEM((6, cx, 8, cz), F32), pltpu.VMEM((cx, 8, cz), F32)]
-        + [pltpu.VMEM(owner_rows.shape, jnp.int32)]
+        + [pltpu.VMEM((c, cx, 8, cz), F32) for c in (3, 3, 6)]
+        + [pltpu.VMEM((cx, 8, cz), F32)]
+        + [pltpu.SMEM(a.shape, F32) for a in zoned]
         + [pltpu.VMEM(a.shape, a.dtype) for a in fault]
-        + [pltpu.VMEM((128, 128), F32), pltpu.SemaphoreType.DMA((18,))],
+        + [pltpu.VMEM((128, 128), F32), pltpu.SemaphoreType.DMA((20,))],
         compiler_params=PARAMS,
-    )(*given, flags)
+    )(*given[:14], flags)
+    coupling = pl.pallas_call(
+        coupling_kernel,
+        out_shape=jax.ShapeDtypeStruct(shares, F32),
+        in_specs=[HBM] * 2 + [VMEM] * 2,
+        out_specs=VMEM,
+        scratch_shapes=[
+            pltpu.VMEM(coarse_velocity.shape, F32),
+            pltpu.VMEM(owner_rows.shape, jnp.int32),
+            pltpu.SemaphoreType.DMA((2,)),
+        ],
+        compiler_params=PARAMS,
+    )(given[4], given[14], flags, raw)
     from_below, from_above = ring(up, "gy", 1), ring(down, "gy", -1)
-    coupling = spread(coupling, (1, 2))
-    parts_of = jnp.concatenate([static_friction, friction_drop, 1.0 / weakening_distance, jnp.zeros(4, F32)])
-    parts_of = jnp.broadcast_to(parts_of[:, None], (16, 128))
-    rim, xsend, settings, bounds = call(
+    parts = far(coupling + swap(coupling, "gy", 1), True)
+    rim, xsend, settings = call(
         rim_kernel,
-        [(12, nx, RIM, ny), (128, ny), (7, 32, 128), shares],
-        [VMEM] * 9,
-        from_below, from_above, fine_stress, coarse_stress, raw, parts_of, flags, coupling, swap(coupling, "gy", 6),
+        [(12, nx, RIM, ny), (208, ny), (7, 32, 128)],
+        [VMEM] * 7,
+        from_below, from_above, fine_stress, fine_material, coarse_stress, raw, flags,
     )
     slip = settings[0]
     xr = ring(xsend, "gx", 1)
-    bounds = (bounds, swap(bounds, "gy", 8))
+    bounds = coupling + parts[0] + parts[1] + parts[2] + parts[3]
+    bounds = (bounds, swap(bounds, "gy", 1))
     coarse_moved, cxs, coarse_zr, coarse_stress, coarse_material = call(
         coarse_velocity_kernel,
         [coarse_velocity.shape, (32, ny), (16, cz), coarse_stress.shape, coarse_material.shape],
@@ -593,50 +679,51 @@
     )
     velocity, stress = fine_velocity, fine_stress
 
-    def velocity_half(step, xr, *more):
-        outs = [(3, nx, 32, ny), (96 + (16, 32, 0)[step], ny)]
-        if step == 2:
-            outs.append(more[0].shape)
-        return call(
-            lambda *refs: fine_velocity_kernel(step, *refs),
-            outs, [VMEM] * (8 + len(more)),
-            velocity, stress, fine_material, rim, xr, *bounds, flags, *more,
+    def velocity_half(step, behind, *to_send):
+        args = (velocity, stress, fine_material, rim, behind, *bounds, flags)
+        sends = call(
+            lambda *refs: velocity_edge_kernel(step, *refs),
+            [(96, ny), (96, ny)] if step == 0 else [(128, ny), (96, ny)] if step == 1 else [(72, ny)],
+            [VMEM] * (8 + len(to_send)), *args, *to_send,
         )
-
-    def stress_half(step, xr):
+        moved = [ring(send, "gx", way) for send, way in zip(sends, (-1, 1))]
+        (new,) = call(fine_velocity_kernel, [(3, nx, 32, ny)], [VMEM] * 8, *args)
+        return new, moved
+
+    def stress_half(step, xr, *more):
         return call(
             lambda *refs: fine_stress_kernel(step, *refs),
-            [(6, nx, 32, ny), (32, 128), (96, ny)], [VMEM] * 8,
-            stress, velocity, fine_material, rim, xr, settings, slip, flags,
+            [(6, nx, 32, ny), (32, 128), (96, ny), (32, 128)][: 4 - step], [VMEM] * (8 + len(more)),
+            stress, velocity, fine_material, rim, xr, settings, slip, flags, *more,
         )
 
-    velocity, xsend = velocity_half(0, xr)
-    next_x = ring(xsend, "gx", -1)
-    stress, slip, xsend = stress_half(0, next_x)
-    velocity, xsend = velocity_half(1, ring(xsend, "gx", 1), cxs)
-    coarse_xr = ring(xsend, "gx", -1)
-    stress, slip, xsend = stress_half(1, coarse_xr)
-    (share,) = call(share_kernel, [(32, cz)], [VMEM] * 7, velocity, stress, fine_material, next_x, *bounds, flags)
-    share, xsend = lax.optimization_barrier((share, xsend))
-    share = spread(share, (1,))
-    velocity, xsend, share = velocity_half(2, ring(xsend, "gx", 1), share, swap(share, "gy", 2))
-    restricted = spread(share, (6, 8))
-    restricted_next, restricted_before = ring(restricted, "gx", -1), ring(restricted, "gx", 1)
-    xr = ring(xsend, "gx", -1)
-    stress, velocity, slip = pl.pallas_call(
+    given_behind = xr
+    velocity, (xr, v_behind) = velocity_half(0, given_behind)
+    stress, slip, behind, slip_behind = stress_half(0, xr, v_behind, given_behind)
+    velocity, (coarse_xr, v_behind) = velocity_half(1, behind, cxs)
+    stress, slip, behind = stress_half(1, coarse_xr, v_behind, given_behind, behind, slip_behind)
+    (share,) = call(share_kernel, [shares], [VMEM] * 7, velocity, stress, fine_material, behind, *bounds, flags)
+    share = share + swap(share, "gy", 1)
+    velocity, (xr,) = velocity_half(2, behind)
+    share, velocity = lax.optimization_barrier((share, velocity))
+    parts = far(share, False)
+    rest = parts[0] + parts[1] + parts[2] + parts[3]
+    restricted = share + rest + swap(rest, "gy", 1)
+    restricted_next = ring(restricted, "gx", -1)
+    stress, velocity, slip, mark = pl.pallas_call(
         lambda *refs: fine_stress_kernel(2, *refs),
-        out_shape=[jax.ShapeDtypeStruct(a.shape, F32) for a in (fine_stress, fine_velocity, fault_slip)],
+        out_shape=[jax.ShapeDtypeStruct(a.shape, F32) for a in (fine_stress, fine_velocity, fault_slip, raw[0:8])],
         in_specs=[VMEM] * 8,
-        out_specs=[pl.BlockSpec(memory_space=pl.ANY)] * 2 + [VMEM],
+        out_specs=[pl.BlockSpec(memory_space=pl.ANY)] * 2 + [VMEM] * 2,
         scratch_shapes=[pltpu.VMEM((6, nx, 32, ny), F32), pltpu.SemaphoreType.DMA((2 * nx + 2,))],
         compiler_params=PARAMS,
     )(stress, velocity, fine_material, rim, xr, settings, slip, flags)
     coarse_next, coarse_stress_next = call(
         coarse_stress_kernel,
         [coarse_velocity.shape, coarse_stress.shape],
-        [VMEM] * 11,
+        [VMEM] * 10,
         coarse_moved, coarse_stress, coarse_material, coarse_xr, coarse_zr, owner_rows, restricted, restricted_next,
-        restricted_before, flags, slip,
+        flags, mark,
     )
     return (coarse_next, coarse_stress_next, velocity, stress, slip)
 

time: 79.8 us -> 70.8 us (0.89)
  the two profiles are of different devices: /device:TPU:16 before, /device:TPU:48 now
where the time goes in v3:
time: 70.8 us; the launch traced here: 70.5 us
  starting transfers between devices  31.2 us (44%)
  waiting for transfers between devices  24.8 us (35%)
  Pallas kernels  13.4 us (19%)
  between operations  0.94 us (1%)
    ppermute x9, waiting for transfers between devices, ring(): lax.ppermute(value, axis, [(i, (i + steps) % count) for i in range(count)])  18.5 us
    ppermute x8, starting transfers between devices, far(): parts.append(lax.ppermute(value, 'gy', pairs))  17.5 us
    ppermute x9, starting transfers between devices, ring(): lax.ppermute(value, axis, [(i, (i + steps) % count) for i in range(count)])  9.27 us
    pallas_call x12, Pallas kernels, call(): pl.pallas_call(kernel, out_shape=tuple((jax.ShapeDtypeStruct(shape, F32)...  7.31 us
    ppermute x4, starting transfers between devices, swap(): return lax.ppermute(value, axis, [(i, i ^ bit) for i in range(count)])  4.45 us
    ppermute x8, waiting for transfers between devices, far(): parts.append(lax.ppermute(value, 'gy', pairs))  4.31 us
    pallas_call x1, Pallas kernels, body(): pl.pallas_call(lambda *refs: fine_stress_kernel(2, *refs), out_shape=[jax...  2.8 us
    pallas_call x1, Pallas kernels, body(): pl.pallas_call(pack_kernel, out_shape=[jax.ShapeDtypeStruct(shape, F32) f...  2.3 us
  transfers between devices with their start and end apart: 21, of which 9 were waited for; matrix products, arithmetic and copies ran while one was open for 0% of the time, Pallas kernels for 9%

profile of v3, /device:TPU:48, one launch (start us, length us, event | category | flops | bytes accessed | tf_op | source)
XLA Modules:
  0.0 70.5 jit_solution(8193650037317351669)
XLA Ops:
  0.8 2.3 %shard_map.182 = (f32[408,256]{1,0:T(8,128)S(1)}, f32[528,256]{1,0:T(8,128)S(1)}, f32[24,128]{1,0:T(8,128)S(1)}) custom-call(f32[3,12,24,256]{3,2,1,0:T(8,128)} %refs_0_.2, f32[6,12,24,256]{3,2,1,0:T(8,128)} %refs_0_.3, f32[3,12,24,256]{3,2,1,0:T(8,128)} %refs_2_.11, f32[6,4,16,128]{3,2,1,0:T(8,128)} %cs.5, f32[3,4,16,128]{3,2,1,0:T(8,128)} %cv.5, ...), custom_call_target="tpu_custom_call" | custom-call | tf_op jit(solution)/shard_map/pallas_call | solution.py:635
  3.7 1.0 %shard_map.185 = f32[24,128]{1,0:T(8,128)S(1)} custom-call(f32[3,4,16,128]{3,2,1,0:T(8,128)} %cv.5, s32[2,4,128]{2,1,0:T(4,128)} %rows_ref.3, f32[8,256]{1,0:T(8,128)S(1)} %broadcast_in_dim.2._.flags.refs_7_, f32[24,128]{1,0:T(8,128)S(1)} %get-tuple-element.37.raw._), custom_call_target="tpu_custom_call" | custom-call | tf_op jit(solution)/shard_map/pallas_call | solution.py:650
  4.7 1.7 %collective-permute-start.3 = (f32[24,128]{1,0:T(8,128)S(1)}, f32[24,128]{1,0:T(8,128)S(1)}, u32[]{:S(2)}, u32[]{:S(2)}) collective-permute-start(f32[24,128]{1,0:T(8,128)S(1)} %shard_map.185), channel_id=1, source_target_pairs={{0,1},{1,0},{2,3},{3,2},{4,5},{5,4},{6,7},{7,6},{8,9},{9,8},{10,11... | collective-permute-start | bytes 36872 | tf_op jit(solution)/shard_map/ppermute | solution.py:588
  6.3 0.8 %collective-permute-done.3 = f32[24,128]{1,0:T(8,128)S(1)} collective-permute-done((f32[24,128]{1,0:T(8,128)S(1)}, f32[24,128]{1,0:T(8,128)S(1)}, u32[]{:S(2)}, u32[]{:S(2)}) %collective-permute-start.3) | collective-permute-done | bytes 12320 | tf_op jit(solution)/shard_map/ppermute | solution.py:588
  7.2 7.9 %collective-permute-start.7 = (f32[24,128]{1,0:T(8,128)S(1)}, f32[24,128]{1,0:T(8,128)S(1)}, u32[]{:S(2)}, u32[]{:S(2)}) collective-permute-start(f32[24,128]{1,0:T(8,128)S(1)} %add.33), channel_id=1, source_target_pairs={{4,8},{10,6},{20,24},{26,22},{36,40},{42,38},{52,56},{58,54},{68,7... | collective-permute-start | bytes 36872 | tf_op jit(solution)/shard_map/ppermute | solution.py:603
  15.0 1.3 %collective-permute-start.6 = (f32[24,128]{1,0:T(8,128)S(1)}, f32[24,128]{1,0:T(8,128)S(1)}, u32[]{:S(2)}, u32[]{:S(2)}) collective-permute-start(f32[24,128]{1,0:T(8,128)S(1)} %add.33), channel_id=1, source_target_pairs={{4,0},{5,15},{10,14},{11,3},{20,16},{21,31},{26,30},{27,19},{36,32... | collective-permute-start | bytes 36872 | tf_op jit(solution)/shard_map/ppermute | solution.py:603
  16.3 1.3 %collective-permute-start.5 = (f32[24,128]{1,0:T(8,128)S(1)}, f32[24,128]{1,0:T(8,128)S(1)}, u32[]{:S(2)}, u32[]{:S(2)}) collective-permute-start(f32[24,128]{1,0:T(8,128)S(1)} %add.33), channel_id=1, source_target_pairs={{4,6},{5,11},{10,12},{11,1},{20,22},{21,27},{26,28},{27,17},{36,38... | collective-permute-start | bytes 36872 | tf_op jit(solution)/shard_map/ppermute | solution.py:603
  17.7 1.9 %collective-permute-start.4 = (f32[24,128]{1,0:T(8,128)S(1)}, f32[24,128]{1,0:T(8,128)S(1)}, u32[]{:S(2)}, u32[]{:S(2)}) collective-permute-start(f32[24,128]{1,0:T(8,128)S(1)} %add.33), channel_id=1, source_target_pairs={{4,2},{5,13},{10,8},{11,5},{20,18},{21,29},{26,24},{27,21},{36,34}... | collective-permute-start | bytes 36872 | tf_op jit(solution)/shard_map/ppermute | solution.py:603
  19.9 2.2 %collective-permute-start.2 = (f32[208,256]{1,0:T(8,128)S(1)}, f32[208,256]{1,0:T(8,128)S(1)}, u32[]{:S(2)}, u32[]{:S(2)}) collective-permute-start(f32[208,256]{1,0:T(8,128)S(1)} %get-tuple-element.38), channel_id=1, source_target_pairs={{0,16},{16,32},{32,48},{48,64},{64,80},{80,96},{96,112},{112,0},{1... | collective-permute-start | bytes 638984 | tf_op jit(solution)/shard_map/ppermute | solution.py:32
  22.2 1.3 %collective-permute-start.8 = (f32[24,128]{1,0:T(8,128)S(1)}, f32[24,128]{1,0:T(8,128)S(1)}, u32[]{:S(2)}, u32[]{:S(2)}) collective-permute-start(f32[24,128]{1,0:T(8,128)S(1)} %add_add_fusion.2.bounds_a.refs_5_), channel_id=1, source_target_pairs={{0,1},{1,0},{2,3},{3,2},{4,5},{5,4},{6,7},{7,6},{8,9},{9,8},{10,11... | collective-permute-start | bytes 36872 | tf_op jit(solution)/shard_map/ppermute | solution.py:588
  23.5 0.8 %collective-permute-done.8.bounds_b.refs_6_ = f32[24,128]{1,0:T(8,128)S(1)} collective-permute-done((f32[24,128]{1,0:T(8,128)S(1)}, f32[24,128]{1,0:T(8,128)S(1)}, u32[]{:S(2)}, u32[]{:S(2)}) %collective-permute-start.8) | collective-permute-done | bytes 12320 | tf_op jit(solution)/shard_map/ppermute | solution.py:588
  24.3 4.9 %collective-permute-done.2.xr.behind.refs_4_.refs_9_ = f32[208,256]{1,0:T(8,128)S(1)} collective-permute-done((f32[208,256]{1,0:T(8,128)S(1)}, f32[208,256]{1,0:T(8,128)S(1)}, u32[]{:S(2)}, u32[]{:S(2)}) %collective-permute-start.2) | collective-permute-done | bytes 213024 | tf_op jit(solution)/shard_map/ppermute | solution.py:32
  29.5 2.8 %collective-permute-start.9 = (f32[96,256]{1,0:T(8,128)S(1)}, f32[96,256]{1,0:T(8,128)S(1)}, u32[]{:S(2)}, u32[]{:S(2)}) collective-permute-start(f32[96,256]{1,0:T(8,128)S(1)} %get-tuple-element.43), channel_id=1, source_target_pairs={{0,112},{16,0},{32,16},{48,32},{64,48},{80,64},{96,80},{112,96},{1... | collective-permute-start | bytes 294920 | tf_op jit(solution)/shard_map/ppermute | solution.py:32
  32.5 0.8 %shard_map.186.refs_1_.refs_0_.v = f32[3,12,32,256]{3,2,1,0:T(8,128)S(1)} custom-call(f32[3,12,24,256]{3,2,1,0:T(8,128)S(1)} %copy-done.2, f32[6,12,24,256]{3,2,1,0:T(8,128)S(1)} %copy-done.1, f32[3,12,24,256]{3,2,1,0:T(8,128)S(1)} %copy-done, f32[12,12,8,256]{3,2,1,0:T(8,128)S(1)} %get-tuple-element.42.rim.refs_3_, ...), custom_call_target="tpu_custom_call" | custom-call | tf_op jit(solution)/shard_map/pallas_call | solution.py:21
  33.3 1.9 %collective-permute-done.9.refs_4_ = f32[96,256]{1,0:T(8,128)S(1)} collective-permute-done((f32[96,256]{1,0:T(8,128)S(1)}, f32[96,256]{1,0:T(8,128)S(1)}, u32[]{:S(2)}, u32[]{:S(2)}) %collective-permute-start.9) | collective-permute-done | bytes 98336 | tf_op jit(solution)/shard_map/ppermute | solution.py:32
  35.2 3.9 %collective-permute-done.10.refs_8_ = f32[96,256]{1,0:T(8,128)S(1)} collective-permute-done((f32[96,256]{1,0:T(8,128)S(1)}, f32[96,256]{1,0:T(8,128)S(1)}, u32[]{:S(2)}, u32[]{:S(2)}) %collective-permute-start.10) | collective-permute-done | bytes 98336 | tf_op jit(solution)/shard_map/ppermute | solution.py:32
  39.1 1.3 %shard_map.188 = (f32[6,12,32,256]{3,2,1,0:T(8,128)S(1)}, f32[32,128]{1,0:T(8,128)S(1)}, f32[96,256]{1,0:T(8,128)S(1)}, f32[32,128]{1,0:T(8,128)S(1)}) custom-call(f32[6,12,24,256]{3,2,1,0:T(8,128)S(1)} %copy-done.1, f32[3,12,32,256]{3,2,1,0:T(8,128)S(1)} %shard_map.186.refs_1_.refs_0_.v, f32[3,12,24,256]{3,2,1,0:T(8,128)S(1)} %copy-done, ...), custom_call_target="tpu_custom_call" | custom-call | tf_op jit(solution)/shard_map/pallas_call | solution.py:21
  40.7 0.8 %collective-permute-start.11 = (f32[128,256]{1,0:T(8,128)S(1)}, f32[128,256]{1,0:T(8,128)S(1)}, u32[]{:S(2)}, u32[]{:S(2)}) collective-permute-start(f32[128,256]{1,0:T(8,128)S(1)} %get-tuple-element.49), channel_id=1, source_target_pairs={{0,112},{16,0},{32,16},{48,32},{64,48},{80,64},{96,80},{112,96},{1... | collective-permute-start | bytes 393224 | tf_op jit(solution)/shard_map/ppermute | solution.py:32
  41.5 1.3 %collective-permute-start.12 = (f32[96,256]{1,0:T(8,128)S(1)}, f32[96,256]{1,0:T(8,128)S(1)}, u32[]{:S(2)}, u32[]{:S(2)}) collective-permute-start(f32[96,256]{1,0:T(8,128)S(1)} %get-tuple-element.52), channel_id=1, source_target_pairs={{0,16},{16,32},{32,48},{48,64},{64,80},{80,96},{96,112},{112,0},{1... | collective-permute-start | bytes 294920 | tf_op jit(solution)/shard_map/ppermute | solution.py:32
  42.8 0.8 %shard_map.190.refs_1_.v.refs_0_ = f32[3,12,32,256]{3,2,1,0:T(8,128)S(1)} custom-call(f32[3,12,32,256]{3,2,1,0:T(8,128)S(1)} %shard_map.186.refs_1_.refs_0_.v, f32[6,12,32,256]{3,2,1,0:T(8,128)S(1)} %get-tuple-element.46.refs_1_.s.refs_0_, f32[3,12,24,256]{3,2,1,0:T(8,128)S(1)} %copy-done, f32[12,12,8,256]{3,2,1,0:T(8,128)S(1)} %get-tuple-element.42.rim.refs_3_, ...), custom_call_target="tpu_custom_call" | custom-call | tf_op jit(solution)/shard_map/pallas_call | solution.py:21
  43.5 4.7 %collective-permute-done.12.refs_8_ = f32[96,256]{1,0:T(8,128)S(1)} collective-permute-done((f32[96,256]{1,0:T(8,128)S(1)}, f32[96,256]{1,0:T(8,128)S(1)}, u32[]{:S(2)}, u32[]{:S(2)}) %collective-permute-start.12) | collective-permute-done | bytes 98336 | tf_op jit(solution)/shard_map/ppermute | solution.py:32
  48.2 1.3 %shard_map.191 = (f32[6,12,32,256]{3,2,1,0:T(8,128)S(1)}, f32[32,128]{1,0:T(8,128)S(1)}, f32[96,256]{1,0:T(8,128)S(1)}) custom-call(f32[6,12,32,256]{3,2,1,0:T(8,128)S(1)} %get-tuple-element.46.refs_1_.s.refs_0_, f32[3,12,32,256]{3,2,1,0:T(8,128)S(1)} %shard_map.190.refs_1_.v.refs_0_, f32[3,12,24,256]{3,2,1,0:T(8,128)S(1)} %copy-done, ...), custom_call_target="tpu_custom_call" | custom-call | tf_op jit(solution)/shard_map/pallas_call | solution.py:21
  51.3 1.3 %collective-permute-start.17 = (f32[24,128]{1,0:T(8,128)S(1)}, f32[24,128]{1,0:T(8,128)S(1)}, u32[]{:S(2)}, u32[]{:S(2)}) collective-permute-start(f32[24,128]{1,0:T(8,128)S(1)} %add.38), channel_id=1, source_target_pairs={{8,4},{6,10},{24,20},{22,26},{40,36},{38,42},{56,52},{54,58},{72,6... | collective-permute-start | bytes 36872 | tf_op jit(solution)/shard_map/ppermute | solution.py:603
  52.6 1.3 %collective-permute-start.16 = (f32[24,128]{1,0:T(8,128)S(1)}, f32[24,128]{1,0:T(8,128)S(1)}, u32[]{:S(2)}, u32[]{:S(2)}) collective-permute-start(f32[24,128]{1,0:T(8,128)S(1)} %add.38), channel_id=1, source_target_pairs={{0,4},{15,5},{14,10},{3,11},{16,20},{31,21},{30,26},{19,27},{32,36... | collective-permute-start | bytes 36872 | tf_op jit(solution)/shard_map/ppermute | solution.py:603
  53.9 1.3 %collective-permute-start.15 = (f32[24,128]{1,0:T(8,128)S(1)}, f32[24,128]{1,0:T(8,128)S(1)}, u32[]{:S(2)}, u32[]{:S(2)}) collective-permute-start(f32[24,128]{1,0:T(8,128)S(1)} %add.38), channel_id=1, source_target_pairs={{6,4},{11,5},{12,10},{1,11},{22,20},{27,21},{28,26},{17,27},{38,36... | collective-permute-start | bytes 36872 | tf_op jit(solution)/shard_map/ppermute | solution.py:603
  55.2 1.3 %collective-permute-start.14 = (f32[24,128]{1,0:T(8,128)S(1)}, f32[24,128]{1,0:T(8,128)S(1)}, u32[]{:S(2)}, u32[]{:S(2)}) collective-permute-start(f32[24,128]{1,0:T(8,128)S(1)} %add.38), channel_id=1, source_target_pairs={{2,4},{13,5},{8,10},{5,11},{18,20},{29,21},{24,26},{21,27},{34,36}... | collective-permute-start | bytes 36872 | tf_op jit(solution)/shard_map/ppermute | solution.py:603
  56.5 4.3 %collective-permute-done.17 = f32[24,128]{1,0:T(8,128)S(1)} collective-permute-done((f32[24,128]{1,0:T(8,128)S(1)}, f32[24,128]{1,0:T(8,128)S(1)}, u32[]{:S(2)}, u32[]{:S(2)}) %collective-permute-start.17) | collective-permute-done | bytes 12320 | tf_op jit(solution)/shard_map/ppermute | solution.py:603
  60.8 1.4 %collective-permute-start.18 = (f32[24,128]{1,0:T(8,128)S(1)}, f32[24,128]{1,0:T(8,128)S(1)}, u32[]{:S(2)}, u32[]{:S(2)}) collective-permute-start(f32[24,128]{1,0:T(8,128)S(1)} %add_add_fusion.1), channel_id=1, source_target_pairs={{0,1},{1,0},{2,3},{3,2},{4,5},{5,4},{6,7},{7,6},{8,9},{9,8},{10,11... | collective-permute-start | bytes 36872 | tf_op jit(solution)/shard_map/ppermute | solution.py:588
  62.4 0.9 %collective-permute-start.20 = (f32[72,256]{1,0:T(8,128)S(1)}, f32[72,256]{1,0:T(8,128)S(1)}, u32[]{:S(2)}, u32[]{:S(2)}) collective-permute-start(f32[72,256]{1,0:T(8,128)S(1)} %shard_map.194), channel_id=1, source_target_pairs={{0,112},{16,0},{32,16},{48,32},{64,48},{80,64},{96,80},{112,96},{1... | collective-permute-start | bytes 221192 | tf_op jit(solution)/shard_map/ppermute | solution.py:32
  63.9 3.0 %collective-permute-done.20.refs_4_ = f32[72,256]{1,0:T(8,128)S(1)} collective-permute-done((f32[72,256]{1,0:T(8,128)S(1)}, f32[72,256]{1,0:T(8,128)S(1)}, u32[]{:S(2)}, u32[]{:S(2)}) %collective-permute-start.20) | collective-permute-done | bytes 73760 | tf_op jit(solution)/shard_map/ppermute | solution.py:32
  66.9 2.8 %shard_map.195 = (f32[6,12,24,256]{3,2,1,0:T(8,128)}, f32[3,12,24,256]{3,2,1,0:T(8,128)}, f32[12,24]{1,0:T(8,128)}, f32[8,128]{1,0:T(8,128)S(1)}) custom-call(f32[6,12,32,256]{3,2,1,0:T(8,128)S(1)} %get-tuple-element.54.s.refs_1_.refs_0_, f32[3,12,32,256]{3,2,1,0:T(8,128)S(1)} %shard_map.193.refs_1_, f32[3,12,24,256]{3,2,1,0:T(8,128)S(1)} %copy-done, ...), custom_call_target="tpu_custom_call" | custom-call | tf_op jit(solution)/shard_map/pallas_call | solution.py:713
  69.7 0.8 %shard_map.196 = (f32[3,4,16,128]{3,2,1,0:T(8,128)}, f32[6,4,16,128]{3,2,1,0:T(8,128)}) custom-call(f32[3,4,16,128]{3,2,1,0:T(8,128)S(1)} %get-tuple-element.39.cv, f32[6,4,16,128]{3,2,1,0:T(8,128)S(1)} %get-tuple-element.40.cs, f32[3,4,16,128]{3,2,1,0:T(8,128)S(1)} %get-tuple-element.41.cm, f32[128,256]{1,0:T(8,128)S(1)} %collective-permute-done.11.refs_4_.xr, ...), custom_call_target="tpu_custom_call" | custom-call | tf_op jit(solution)/shard_map/pallas_call | solution.py:21
  (47 shorter events, 4.3 us)
Async XLA Ops:
  0.8 18.7 %copy-start = (f32[3,12,24,256]{3,2,1,0:T(8,128)S(1)}, f32[3,12,24,256]{3,2,1,0:T(8,128)}, u32[]{:S(2)}) copy-start(f32[3,12,24,256]{3,2,1,0:T(8,128)} %refs_2_.11) | copy-start | bytes 2654212
  0.8 18.7 %copy-start.1 = (f32[6,12,24,256]{3,2,1,0:T(8,128)S(1)}, f32[6,12,24,256]{3,2,1,0:T(8,128)}, u32[]{:S(2)}) copy-start(f32[6,12,24,256]{3,2,1,0:T(8,128)} %refs_0_.3) | copy-start | bytes 5308420
  0.8 18.8 %copy-start.3 = (f32[6,4,16,128]{3,2,1,0:T(8,128)S(1)}, f32[6,4,16,128]{3,2,1,0:T(8,128)}, u32[]{:S(2)}) copy-start(f32[6,4,16,128]{3,2,1,0:T(8,128)} %cs.5) | copy-start | bytes 589828
  3.1 16.4 %collective-permute-start.1 = (f32[528,256]{1,0:T(8,128)S(1)}, f32[528,256]{1,0:T(8,128)S(1)}, u32[]{:S(2)}, u32[]{:S(2)}) collective-permute-start(f32[528,256]{1,0:T(8,128)S(1)} %get-tuple-element.36), channel_id=1, source_target_pairs={{0,15},{1,0},{2,1},{3,2},{4,3},{5,4},{6,5},{7,6},{8,7},{9,8},{10,9... | collective-permute-start | bytes 1622024 | tf_op jit(solution)/shard_map/ppermute | solution.py:32
  3.2 14.4 %collective-permute-start = (f32[408,256]{1,0:T(8,128)S(1)}, f32[408,256]{1,0:T(8,128)S(1)}, u32[]{:S(2)}, u32[]{:S(2)}) collective-permute-start(f32[408,256]{1,0:T(8,128)S(1)} %get-tuple-element.35), channel_id=1, source_target_pairs={{0,1},{1,2},{2,3},{3,4},{4,5},{5,6},{6,7},{7,8},{8,9},{9,10},{10,1... | collective-permute-start | bytes 1253384 | tf_op jit(solution)/shard_map/ppermute | solution.py:32
  4.7 2.5 %collective-permute-start.3 = (f32[24,128]{1,0:T(8,128)S(1)}, f32[24,128]{1,0:T(8,128)S(1)}, u32[]{:S(2)}, u32[]{:S(2)}) collective-permute-start(f32[24,128]{1,0:T(8,128)S(1)} %shard_map.185), channel_id=1, source_target_pairs={{0,1},{1,0},{2,3},{3,2},{4,5},{5,4},{6,7},{7,6},{8,9},{9,8},{10,11... | collective-permute-start | bytes 36872 | tf_op jit(solution)/shard_map/ppermute | solution.py:588
  7.2 22.1 %copy-start.2 = (f32[3,12,24,256]{3,2,1,0:T(8,128)S(1)}, f32[3,12,24,256]{3,2,1,0:T(8,128)}, u32[]{:S(2)}) copy-start(f32[3,12,24,256]{3,2,1,0:T(8,128)} %refs_0_.2) | copy-start | bytes 2654212
  7.2 15.0 %collective-permute-start.7 = (f32[24,128]{1,0:T(8,128)S(1)}, f32[24,128]{1,0:T(8,128)S(1)}, u32[]{:S(2)}, u32[]{:S(2)}) collective-permute-start(f32[24,128]{1,0:T(8,128)S(1)} %add.33), channel_id=1, source_target_pairs={{4,8},{10,6},{20,24},{26,22},{36,40},{42,38},{52,56},{58,54},{68,7... | collective-permute-start | bytes 36872 | tf_op jit(solution)/shard_map/ppermute | solution.py:603
  15.0 7.1 %collective-permute-start.6 = (f32[24,128]{1,0:T(8,128)S(1)}, f32[24,128]{1,0:T(8,128)S(1)}, u32[]{:S(2)}, u32[]{:S(2)}) collective-permute-start(f32[24,128]{1,0:T(8,128)S(1)} %add.33), channel_id=1, source_target_pairs={{4,0},{5,15},{10,14},{11,3},{20,16},{21,31},{26,30},{27,19},{36,32... | collective-permute-start | bytes 36872 | tf_op jit(solution)/shard_map/ppermute | solution.py:603
  16.3 5.8 %collective-permute-start.5 = (f32[24,128]{1,0:T(8,128)S(1)}, f32[24,128]{1,0:T(8,128)S(1)}, u32[]{:S(2)}, u32[]{:S(2)}) collective-permute-start(f32[24,128]{1,0:T(8,128)S(1)} %add.33), channel_id=1, source_target_pairs={{4,6},{5,11},{10,12},{11,1},{20,22},{21,27},{26,28},{27,17},{36,38... | collective-permute-start | bytes 36872 | tf_op jit(solution)/shard_map/ppermute | solution.py:603
  17.7 4.5 %collective-permute-start.4 = (f32[24,128]{1,0:T(8,128)S(1)}, f32[24,128]{1,0:T(8,128)S(1)}, u32[]{:S(2)}, u32[]{:S(2)}) collective-permute-start(f32[24,128]{1,0:T(8,128)S(1)} %add.33), channel_id=1, source_target_pairs={{4,2},{5,13},{10,8},{11,5},{20,18},{21,29},{26,24},{27,21},{36,34}... | collective-permute-start | bytes 36872 | tf_op jit(solution)/shard_map/ppermute | solution.py:603
  19.9 9.4 %collective-permute-start.2 = (f32[208,256]{1,0:T(8,128)S(1)}, f32[208,256]{1,0:T(8,128)S(1)}, u32[]{:S(2)}, u32[]{:S(2)}) collective-permute-start(f32[208,256]{1,0:T(8,128)S(1)} %get-tuple-element.38), channel_id=1, source_target_pairs={{0,16},{16,32},{32,48},{48,64},{64,80},{80,96},{96,112},{112,0},{1... | collective-permute-start | bytes 638984 | tf_op jit(solution)/shard_map/ppermute | solution.py:32
  22.2 2.1 %collective-permute-start.8 = (f32[24,128]{1,0:T(8,128)S(1)}, f32[24,128]{1,0:T(8,128)S(1)}, u32[]{:S(2)}, u32[]{:S(2)}) collective-permute-start(f32[24,128]{1,0:T(8,128)S(1)} %add_add_fusion.2.bounds_a.refs_5_), channel_id=1, source_target_pairs={{0,1},{1,0},{2,3},{3,2},{4,5},{5,4},{6,7},{7,6},{8,9},{9,8},{10,11... | collective-permute-start | bytes 36872 | tf_op jit(solution)/shard_map/ppermute | solution.py:588
  29.2 3.1 %copy-start.4 = (f32[3,4,16,128]{3,2,1,0:T(8,128)S(1)}, f32[3,4,16,128]{3,2,1,0:T(8,128)}, u32[]{:S(2)}) copy-start(f32[3,4,16,128]{3,2,1,0:T(8,128)} %cv.5) | copy-start | bytes 294916
  29.2 3.1 %copy-start.5 = (f32[3,4,16,128]{3,2,1,0:T(8,128)S(1)}, f32[3,4,16,128]{3,2,1,0:T(8,128)}, u32[]{:S(2)}) copy-start(f32[3,4,16,128]{3,2,1,0:T(8,128)} %cm.3) | copy-start | bytes 294916
  29.3 3.1 %copy-start.6 = (s32[2,4,128]{2,1,0:T(4,128)S(1)}, s32[2,4,128]{2,1,0:T(4,128)}, u32[]{:S(2)}) copy-start(s32[2,4,128]{2,1,0:T(4,128)} %rows_ref.3) | copy-start | bytes 12292
  29.5 5.7 %collective-permute-start.9 = (f32[96,256]{1,0:T(8,128)S(1)}, f32[96,256]{1,0:T(8,128)S(1)}, u32[]{:S(2)}, u32[]{:S(2)}) collective-permute-start(f32[96,256]{1,0:T(8,128)S(1)} %get-tuple-element.43), channel_id=1, source_target_pairs={{0,112},{16,0},{32,16},{48,32},{64,48},{80,64},{96,80},{112,96},{1... | collective-permute-start | bytes 294920 | tf_op jit(solution)/shard_map/ppermute | solution.py:32
  32.3 6.8 %collective-permute-start.10 = (f32[96,256]{1,0:T(8,128)S(1)}, f32[96,256]{1,0:T(8,128)S(1)}, u32[]{:S(2)}, u32[]{:S(2)}) collective-permute-start(f32[96,256]{1,0:T(8,128)S(1)} %get-tuple-element.45), channel_id=1, source_target_pairs={{0,16},{16,32},{32,48},{48,64},{64,80},{80,96},{96,112},{112,0},{1... | collective-permute-start | bytes 294920 | tf_op jit(solution)/shard_map/ppermute | solution.py:32
  40.7 7.5 %collective-permute-start.11 = (f32[128,256]{1,0:T(8,128)S(1)}, f32[128,256]{1,0:T(8,128)S(1)}, u32[]{:S(2)}, u32[]{:S(2)}) collective-permute-start(f32[128,256]{1,0:T(8,128)S(1)} %get-tuple-element.49), channel_id=1, source_target_pairs={{0,112},{16,0},{32,16},{48,32},{64,48},{80,64},{96,80},{112,96},{1... | collective-permute-start | bytes 393224 | tf_op jit(solution)/shard_map/ppermute | solution.py:32
  41.5 6.7 %collective-permute-start.12 = (f32[96,256]{1,0:T(8,128)S(1)}, f32[96,256]{1,0:T(8,128)S(1)}, u32[]{:S(2)}, u32[]{:S(2)}) collective-permute-start(f32[96,256]{1,0:T(8,128)S(1)} %get-tuple-element.52), channel_id=1, source_target_pairs={{0,16},{16,32},{32,48},{48,64},{64,80},{80,96},{96,112},{112,0},{1... | collective-permute-start | bytes 294920 | tf_op jit(solution)/shard_map/ppermute | solution.py:32
  50.1 1.3 %collective-permute-start.13 = (f32[24,128]{1,0:T(8,128)S(1)}, f32[24,128]{1,0:T(8,128)S(1)}, u32[]{:S(2)}, u32[]{:S(2)}) collective-permute-start(f32[24,128]{1,0:T(8,128)S(1)} %shard_map.192), channel_id=1, source_target_pairs={{0,1},{1,0},{2,3},{3,2},{4,5},{5,4},{6,7},{7,6},{8,9},{9,8},{10,11... | collective-permute-start | bytes 36872 | tf_op jit(solution)/shard_map/ppermute | solution.py:588
  51.3 9.5 %collective-permute-start.17 = (f32[24,128]{1,0:T(8,128)S(1)}, f32[24,128]{1,0:T(8,128)S(1)}, u32[]{:S(2)}, u32[]{:S(2)}) collective-permute-start(f32[24,128]{1,0:T(8,128)S(1)} %add.38), channel_id=1, source_target_pairs={{8,4},{6,10},{24,20},{22,26},{40,36},{38,42},{56,52},{54,58},{72,6... | collective-permute-start | bytes 36872 | tf_op jit(solution)/shard_map/ppermute | solution.py:603
  52.6 8.2 %collective-permute-start.16 = (f32[24,128]{1,0:T(8,128)S(1)}, f32[24,128]{1,0:T(8,128)S(1)}, u32[]{:S(2)}, u32[]{:S(2)}) collective-permute-start(f32[24,128]{1,0:T(8,128)S(1)} %add.38), channel_id=1, source_target_pairs={{0,4},{15,5},{14,10},{3,11},{16,20},{31,21},{30,26},{19,27},{32,36... | collective-permute-start | bytes 36872 | tf_op jit(solution)/shard_map/ppermute | solution.py:603
  53.9 6.9 %collective-permute-start.15 = (f32[24,128]{1,0:T(8,128)S(1)}, f32[24,128]{1,0:T(8,128)S(1)}, u32[]{:S(2)}, u32[]{:S(2)}) collective-permute-start(f32[24,128]{1,0:T(8,128)S(1)} %add.38), channel_id=1, source_target_pairs={{6,4},{11,5},{12,10},{1,11},{22,20},{27,21},{28,26},{17,27},{38,36... | collective-permute-start | bytes 36872 | tf_op jit(solution)/shard_map/ppermute | solution.py:603
  55.2 5.6 %collective-permute-start.14 = (f32[24,128]{1,0:T(8,128)S(1)}, f32[24,128]{1,0:T(8,128)S(1)}, u32[]{:S(2)}, u32[]{:S(2)}) collective-permute-start(f32[24,128]{1,0:T(8,128)S(1)} %add.38), channel_id=1, source_target_pairs={{2,4},{13,5},{8,10},{5,11},{18,20},{29,21},{24,26},{21,27},{34,36}... | collective-permute-start | bytes 36872 | tf_op jit(solution)/shard_map/ppermute | solution.py:603
  60.8 2.5 %collective-permute-start.18 = (f32[24,128]{1,0:T(8,128)S(1)}, f32[24,128]{1,0:T(8,128)S(1)}, u32[]{:S(2)}, u32[]{:S(2)}) collective-permute-start(f32[24,128]{1,0:T(8,128)S(1)} %add_add_fusion.1), channel_id=1, source_target_pairs={{0,1},{1,0},{2,3},{3,2},{4,5},{5,4},{6,7},{7,6},{8,9},{9,8},{10,11... | collective-permute-start | bytes 36872 | tf_op jit(solution)/shard_map/ppermute | solution.py:588
  62.4 4.5 %collective-permute-start.20 = (f32[72,256]{1,0:T(8,128)S(1)}, f32[72,256]{1,0:T(8,128)S(1)}, u32[]{:S(2)}, u32[]{:S(2)}) collective-permute-start(f32[72,256]{1,0:T(8,128)S(1)} %shard_map.194), channel_id=1, source_target_pairs={{0,112},{16,0},{32,16},{48,32},{64,48},{80,64},{96,80},{112,96},{1... | collective-permute-start | bytes 221192 | tf_op jit(solution)/shard_map/ppermute | solution.py:32
  63.3 6.4 %collective-permute-start.19 = (f32[24,128]{1,0:T(8,128)S(1)}, f32[24,128]{1,0:T(8,128)S(1)}, u32[]{:S(2)}, u32[]{:S(2)}) collective-permute-start(f32[24,128]{1,0:T(8,128)S(1)} %add_add_fusion.rest), channel_id=1, source_target_pairs={{0,112},{16,0},{32,16},{48,32},{64,48},{80,64},{96,80},{112,96},{1... | collective-permute-start | bytes 36872 | tf_op jit(solution)/shard_map/ppermute | solution.py:32

commit v4 on v3

--- a/solution.py
+++ b/solution.py
@@ -115,6 +115,7 @@
 
 
 RIM = 8
+EDGES = (0, 10, 11)
 
 
 def part_of(field, refs):
@@ -305,6 +306,8 @@
 
 
 def reader(ref, rim, first):
+    if ref.shape[1] == len(EDGES):
+        return lambda c, x: ref[c, EDGES.index(x)]
     if ref.shape[2] == 32:
         return lambda c, x: ref[c, x]
     return lambda c, x: jnp.concatenate([ref[c, x], rim[first + c, x]], axis=0)
@@ -461,6 +464,20 @@
         out[k * nz : (k + 1) * nz, :] = jnp.where(has_x, value, 0.0)
 
 
+def stress_edge_kernel(s, v, m, rim, xr, settings, slip, flags, v_behind, given, out, behind, slip_behind):
+    half = s.shape[3] // 2
+    stress_behind(given, v_behind, [v[c, 0] for c in FINE_V], given, None, flags, behind, slip_behind)
+
+    def put(x, new):
+        for k, c in enumerate(FINE_S):
+            out[c, EDGES.index(x)] = new[k]
+
+    shear_plane = stress_planes(EDGES, s, v, m, rim, xr, flags, put)
+    _, fixed = friction(shear_plane, settings, slip[...])
+    for at, x in enumerate(EDGES):
+        out[3, at, :, half:] = with_fault(out[3, at, :, half:], fixed, x)
+
+
 def fine_stress_kernel(step, s, v, m, rim, xr, settings, slip, flags, *refs):
     last = step == 2
     copies = []
@@ -472,15 +489,12 @@
         copies.append(pltpu.make_async_copy(v.at[:, :, 0:own, :], v_final, sem.at[0]))
         copies[0].start()
     else:
-        if step == 0:
-            v_behind, given, out, slip_out, behind, slip_behind = refs
-            old, slip_before = given, None
+        if step == 1:
+            v_behind, given, old, slip_before, out, slip_out, behind = refs
+            first = [v[c, 0] for c in FINE_V]
+            stress_behind(old, v_behind, first, given, slip_before, flags, behind, None)
         else:
-            v_behind, given, old, slip_before, out, slip_out, behind = refs
-            slip_behind = None
-        stress_behind(
-            old, v_behind, [v[c, 0] for c in FINE_V], given, slip_before, flags, behind, slip_behind
-        )
+            out, slip_out = refs
 
     def put(x, new):
         for k, c in enumerate(FINE_S):
@@ -588,19 +602,11 @@
     return lax.ppermute(value, axis, [(i, i ^ bit) for i in range(count)])
 
 
-PARTNERS = ((2, (1, 3, 0, 4), (6, 5, 7)), (5, (4, 6, 7, 3), (2, 0, 1)))
-
-
-def far(value, out):
+def apart(value, out):
     parts = []
-    for turn in range(4):
-        pairs = []
-        for home, *lists in PARTNERS:
-            for core, chips in enumerate(lists):
-                if turn < len(chips):
-                    pair = (2 * home + core, 2 * chips[turn] + core)
-                    pairs.append(pair if out else pair[::-1])
-        parts.append(lax.ppermute(value, "gy", pairs))
+    for turn in range(1, 8):
+        pairs = [(home, 2 * ((home // 2 + turn) % 8) + home % 2) for home in (5, 10)]
+        parts.append(lax.ppermute(value, "gy", [pair if out else pair[::-1] for pair in pairs]))
     return parts
 
 
@@ -660,7 +666,7 @@
         compiler_params=PARAMS,
     )(given[4], given[14], flags, raw)
     from_below, from_above = ring(up, "gy", 1), ring(down, "gy", -1)
-    parts = far(coupling + swap(coupling, "gy", 1), True)
+    parts = apart(coupling, True)
     rim, xsend, settings = call(
         rim_kernel,
         [(12, nx, RIM, ny), (208, ny), (7, 32, 128)],
@@ -669,7 +675,7 @@
     )
     slip = settings[0]
     xr = ring(xsend, "gx", 1)
-    bounds = coupling + parts[0] + parts[1] + parts[2] + parts[3]
+    bounds = coupling + sum(parts[1:], parts[0])
     bounds = (bounds, swap(bounds, "gy", 1))
     coarse_moved, cxs, coarse_zr, coarse_stress, coarse_material = call(
         coarse_velocity_kernel,
@@ -681,34 +687,40 @@
 
     def velocity_half(step, behind, *to_send):
         args = (velocity, stress, fine_material, rim, behind, *bounds, flags)
+        near = (velocity, edges, *args[2:]) if step == 1 else args
         sends = call(
             lambda *refs: velocity_edge_kernel(step, *refs),
             [(96, ny), (96, ny)] if step == 0 else [(128, ny), (96, ny)] if step == 1 else [(72, ny)],
-            [VMEM] * (8 + len(to_send)), *args, *to_send,
+            [VMEM] * (8 + len(to_send) * (step < 2)), *near, *(to_send if step < 2 else ()),
         )
+        sends = list(sends)
+        if step == 2:
+            sends[0], *to_send = lax.optimization_barrier((sends[0], *to_send))
         moved = [ring(send, "gx", way) for send, way in zip(sends, (-1, 1))]
         (new,) = call(fine_velocity_kernel, [(3, nx, 32, ny)], [VMEM] * 8, *args)
-        return new, moved
+        return (new, moved, *to_send) if step == 2 else (new, moved)
 
     def stress_half(step, xr, *more):
         return call(
             lambda *refs: fine_stress_kernel(step, *refs),
-            [(6, nx, 32, ny), (32, 128), (96, ny), (32, 128)][: 4 - step], [VMEM] * (8 + len(more)),
+            [(6, nx, 32, ny), (32, 128), (96, ny)][: 2 + step], [VMEM] * (8 + len(more)),
             stress, velocity, fine_material, rim, xr, settings, slip, flags, *more,
         )
 
     given_behind = xr
     velocity, (xr, v_behind) = velocity_half(0, given_behind)
-    stress, slip, behind, slip_behind = stress_half(0, xr, v_behind, given_behind)
+    edges, behind, slip_behind = call(
+        stress_edge_kernel, [(6, len(EDGES), 32, ny), (96, ny), (32, 128)], [VMEM] * 10,
+        stress, velocity, fine_material, rim, xr, settings, slip, flags, v_behind, given_behind,
+    )
+    stress, slip = stress_half(0, xr)
     velocity, (coarse_xr, v_behind) = velocity_half(1, behind, cxs)
     stress, slip, behind = stress_half(1, coarse_xr, v_behind, given_behind, behind, slip_behind)
     (share,) = call(share_kernel, [shares], [VMEM] * 7, velocity, stress, fine_material, behind, *bounds, flags)
     share = share + swap(share, "gy", 1)
-    velocity, (xr,) = velocity_half(2, behind)
-    share, velocity = lax.optimization_barrier((share, velocity))
-    parts = far(share, False)
-    rest = parts[0] + parts[1] + parts[2] + parts[3]
-    restricted = share + rest + swap(rest, "gy", 1)
+    velocity, (xr,), share = velocity_half(2, behind, share)
+    parts = apart(share, False)
+    restricted = share + sum(parts[1:], parts[0])
     restricted_next = ring(restricted, "gx", -1)
     stress, velocity, slip, mark = pl.pallas_call(
         lambda *refs: fine_stress_kernel(2, *refs),

time: 70.8 us -> 67.8 us (0.958)
  the two profiles are of different devices: /device:TPU:48 before, /device:TPU:31 now
where the time goes in v4:
time: 67.8 us; the launch traced here: 67 us
  starting transfers between devices  31.7 us (47%)
  waiting for transfers between devices  20.5 us (30%)
  Pallas kernels  13.6 us (20%)
  between operations  1.04 us (2%)
    ppermute x14, starting transfers between devices, apart(): lax.ppermute(value, 'gy', [pair if out else pair[::-1] for pair in pairs])  16.4 us
    ppermute x14, waiting for transfers between devices, apart(): lax.ppermute(value, 'gy', [pair if out else pair[::-1] for pair in pairs])  12.5 us
    ppermute x9, starting transfers between devices, ring(): lax.ppermute(value, axis, [(i, (i + steps) % count) for i in range(count)])  12.1 us
    pallas_call x13, Pallas kernels, call(): pl.pallas_call(kernel, out_shape=tuple((jax.ShapeDtypeStruct(shape, F32)...  7.55 us
    ppermute x9, waiting for transfers between devices, ring(): lax.ppermute(value, axis, [(i, (i + steps) % count) for i in range(count)])  6.08 us
    ppermute x2, starting transfers between devices, swap(): return lax.ppermute(value, axis, [(i, i ^ bit) for i in range(count)])  3.21 us
    pallas_call x1, Pallas kernels, body(): pl.pallas_call(lambda *refs: fine_stress_kernel(2, *refs), out_shape=[jax...  2.76 us
    pallas_call x1, Pallas kernels, body(): pl.pallas_call(pack_kernel, out_shape=[jax.ShapeDtypeStruct(shape, F32) f...  2.3 us
  transfers between devices with their start and end apart: 25, of which 8 were waited for; matrix products, arithmetic and copies ran while one was open for 0% of the time, Pallas kernels for 12%

profile of v4, /device:TPU:31, one launch (start us, length us, event | category | flops | bytes accessed | tf_op | source)
XLA Modules:
  0.0 67.0 jit_solution(18200158917687539798)
XLA Ops:
  0.8 2.3 %shard_map.182 = (f32[408,256]{1,0:T(8,128)S(1)}, f32[528,256]{1,0:T(8,128)S(1)}, f32[24,128]{1,0:T(8,128)S(1)}) custom-call(f32[3,12,24,256]{3,2,1,0:T(8,128)} %refs_0_.2, f32[6,12,24,256]{3,2,1,0:T(8,128)} %refs_0_.3, f32[3,12,24,256]{3,2,1,0:T(8,128)} %refs_2_.11, f32[6,4,16,128]{3,2,1,0:T(8,128)} %cs.5, f32[3,4,16,128]{3,2,1,0:T(8,128)} %cv.5, ...), custom_call_target="tpu_custom_call" | custom-call | tf_op jit(solution)/shard_map/pallas_call | solution.py:641
  3.1 0.7 %collective-permute-start.1 = (f32[528,256]{1,0:T(8,128)S(1)}, f32[528,256]{1,0:T(8,128)S(1)}, u32[]{:S(2)}, u32[]{:S(2)}) collective-permute-start(f32[528,256]{1,0:T(8,128)S(1)} %get-tuple-element.37), channel_id=1, source_target_pairs={{0,15},{1,0},{2,1},{3,2},{4,3},{5,4},{6,5},{7,6},{8,7},{9,8},{10,9... | collective-permute-start | bytes 1622024 | tf_op jit(solution)/shard_map/ppermute | solution.py:32
  3.9 1.6 %collective-permute-start = (f32[408,256]{1,0:T(8,128)S(1)}, f32[408,256]{1,0:T(8,128)S(1)}, u32[]{:S(2)}, u32[]{:S(2)}) collective-permute-start(f32[408,256]{1,0:T(8,128)S(1)} %get-tuple-element.36), channel_id=1, source_target_pairs={{0,1},{1,2},{2,3},{3,4},{4,5},{5,6},{6,7},{7,8},{8,9},{9,10},{10,1... | collective-permute-start | bytes 1253384 | tf_op jit(solution)/shard_map/ppermute | solution.py:32
  5.5 1.0 %shard_map.185 = f32[24,128]{1,0:T(8,128)S(1)} custom-call(f32[3,4,16,128]{3,2,1,0:T(8,128)} %cv.5, s32[2,4,128]{2,1,0:T(4,128)} %rows_ref.3, f32[8,256]{1,0:T(8,128)S(1)} %broadcast_in_dim.2._.flags.refs_7_, f32[24,128]{1,0:T(8,128)S(1)} %get-tuple-element.38.raw._), custom_call_target="tpu_custom_call" | custom-call | tf_op jit(solution)/shard_map/pallas_call | solution.py:656
  6.4 0.8 %collective-permute-start.9 = (f32[24,128]{1,0:T(8,128)S(1)}, f32[24,128]{1,0:T(8,128)S(1)}, u32[]{:S(2)}, u32[]{:S(2)}) collective-permute-start(f32[24,128]{1,0:T(8,128)S(1)} %shard_map.185), channel_id=1, source_target_pairs={{5,3},{10,8},{21,19},{26,24},{37,35},{42,40},{53,51},{58,56},{69,6... | collective-permute-start | bytes 36872 | tf_op jit(solution)/shard_map/ppermute | solution.py:609
  7.2 0.7 collective-permute-start.8
  7.9 0.7 collective-permute-start.7
  8.6 0.7 collective-permute-start.6
  9.3 0.7 collective-permute-start.5
  10.5 1.3 %collective-permute-start.4 = (f32[24,128]{1,0:T(8,128)S(1)}, f32[24,128]{1,0:T(8,128)S(1)}, u32[]{:S(2)}, u32[]{:S(2)}) collective-permute-start(f32[24,128]{1,0:T(8,128)S(1)} %shard_map.185), channel_id=1, source_target_pairs={{5,9},{10,14},{21,25},{26,30},{37,41},{42,46},{53,57},{58,62},{69,... | collective-permute-start | bytes 36872 | tf_op jit(solution)/shard_map/ppermute | solution.py:609
  11.7 0.7 %collective-permute-done.1.from_above.above = f32[528,256]{1,0:T(8,128)S(1)} collective-permute-done((f32[528,256]{1,0:T(8,128)S(1)}, f32[528,256]{1,0:T(8,128)S(1)}, u32[]{:S(2)}, u32[]{:S(2)}) %collective-permute-start.1) | collective-permute-done | bytes 540704 | tf_op jit(solution)/shard_map/ppermute | solution.py:32
  13.9 12.5 %collective-permute-done.4 = f32[24,128]{1,0:T(8,128)S(1)} collective-permute-done((f32[24,128]{1,0:T(8,128)S(1)}, f32[24,128]{1,0:T(8,128)S(1)}, u32[]{:S(2)}, u32[]{:S(2)}) %collective-permute-start.4) | collective-permute-done | bytes 12320 | tf_op jit(solution)/shard_map/ppermute | solution.py:609
  26.5 1.2 %collective-permute-done.10.bounds_b.refs_6_ = f32[24,128]{1,0:T(8,128)S(1)} collective-permute-done((f32[24,128]{1,0:T(8,128)S(1)}, f32[24,128]{1,0:T(8,128)S(1)}, u32[]{:S(2)}, u32[]{:S(2)}) %collective-permute-start.10) | collective-permute-done | bytes 12320 | tf_op jit(solution)/shard_map/ppermute | solution.py:602
  28.0 3.6 %collective-permute-start.12 = (f32[96,256]{1,0:T(8,128)S(1)}, f32[96,256]{1,0:T(8,128)S(1)}, u32[]{:S(2)}, u32[]{:S(2)}) collective-permute-start(f32[96,256]{1,0:T(8,128)S(1)} %get-tuple-element.46), channel_id=1, source_target_pairs={{0,16},{16,32},{32,48},{48,64},{64,80},{80,96},{96,112},{112,0},{1... | collective-permute-start | bytes 294920 | tf_op jit(solution)/shard_map/ppermute | solution.py:32
  31.7 0.8 %shard_map.186.v.refs_0_.refs_1_ = f32[3,12,32,256]{3,2,1,0:T(8,128)S(1)} custom-call(f32[3,12,24,256]{3,2,1,0:T(8,128)S(1)} %copy-done.2, f32[6,12,24,256]{3,2,1,0:T(8,128)S(1)} %copy-done.1, f32[3,12,24,256]{3,2,1,0:T(8,128)S(1)} %copy-done, f32[12,12,8,256]{3,2,1,0:T(8,128)S(1)} %get-tuple-element.43.rim.refs_3_, ...), custom_call_target="tpu_custom_call" | custom-call | tf_op jit(solution)/shard_map/pallas_call | solution.py:21
  32.5 1.8 %collective-permute-done.11.xr.refs_4_ = f32[96,256]{1,0:T(8,128)S(1)} collective-permute-done((f32[96,256]{1,0:T(8,128)S(1)}, f32[96,256]{1,0:T(8,128)S(1)}, u32[]{:S(2)}, u32[]{:S(2)}) %collective-permute-start.11) | collective-permute-done | bytes 98336 | tf_op jit(solution)/shard_map/ppermute | solution.py:32
  35.3 3.4 %collective-permute-start.14 = (f32[96,256]{1,0:T(8,128)S(1)}, f32[96,256]{1,0:T(8,128)S(1)}, u32[]{:S(2)}, u32[]{:S(2)}) collective-permute-start(f32[96,256]{1,0:T(8,128)S(1)} %get-tuple-element.54), channel_id=1, source_target_pairs={{0,16},{16,32},{32,48},{48,64},{64,80},{80,96},{96,112},{112,0},{1... | collective-permute-start | bytes 294920 | tf_op jit(solution)/shard_map/ppermute | solution.py:32
  38.6 1.1 %shard_map.190 = (f32[6,12,32,256]{3,2,1,0:T(8,128)S(1)}, f32[32,128]{1,0:T(8,128)S(1)}) custom-call(f32[6,12,24,256]{3,2,1,0:T(8,128)S(1)} %copy-done.1, f32[3,12,32,256]{3,2,1,0:T(8,128)S(1)} %shard_map.186.v.refs_0_.refs_1_, f32[3,12,24,256]{3,2,1,0:T(8,128)S(1)} %copy-done, f32[12,12,8,256]{3,2,1,0:T(8,128)S(1)} %get-tuple-element.43.rim.refs_3_, ...), custom_call_target="tpu_custom_call" | custom-call | tf_op jit(solution)/shard_map/pallas_call | solution.py:21
  39.8 0.8 %shard_map.191.refs_1_.refs_0_.v = f32[3,12,32,256]{3,2,1,0:T(8,128)S(1)} custom-call(f32[3,12,32,256]{3,2,1,0:T(8,128)S(1)} %shard_map.186.v.refs_0_.refs_1_, f32[6,12,32,256]{3,2,1,0:T(8,128)S(1)} %get-tuple-element.52.s.refs_0_, f32[3,12,24,256]{3,2,1,0:T(8,128)S(1)} %copy-done, f32[12,12,8,256]{3,2,1,0:T(8,128)S(1)} %get-tuple-element.43.rim.refs_3_, ...), custom_call_target="tpu_custom_call" | custom-call | tf_op jit(solution)/shard_map/pallas_call | solution.py:21
  41.1 1.3 %shard_map.192 = (f32[6,12,32,256]{3,2,1,0:T(8,128)S(1)}, f32[32,128]{1,0:T(8,128)S(1)}, f32[96,256]{1,0:T(8,128)S(1)}) custom-call(f32[6,12,32,256]{3,2,1,0:T(8,128)S(1)} %get-tuple-element.52.s.refs_0_, f32[3,12,32,256]{3,2,1,0:T(8,128)S(1)} %shard_map.191.refs_1_.refs_0_.v, f32[3,12,24,256]{3,2,1,0:T(8,128)S(1)} %copy-done, ...), custom_call_target="tpu_custom_call" | custom-call | tf_op jit(solution)/shard_map/pallas_call | solution.py:21
  42.9 3.1 %collective-permute-start.15 = (f32[24,128]{1,0:T(8,128)S(1)}, f32[24,128]{1,0:T(8,128)S(1)}, u32[]{:S(2)}, u32[]{:S(2)}) collective-permute-start(f32[24,128]{1,0:T(8,128)S(1)} %shard_map.194), channel_id=1, source_target_pairs={{0,1},{1,0},{2,3},{3,2},{4,5},{5,4},{6,7},{7,6},{8,9},{9,8},{10,11... | collective-permute-start | bytes 36872 | tf_op jit(solution)/shard_map/ppermute | solution.py:602
  46.2 0.7 %collective-permute-done.15 = f32[24,128]{1,0:T(8,128)S(1)} collective-permute-done((f32[24,128]{1,0:T(8,128)S(1)}, f32[24,128]{1,0:T(8,128)S(1)}, u32[]{:S(2)}, u32[]{:S(2)}) %collective-permute-start.15) | collective-permute-done | bytes 12320 | tf_op jit(solution)/shard_map/ppermute | solution.py:602
  47.6 0.7 collective-permute-start.21
  48.2 0.7 collective-permute-start.20
  48.9 0.7 collective-permute-start.19
  50.3 7.1 %collective-permute-start.17 = (f32[24,128]{1,0:T(8,128)S(1)}, f32[24,128]{1,0:T(8,128)S(1)}, u32[]{:S(2)}, u32[]{:S(2)}) collective-permute-start(f32[24,128]{1,0:T(8,128)S(1)} %add.52), channel_id=1, source_target_pairs={{9,5},{14,10},{25,21},{30,26},{41,37},{46,42},{57,53},{62,58},{73,... | collective-permute-start | bytes 36872 | tf_op jit(solution)/shard_map/ppermute | solution.py:609
  57.4 0.7 collective-permute-start.16
  58.2 1.9 %collective-permute-start.23 = (f32[24,128]{1,0:T(8,128)S(1)}, f32[24,128]{1,0:T(8,128)S(1)}, u32[]{:S(2)}, u32[]{:S(2)}) collective-permute-start(f32[24,128]{1,0:T(8,128)S(1)} %add_add_fusion.rest), channel_id=1, source_target_pairs={{0,112},{16,0},{32,16},{48,32},{64,48},{80,64},{96,80},{112,96},{1... | collective-permute-start | bytes 36872 | tf_op jit(solution)/shard_map/ppermute | solution.py:32
  60.1 0.8 %shard_map.195.refs_1_ = f32[3,12,32,256]{3,2,1,0:T(8,128)S(1)} custom-call(f32[3,12,32,256]{3,2,1,0:T(8,128)S(1)} %shard_map.191.refs_1_.refs_0_.v, f32[6,12,32,256]{3,2,1,0:T(8,128)S(1)} %get-tuple-element.56.refs_1_.s.refs_0_, f32[3,12,24,256]{3,2,1,0:T(8,128)S(1)} %copy-done, f32[12,12,8,256]{3,2,1,0:T(8,128)S(1)} %get-tuple-element.43.rim.refs_3_, ...), custom_call_target="tpu_custom_call" | custom-call | tf_op jit(solution)/shard_map/pallas_call | solution.py:21
  60.9 2.5 %collective-permute-done.24.refs_4_ = f32[72,256]{1,0:T(8,128)S(1)} collective-permute-done((f32[72,256]{1,0:T(8,128)S(1)}, f32[72,256]{1,0:T(8,128)S(1)}, u32[]{:S(2)}, u32[]{:S(2)}) %collective-permute-start.24) | collective-permute-done | bytes 73760 | tf_op jit(solution)/shard_map/ppermute | solution.py:32
  63.4 2.8 %shard_map.196 = (f32[6,12,24,256]{3,2,1,0:T(8,128)}, f32[3,12,24,256]{3,2,1,0:T(8,128)}, f32[12,24]{1,0:T(8,128)}, f32[8,128]{1,0:T(8,128)S(1)}) custom-call(f32[6,12,32,256]{3,2,1,0:T(8,128)S(1)} %get-tuple-element.56.refs_1_.s.refs_0_, f32[3,12,32,256]{3,2,1,0:T(8,128)S(1)} %shard_map.195.refs_1_, f32[3,12,24,256]{3,2,1,0:T(8,128)S(1)} %copy-done, ...), custom_call_target="tpu_custom_call" | custom-call | tf_op jit(solution)/shard_map/pallas_call | solution.py:725
  66.2 0.8 %shard_map.197 = (f32[3,4,16,128]{3,2,1,0:T(8,128)}, f32[6,4,16,128]{3,2,1,0:T(8,128)}) custom-call(f32[3,4,16,128]{3,2,1,0:T(8,128)S(1)} %get-tuple-element.40.cv, f32[6,4,16,128]{3,2,1,0:T(8,128)S(1)} %get-tuple-element.41.cs, f32[3,4,16,128]{3,2,1,0:T(8,128)S(1)} %get-tuple-element.42.cm, f32[128,256]{1,0:T(8,128)S(1)} %collective-permute-done.13.refs_4_.xr, ...), custom_call_target="tpu_custom_call" | custom-call | tf_op jit(solution)/shard_map/pallas_call | solution.py:21
  (54 shorter events, 6.2 us)
Async XLA Ops:
  0.8 12.3 %copy-start = (f32[3,12,24,256]{3,2,1,0:T(8,128)S(1)}, f32[3,12,24,256]{3,2,1,0:T(8,128)}, u32[]{:S(2)}) copy-start(f32[3,12,24,256]{3,2,1,0:T(8,128)} %refs_2_.11) | copy-start | bytes 2654212
  0.8 12.3 %copy-start.1 = (f32[6,12,24,256]{3,2,1,0:T(8,128)S(1)}, f32[6,12,24,256]{3,2,1,0:T(8,128)}, u32[]{:S(2)}) copy-start(f32[6,12,24,256]{3,2,1,0:T(8,128)} %refs_0_.3) | copy-start | bytes 5308420
  0.8 12.3 %copy-start.3 = (f32[6,4,16,128]{3,2,1,0:T(8,128)S(1)}, f32[6,4,16,128]{3,2,1,0:T(8,128)}, u32[]{:S(2)}) copy-start(f32[6,4,16,128]{3,2,1,0:T(8,128)} %cs.5) | copy-start | bytes 589828
  3.1 9.3 %collective-permute-start.1 = (f32[528,256]{1,0:T(8,128)S(1)}, f32[528,256]{1,0:T(8,128)S(1)}, u32[]{:S(2)}, u32[]{:S(2)}) collective-permute-start(f32[528,256]{1,0:T(8,128)S(1)} %get-tuple-element.37), channel_id=1, source_target_pairs={{0,15},{1,0},{2,1},{3,2},{4,3},{5,4},{6,5},{7,6},{8,7},{9,8},{10,9... | collective-permute-start | bytes 1622024 | tf_op jit(solution)/shard_map/ppermute | solution.py:32
  3.9 6.6 %collective-permute-start = (f32[408,256]{1,0:T(8,128)S(1)}, f32[408,256]{1,0:T(8,128)S(1)}, u32[]{:S(2)}, u32[]{:S(2)}) collective-permute-start(f32[408,256]{1,0:T(8,128)S(1)} %get-tuple-element.36), channel_id=1, source_target_pairs={{0,1},{1,2},{2,3},{3,4},{4,5},{5,6},{6,7},{7,8},{8,9},{9,10},{10,1... | collective-permute-start | bytes 1253384 | tf_op jit(solution)/shard_map/ppermute | solution.py:32
  6.4 21.2 %copy-start.2 = (f32[3,12,24,256]{3,2,1,0:T(8,128)S(1)}, f32[3,12,24,256]{3,2,1,0:T(8,128)}, u32[]{:S(2)}) copy-start(f32[3,12,24,256]{3,2,1,0:T(8,128)} %refs_0_.2) | copy-start | bytes 2654212
  6.4 2.1 %collective-permute-start.9 = (f32[24,128]{1,0:T(8,128)S(1)}, f32[24,128]{1,0:T(8,128)S(1)}, u32[]{:S(2)}, u32[]{:S(2)}) collective-permute-start(f32[24,128]{1,0:T(8,128)S(1)} %shard_map.185), channel_id=1, source_target_pairs={{5,3},{10,8},{21,19},{26,24},{37,35},{42,40},{53,51},{58,56},{69,6... | collective-permute-start | bytes 36872 | tf_op jit(solution)/shard_map/ppermute | solution.py:609
  7.2 2.0 %collective-permute-start.8 = (f32[24,128]{1,0:T(8,128)S(1)}, f32[24,128]{1,0:T(8,128)S(1)}, u32[]{:S(2)}, u32[]{:S(2)}) collective-permute-start(f32[24,128]{1,0:T(8,128)S(1)} %shard_map.185), channel_id=1, source_target_pairs={{5,1},{10,6},{21,17},{26,22},{37,33},{42,38},{53,49},{58,54},{69,6... | collective-permute-start | bytes 36872 | tf_op jit(solution)/shard_map/ppermute | solution.py:609
  7.9 5.5 %collective-permute-start.7 = (f32[24,128]{1,0:T(8,128)S(1)}, f32[24,128]{1,0:T(8,128)S(1)}, u32[]{:S(2)}, u32[]{:S(2)}) collective-permute-start(f32[24,128]{1,0:T(8,128)S(1)} %shard_map.185), channel_id=1, source_target_pairs={{5,15},{10,4},{21,31},{26,20},{37,47},{42,36},{53,63},{58,52},{69,... | collective-permute-start | bytes 36872 | tf_op jit(solution)/shard_map/ppermute | solution.py:609
  8.6 5.3 %collective-permute-start.6 = (f32[24,128]{1,0:T(8,128)S(1)}, f32[24,128]{1,0:T(8,128)S(1)}, u32[]{:S(2)}, u32[]{:S(2)}) collective-permute-start(f32[24,128]{1,0:T(8,128)S(1)} %shard_map.185), channel_id=1, source_target_pairs={{5,13},{10,2},{21,29},{26,18},{37,45},{42,34},{53,61},{58,50},{69,... | collective-permute-start | bytes 36872 | tf_op jit(solution)/shard_map/ppermute | solution.py:609
  9.3 4.6 %collective-permute-start.5 = (f32[24,128]{1,0:T(8,128)S(1)}, f32[24,128]{1,0:T(8,128)S(1)}, u32[]{:S(2)}, u32[]{:S(2)}) collective-permute-start(f32[24,128]{1,0:T(8,128)S(1)} %shard_map.185), channel_id=1, source_target_pairs={{5,11},{10,0},{21,27},{26,16},{37,43},{42,32},{53,59},{58,48},{69,... | collective-permute-start | bytes 36872 | tf_op jit(solution)/shard_map/ppermute | solution.py:609
  10.5 15.9 %collective-permute-start.4 = (f32[24,128]{1,0:T(8,128)S(1)}, f32[24,128]{1,0:T(8,128)S(1)}, u32[]{:S(2)}, u32[]{:S(2)}) collective-permute-start(f32[24,128]{1,0:T(8,128)S(1)} %shard_map.185), channel_id=1, source_target_pairs={{5,9},{10,14},{21,25},{26,30},{37,41},{42,46},{53,57},{58,62},{69,... | collective-permute-start | bytes 36872 | tf_op jit(solution)/shard_map/ppermute | solution.py:609
  12.4 14.0 %collective-permute-start.3 = (f32[24,128]{1,0:T(8,128)S(1)}, f32[24,128]{1,0:T(8,128)S(1)}, u32[]{:S(2)}, u32[]{:S(2)}) collective-permute-start(f32[24,128]{1,0:T(8,128)S(1)} %shard_map.185), channel_id=1, source_target_pairs={{5,7},{10,12},{21,23},{26,28},{37,39},{42,44},{53,55},{58,60},{69,... | collective-permute-start | bytes 36872 | tf_op jit(solution)/shard_map/ppermute | solution.py:609
  13.4 14.2 %collective-permute-start.2 = (f32[208,256]{1,0:T(8,128)S(1)}, f32[208,256]{1,0:T(8,128)S(1)}, u32[]{:S(2)}, u32[]{:S(2)}) collective-permute-start(f32[208,256]{1,0:T(8,128)S(1)} %get-tuple-element.39), channel_id=1, source_target_pairs={{0,16},{16,32},{32,48},{48,64},{64,80},{80,96},{96,112},{112,0},{1... | collective-permute-start | bytes 638984 | tf_op jit(solution)/shard_map/ppermute | solution.py:32
  26.4 1.3 %collective-permute-start.10 = (f32[24,128]{1,0:T(8,128)S(1)}, f32[24,128]{1,0:T(8,128)S(1)}, u32[]{:S(2)}, u32[]{:S(2)}) collective-permute-start(f32[24,128]{1,0:T(8,128)S(1)} %add_add_fusion.1.bounds_a.refs_5_), channel_id=1, source_target_pairs={{0,1},{1,0},{2,3},{3,2},{4,5},{5,4},{6,7},{7,6},{8,9},{9,8},{10,11... | collective-permute-start | bytes 36872 | tf_op jit(solution)/shard_map/ppermute | solution.py:602
  27.7 3.9 %copy-start.4 = (f32[3,4,16,128]{3,2,1,0:T(8,128)S(1)}, f32[3,4,16,128]{3,2,1,0:T(8,128)}, u32[]{:S(2)}) copy-start(f32[3,4,16,128]{3,2,1,0:T(8,128)} %cv.5) | copy-start | bytes 294916
  27.7 3.9 %copy-start.5 = (f32[3,4,16,128]{3,2,1,0:T(8,128)S(1)}, f32[3,4,16,128]{3,2,1,0:T(8,128)}, u32[]{:S(2)}) copy-start(f32[3,4,16,128]{3,2,1,0:T(8,128)} %cm.3) | copy-start | bytes 294916
  27.7 3.9 %copy-start.6 = (s32[2,4,128]{2,1,0:T(4,128)S(1)}, s32[2,4,128]{2,1,0:T(4,128)}, u32[]{:S(2)}) copy-start(s32[2,4,128]{2,1,0:T(4,128)} %rows_ref.3) | copy-start | bytes 12292
  27.9 6.4 %collective-permute-start.11 = (f32[96,256]{1,0:T(8,128)S(1)}, f32[96,256]{1,0:T(8,128)S(1)}, u32[]{:S(2)}, u32[]{:S(2)}) collective-permute-start(f32[96,256]{1,0:T(8,128)S(1)} %get-tuple-element.44), channel_id=1, source_target_pairs={{0,112},{16,0},{32,16},{48,32},{64,48},{80,64},{96,80},{112,96},{1... | collective-permute-start | bytes 294920 | tf_op jit(solution)/shard_map/ppermute | solution.py:32
  28.0 6.3 %collective-permute-start.12 = (f32[96,256]{1,0:T(8,128)S(1)}, f32[96,256]{1,0:T(8,128)S(1)}, u32[]{:S(2)}, u32[]{:S(2)}) collective-permute-start(f32[96,256]{1,0:T(8,128)S(1)} %get-tuple-element.46), channel_id=1, source_target_pairs={{0,16},{16,32},{32,48},{48,64},{64,80},{80,96},{96,112},{112,0},{1... | collective-permute-start | bytes 294920 | tf_op jit(solution)/shard_map/ppermute | solution.py:32
  35.0 6.1 %collective-permute-start.13 = (f32[128,256]{1,0:T(8,128)S(1)}, f32[128,256]{1,0:T(8,128)S(1)}, u32[]{:S(2)}, u32[]{:S(2)}) collective-permute-start(f32[128,256]{1,0:T(8,128)S(1)} %get-tuple-element.50), channel_id=1, source_target_pairs={{0,112},{16,0},{32,16},{48,32},{64,48},{80,64},{96,80},{112,96},{1... | collective-permute-start | bytes 393224 | tf_op jit(solution)/shard_map/ppermute | solution.py:32
  35.3 5.3 %collective-permute-start.14 = (f32[96,256]{1,0:T(8,128)S(1)}, f32[96,256]{1,0:T(8,128)S(1)}, u32[]{:S(2)}, u32[]{:S(2)}) collective-permute-start(f32[96,256]{1,0:T(8,128)S(1)} %get-tuple-element.54), channel_id=1, source_target_pairs={{0,16},{16,32},{32,48},{48,64},{64,80},{80,96},{96,112},{112,0},{1... | collective-permute-start | bytes 294920 | tf_op jit(solution)/shard_map/ppermute | solution.py:32
  42.9 4.0 %collective-permute-start.15 = (f32[24,128]{1,0:T(8,128)S(1)}, f32[24,128]{1,0:T(8,128)S(1)}, u32[]{:S(2)}, u32[]{:S(2)}) collective-permute-start(f32[24,128]{1,0:T(8,128)S(1)} %shard_map.194), channel_id=1, source_target_pairs={{0,1},{1,0},{2,3},{3,2},{4,5},{5,4},{6,7},{7,6},{8,9},{9,8},{10,11... | collective-permute-start | bytes 36872 | tf_op jit(solution)/shard_map/ppermute | solution.py:602
  46.9 3.3 %collective-permute-start.22 = (f32[24,128]{1,0:T(8,128)S(1)}, f32[24,128]{1,0:T(8,128)S(1)}, u32[]{:S(2)}, u32[]{:S(2)}) collective-permute-start(f32[24,128]{1,0:T(8,128)S(1)} %add.52), channel_id=1, source_target_pairs={{3,5},{8,10},{19,21},{24,26},{35,37},{40,42},{51,53},{56,58},{67,6... | collective-permute-start | bytes 36872 | tf_op jit(solution)/shard_map/ppermute | solution.py:609
  47.6 9.8 %collective-permute-start.21 = (f32[24,128]{1,0:T(8,128)S(1)}, f32[24,128]{1,0:T(8,128)S(1)}, u32[]{:S(2)}, u32[]{:S(2)}) collective-permute-start(f32[24,128]{1,0:T(8,128)S(1)} %add.52), channel_id=1, source_target_pairs={{1,5},{6,10},{17,21},{22,26},{33,37},{38,42},{49,53},{54,58},{65,6... | collective-permute-start | bytes 36872 | tf_op jit(solution)/shard_map/ppermute | solution.py:609
  48.2 9.8 %collective-permute-start.20 = (f32[24,128]{1,0:T(8,128)S(1)}, f32[24,128]{1,0:T(8,128)S(1)}, u32[]{:S(2)}, u32[]{:S(2)}) collective-permute-start(f32[24,128]{1,0:T(8,128)S(1)} %add.52), channel_id=1, source_target_pairs={{15,5},{4,10},{31,21},{20,26},{47,37},{36,42},{63,53},{52,58},{79,... | collective-permute-start | bytes 36872 | tf_op jit(solution)/shard_map/ppermute | solution.py:609
  48.9 9.2 %collective-permute-start.19 = (f32[24,128]{1,0:T(8,128)S(1)}, f32[24,128]{1,0:T(8,128)S(1)}, u32[]{:S(2)}, u32[]{:S(2)}) collective-permute-start(f32[24,128]{1,0:T(8,128)S(1)} %add.52), channel_id=1, source_target_pairs={{13,5},{2,10},{29,21},{18,26},{45,37},{34,42},{61,53},{50,58},{77,... | collective-permute-start | bytes 36872 | tf_op jit(solution)/shard_map/ppermute | solution.py:609
  49.6 8.6 %collective-permute-start.18 = (f32[24,128]{1,0:T(8,128)S(1)}, f32[24,128]{1,0:T(8,128)S(1)}, u32[]{:S(2)}, u32[]{:S(2)}) collective-permute-start(f32[24,128]{1,0:T(8,128)S(1)} %add.52), channel_id=1, source_target_pairs={{11,5},{0,10},{27,21},{16,26},{43,37},{32,42},{59,53},{48,58},{75,... | collective-permute-start | bytes 36872 | tf_op jit(solution)/shard_map/ppermute | solution.py:609
  50.3 7.9 %collective-permute-start.17 = (f32[24,128]{1,0:T(8,128)S(1)}, f32[24,128]{1,0:T(8,128)S(1)}, u32[]{:S(2)}, u32[]{:S(2)}) collective-permute-start(f32[24,128]{1,0:T(8,128)S(1)} %add.52), channel_id=1, source_target_pairs={{9,5},{14,10},{25,21},{30,26},{41,37},{46,42},{57,53},{62,58},{73,... | collective-permute-start | bytes 36872 | tf_op jit(solution)/shard_map/ppermute | solution.py:609
  57.4 0.8 %collective-permute-start.16 = (f32[24,128]{1,0:T(8,128)S(1)}, f32[24,128]{1,0:T(8,128)S(1)}, u32[]{:S(2)}, u32[]{:S(2)}) collective-permute-start(f32[24,128]{1,0:T(8,128)S(1)} %add.52), channel_id=1, source_target_pairs={{7,5},{12,10},{23,21},{28,26},{39,37},{44,42},{55,53},{60,58},{71,... | collective-permute-start | bytes 36872 | tf_op jit(solution)/shard_map/ppermute | solution.py:609
  58.0 5.4 %collective-permute-start.24 = (f32[72,256]{1,0:T(8,128)S(1)}, f32[72,256]{1,0:T(8,128)S(1)}, u32[]{:S(2)}, u32[]{:S(2)}) collective-permute-start(f32[72,256]{1,0:T(8,128)S(1)} %shard_map.193), channel_id=1, source_target_pairs={{0,112},{16,0},{32,16},{48,32},{64,48},{80,64},{96,80},{112,96},{1... | collective-permute-start | bytes 221192 | tf_op jit(solution)/shard_map/ppermute | solution.py:32
  58.2 8.0 %collective-permute-start.23 = (f32[24,128]{1,0:T(8,128)S(1)}, f32[24,128]{1,0:T(8,128)S(1)}, u32[]{:S(2)}, u32[]{:S(2)}) collective-permute-start(f32[24,128]{1,0:T(8,128)S(1)} %add_add_fusion.rest), channel_id=1, source_target_pairs={{0,112},{16,0},{32,16},{48,32},{64,48},{80,64},{96,80},{112,96},{1... | collective-permute-start | bytes 36872 | tf_op jit(solution)/shard_map/ppermute | solution.py:32

commit v5 on v4

--- a/solution.py
+++ b/solution.py
@@ -484,7 +484,7 @@
     nx, nz, half = s.shape[1], 32, s.shape[3] // 2
     own = nz - RIM
     if last:
-        final, v_final, slip_out, mark, out, sem = refs
+        final, v_final, slip_final, mark, out, slip_out, sem = refs
         mark[...] = jnp.zeros_like(mark)
         copies.append(pltpu.make_async_copy(v.at[:, :, 0:own, :], v_final, sem.at[0]))
         copies[0].start()
@@ -516,6 +516,8 @@
         copies[-1].start()
         turned = jnp.concatenate([fresh, jnp.zeros((128 - nz, 128), F32)], axis=0).T
         slip_out[...] = turned[0:nx, 0:own]
+        copies.append(pltpu.make_async_copy(slip_out, slip_final, sem.at[len(copies)]))
+        copies[-1].start()
         for copy in copies:
             copy.wait()
     else:
@@ -726,8 +728,12 @@
         lambda *refs: fine_stress_kernel(2, *refs),
         out_shape=[jax.ShapeDtypeStruct(a.shape, F32) for a in (fine_stress, fine_velocity, fault_slip, raw[0:8])],
         in_specs=[VMEM] * 8,
-        out_specs=[pl.BlockSpec(memory_space=pl.ANY)] * 2 + [VMEM] * 2,
-        scratch_shapes=[pltpu.VMEM((6, nx, 32, ny), F32), pltpu.SemaphoreType.DMA((2 * nx + 2,))],
+        out_specs=[pl.BlockSpec(memory_space=pl.ANY)] * 3 + [VMEM],
+        scratch_shapes=[
+            pltpu.VMEM((6, nx, 32, ny), F32),
+            pltpu.VMEM(fault_slip.shape, F32),
+            pltpu.SemaphoreType.DMA((2 * nx + 3,)),
+        ],
         compiler_params=PARAMS,
     )(stress, velocity, fine_material, rim, xr, settings, slip, flags)
     coarse_next, coarse_stress_next = call(

time: 67.8 us -> 67.2 us (level)
  transfers between devices with their start and end apart: 25 -> 25, of which waited for: 8 -> 8; matrix products, arithmetic and copies ran while one was open for 0% -> 0% of each run, Pallas kernels for 12% -> 11%
where the time goes in v5:
time: 67.2 us; the launch traced here: 66.4 us
  starting transfers between devices  31.7 us (47%)
  waiting for transfers between devices  20.5 us (31%)
  Pallas kernels  13 us (19%)
  between operations  1.04 us (2%)
    ppermute x14, starting transfers between devices, apart(): lax.ppermute(value, 'gy', [pair if out else pair[::-1] for pair in pairs])  16.4 us
    ppermute x14, waiting for transfers between devices, apart(): lax.ppermute(value, 'gy', [pair if out else pair[::-1] for pair in pairs])  12.5 us
    ppermute x9, starting transfers between devices, ring(): lax.ppermute(value, axis, [(i, (i + steps) % count) for i in range(count)])  12.1 us
    pallas_call x13, Pallas kernels, call(): pl.pallas_call(kernel, out_shape=tuple((jax.ShapeDtypeStruct(shape, F32)...  7.55 us
    ppermute x9, waiting for transfers between devices, ring(): lax.ppermute(value, axis, [(i, (i + steps) % count) for i in range(count)])  6.08 us
    ppermute x2, starting transfers between devices, swap(): return lax.ppermute(value, axis, [(i, i ^ bit) for i in range(count)])  3.21 us
    pallas_call x1, Pallas kernels, body(): pl.pallas_call(pack_kernel, out_shape=[jax.ShapeDtypeStruct(shape, F32) f...  2.3 us
    pallas_call x1, Pallas kernels, body(): pl.pallas_call(lambda *refs: fine_stress_kernel(2, *refs), out_shape=[jax...  2.19 us
  transfers between devices with their start and end apart: 25, of which 8 were waited for; matrix products, arithmetic and copies ran while one was open for 0% of the time, Pallas kernels for 11%

profile of v5, /device:TPU:31, one launch (start us, length us, event | category | flops | bytes accessed | tf_op | source)
XLA Modules:
  0.0 66.4 jit_solution(2464138956779686764)
XLA Ops:
  0.8 2.3 %shard_map.182 = (f32[408,256]{1,0:T(8,128)S(1)}, f32[528,256]{1,0:T(8,128)S(1)}, f32[24,128]{1,0:T(8,128)S(1)}) custom-call(f32[3,12,24,256]{3,2,1,0:T(8,128)} %refs_0_.2, f32[6,12,24,256]{3,2,1,0:T(8,128)} %refs_0_.3, f32[3,12,24,256]{3,2,1,0:T(8,128)} %refs_2_.11, f32[6,4,16,128]{3,2,1,0:T(8,128)} %cs.5, f32[3,4,16,128]{3,2,1,0:T(8,128)} %cv.5, ...), custom_call_target="tpu_custom_call" | custom-call | tf_op jit(solution)/shard_map/pallas_call | solution.py:643
  3.1 0.7 %collective-permute-start.1 = (f32[528,256]{1,0:T(8,128)S(1)}, f32[528,256]{1,0:T(8,128)S(1)}, u32[]{:S(2)}, u32[]{:S(2)}) collective-permute-start(f32[528,256]{1,0:T(8,128)S(1)} %get-tuple-element.37), channel_id=1, source_target_pairs={{0,15},{1,0},{2,1},{3,2},{4,3},{5,4},{6,5},{7,6},{8,7},{9,8},{10,9... | collective-permute-start | bytes 1622024 | tf_op jit(solution)/shard_map/ppermute | solution.py:32
  3.9 1.6 %collective-permute-start = (f32[408,256]{1,0:T(8,128)S(1)}, f32[408,256]{1,0:T(8,128)S(1)}, u32[]{:S(2)}, u32[]{:S(2)}) collective-permute-start(f32[408,256]{1,0:T(8,128)S(1)} %get-tuple-element.36), channel_id=1, source_target_pairs={{0,1},{1,2},{2,3},{3,4},{4,5},{5,6},{6,7},{7,8},{8,9},{9,10},{10,1... | collective-permute-start | bytes 1253384 | tf_op jit(solution)/shard_map/ppermute | solution.py:32
  5.5 1.0 %shard_map.185 = f32[24,128]{1,0:T(8,128)S(1)} custom-call(f32[3,4,16,128]{3,2,1,0:T(8,128)} %cv.5, s32[2,4,128]{2,1,0:T(4,128)} %rows_ref.3, f32[8,256]{1,0:T(8,128)S(1)} %broadcast_in_dim.2._.flags.refs_7_, f32[24,128]{1,0:T(8,128)S(1)} %get-tuple-element.38.raw._), custom_call_target="tpu_custom_call" | custom-call | tf_op jit(solution)/shard_map/pallas_call | solution.py:658
  6.4 0.8 %collective-permute-start.9 = (f32[24,128]{1,0:T(8,128)S(1)}, f32[24,128]{1,0:T(8,128)S(1)}, u32[]{:S(2)}, u32[]{:S(2)}) collective-permute-start(f32[24,128]{1,0:T(8,128)S(1)} %shard_map.185), channel_id=1, source_target_pairs={{5,3},{10,8},{21,19},{26,24},{37,35},{42,40},{53,51},{58,56},{69,6... | collective-permute-start | bytes 36872 | tf_op jit(solution)/shard_map/ppermute | solution.py:611
  7.2 0.7 collective-permute-start.8
  7.9 0.7 collective-permute-start.7
  8.6 0.7 collective-permute-start.6
  9.3 0.7 collective-permute-start.5
  10.5 1.3 %collective-permute-start.4 = (f32[24,128]{1,0:T(8,128)S(1)}, f32[24,128]{1,0:T(8,128)S(1)}, u32[]{:S(2)}, u32[]{:S(2)}) collective-permute-start(f32[24,128]{1,0:T(8,128)S(1)} %shard_map.185), channel_id=1, source_target_pairs={{5,9},{10,14},{21,25},{26,30},{37,41},{42,46},{53,57},{58,62},{69,... | collective-permute-start | bytes 36872 | tf_op jit(solution)/shard_map/ppermute | solution.py:611
  11.7 0.7 %collective-permute-done.1.from_above.above = f32[528,256]{1,0:T(8,128)S(1)} collective-permute-done((f32[528,256]{1,0:T(8,128)S(1)}, f32[528,256]{1,0:T(8,128)S(1)}, u32[]{:S(2)}, u32[]{:S(2)}) %collective-permute-start.1) | collective-permute-done | bytes 540704 | tf_op jit(solution)/shard_map/ppermute | solution.py:32
  13.9 12.5 %collective-permute-done.4 = f32[24,128]{1,0:T(8,128)S(1)} collective-permute-done((f32[24,128]{1,0:T(8,128)S(1)}, f32[24,128]{1,0:T(8,128)S(1)}, u32[]{:S(2)}, u32[]{:S(2)}) %collective-permute-start.4) | collective-permute-done | bytes 12320 | tf_op jit(solution)/shard_map/ppermute | solution.py:611
  26.5 1.2 %collective-permute-done.10.bounds_b.refs_6_ = f32[24,128]{1,0:T(8,128)S(1)} collective-permute-done((f32[24,128]{1,0:T(8,128)S(1)}, f32[24,128]{1,0:T(8,128)S(1)}, u32[]{:S(2)}, u32[]{:S(2)}) %collective-permute-start.10) | collective-permute-done | bytes 12320 | tf_op jit(solution)/shard_map/ppermute | solution.py:604
  28.0 3.6 %collective-permute-start.12 = (f32[96,256]{1,0:T(8,128)S(1)}, f32[96,256]{1,0:T(8,128)S(1)}, u32[]{:S(2)}, u32[]{:S(2)}) collective-permute-start(f32[96,256]{1,0:T(8,128)S(1)} %get-tuple-element.46), channel_id=1, source_target_pairs={{0,16},{16,32},{32,48},{48,64},{64,80},{80,96},{96,112},{112,0},{1... | collective-permute-start | bytes 294920 | tf_op jit(solution)/shard_map/ppermute | solution.py:32
  31.7 0.8 %shard_map.186.v.refs_0_.refs_1_ = f32[3,12,32,256]{3,2,1,0:T(8,128)S(1)} custom-call(f32[3,12,24,256]{3,2,1,0:T(8,128)S(1)} %copy-done.2, f32[6,12,24,256]{3,2,1,0:T(8,128)S(1)} %copy-done.1, f32[3,12,24,256]{3,2,1,0:T(8,128)S(1)} %copy-done, f32[12,12,8,256]{3,2,1,0:T(8,128)S(1)} %get-tuple-element.43.rim.refs_3_, ...), custom_call_target="tpu_custom_call" | custom-call | tf_op jit(solution)/shard_map/pallas_call | solution.py:21
  32.5 1.8 %collective-permute-done.11.xr.refs_4_ = f32[96,256]{1,0:T(8,128)S(1)} collective-permute-done((f32[96,256]{1,0:T(8,128)S(1)}, f32[96,256]{1,0:T(8,128)S(1)}, u32[]{:S(2)}, u32[]{:S(2)}) %collective-permute-start.11) | collective-permute-done | bytes 98336 | tf_op jit(solution)/shard_map/ppermute | solution.py:32
  35.3 3.4 %collective-permute-start.14 = (f32[96,256]{1,0:T(8,128)S(1)}, f32[96,256]{1,0:T(8,128)S(1)}, u32[]{:S(2)}, u32[]{:S(2)}) collective-permute-start(f32[96,256]{1,0:T(8,128)S(1)} %get-tuple-element.54), channel_id=1, source_target_pairs={{0,16},{16,32},{32,48},{48,64},{64,80},{80,96},{96,112},{112,0},{1... | collective-permute-start | bytes 294920 | tf_op jit(solution)/shard_map/ppermute | solution.py:32
  38.6 1.1 %shard_map.190 = (f32[6,12,32,256]{3,2,1,0:T(8,128)S(1)}, f32[32,128]{1,0:T(8,128)S(1)}) custom-call(f32[6,12,24,256]{3,2,1,0:T(8,128)S(1)} %copy-done.1, f32[3,12,32,256]{3,2,1,0:T(8,128)S(1)} %shard_map.186.v.refs_0_.refs_1_, f32[3,12,24,256]{3,2,1,0:T(8,128)S(1)} %copy-done, f32[12,12,8,256]{3,2,1,0:T(8,128)S(1)} %get-tuple-element.43.rim.refs_3_, ...), custom_call_target="tpu_custom_call" | custom-call | tf_op jit(solution)/shard_map/pallas_call | solution.py:21
  39.8 0.8 %shard_map.191.refs_1_.refs_0_.v = f32[3,12,32,256]{3,2,1,0:T(8,128)S(1)} custom-call(f32[3,12,32,256]{3,2,1,0:T(8,128)S(1)} %shard_map.186.v.refs_0_.refs_1_, f32[6,12,32,256]{3,2,1,0:T(8,128)S(1)} %get-tuple-element.52.s.refs_0_, f32[3,12,24,256]{3,2,1,0:T(8,128)S(1)} %copy-done, f32[12,12,8,256]{3,2,1,0:T(8,128)S(1)} %get-tuple-element.43.rim.refs_3_, ...), custom_call_target="tpu_custom_call" | custom-call | tf_op jit(solution)/shard_map/pallas_call | solution.py:21
  41.1 1.3 %shard_map.192 = (f32[6,12,32,256]{3,2,1,0:T(8,128)S(1)}, f32[32,128]{1,0:T(8,128)S(1)}, f32[96,256]{1,0:T(8,128)S(1)}) custom-call(f32[6,12,32,256]{3,2,1,0:T(8,128)S(1)} %get-tuple-element.52.s.refs_0_, f32[3,12,32,256]{3,2,1,0:T(8,128)S(1)} %shard_map.191.refs_1_.refs_0_.v, f32[3,12,24,256]{3,2,1,0:T(8,128)S(1)} %copy-done, ...), custom_call_target="tpu_custom_call" | custom-call | tf_op jit(solution)/shard_map/pallas_call | solution.py:21
  42.9 3.1 %collective-permute-start.15 = (f32[24,128]{1,0:T(8,128)S(1)}, f32[24,128]{1,0:T(8,128)S(1)}, u32[]{:S(2)}, u32[]{:S(2)}) collective-permute-start(f32[24,128]{1,0:T(8,128)S(1)} %shard_map.194), channel_id=1, source_target_pairs={{0,1},{1,0},{2,3},{3,2},{4,5},{5,4},{6,7},{7,6},{8,9},{9,8},{10,11... | collective-permute-start | bytes 36872 | tf_op jit(solution)/shard_map/ppermute | solution.py:604
  46.2 0.7 %collective-permute-done.15 = f32[24,128]{1,0:T(8,128)S(1)} collective-permute-done((f32[24,128]{1,0:T(8,128)S(1)}, f32[24,128]{1,0:T(8,128)S(1)}, u32[]{:S(2)}, u32[]{:S(2)}) %collective-permute-start.15) | collective-permute-done | bytes 12320 | tf_op jit(solution)/shard_map/ppermute | solution.py:604
  47.6 0.7 collective-permute-start.21
  48.2 0.7 collective-permute-start.20
  48.9 0.7 collective-permute-start.19
  50.3 7.1 %collective-permute-start.17 = (f32[24,128]{1,0:T(8,128)S(1)}, f32[24,128]{1,0:T(8,128)S(1)}, u32[]{:S(2)}, u32[]{:S(2)}) collective-permute-start(f32[24,128]{1,0:T(8,128)S(1)} %add.52), channel_id=1, source_target_pairs={{9,5},{14,10},{25,21},{30,26},{41,37},{46,42},{57,53},{62,58},{73,... | collective-permute-start | bytes 36872 | tf_op jit(solution)/shard_map/ppermute | solution.py:611
  57.4 0.7 collective-permute-start.16
  58.2 1.9 %collective-permute-start.23 = (f32[24,128]{1,0:T(8,128)S(1)}, f32[24,128]{1,0:T(8,128)S(1)}, u32[]{:S(2)}, u32[]{:S(2)}) collective-permute-start(f32[24,128]{1,0:T(8,128)S(1)} %add_add_fusion.rest), channel_id=1, source_target_pairs={{0,112},{16,0},{32,16},{48,32},{64,48},{80,64},{96,80},{112,96},{1... | collective-permute-start | bytes 36872 | tf_op jit(solution)/shard_map/ppermute | solution.py:32
  60.1 0.8 %shard_map.195.refs_1_ = f32[3,12,32,256]{3,2,1,0:T(8,128)S(1)} custom-call(f32[3,12,32,256]{3,2,1,0:T(8,128)S(1)} %shard_map.191.refs_1_.refs_0_.v, f32[6,12,32,256]{3,2,1,0:T(8,128)S(1)} %get-tuple-element.56.refs_1_.s.refs_0_, f32[3,12,24,256]{3,2,1,0:T(8,128)S(1)} %copy-done, f32[12,12,8,256]{3,2,1,0:T(8,128)S(1)} %get-tuple-element.43.rim.refs_3_, ...), custom_call_target="tpu_custom_call" | custom-call | tf_op jit(solution)/shard_map/pallas_call | solution.py:21
  60.9 2.5 %collective-permute-done.24.refs_4_ = f32[72,256]{1,0:T(8,128)S(1)} collective-permute-done((f32[72,256]{1,0:T(8,128)S(1)}, f32[72,256]{1,0:T(8,128)S(1)}, u32[]{:S(2)}, u32[]{:S(2)}) %collective-permute-start.24) | collective-permute-done | bytes 73760 | tf_op jit(solution)/shard_map/ppermute | solution.py:32
  63.4 2.2 %shard_map.196 = (f32[6,12,24,256]{3,2,1,0:T(8,128)}, f32[3,12,24,256]{3,2,1,0:T(8,128)}, f32[12,24]{1,0:T(8,128)}, f32[8,128]{1,0:T(8,128)S(1)}) custom-call(f32[6,12,32,256]{3,2,1,0:T(8,128)S(1)} %get-tuple-element.56.refs_1_.s.refs_0_, f32[3,12,32,256]{3,2,1,0:T(8,128)S(1)} %shard_map.195.refs_1_, f32[3,12,24,256]{3,2,1,0:T(8,128)S(1)} %copy-done, ...), custom_call_target="tpu_custom_call" | custom-call | tf_op jit(solution)/shard_map/pallas_call | solution.py:727
  65.6 0.8 %shard_map.197 = (f32[3,4,16,128]{3,2,1,0:T(8,128)}, f32[6,4,16,128]{3,2,1,0:T(8,128)}) custom-call(f32[3,4,16,128]{3,2,1,0:T(8,128)S(1)} %get-tuple-element.40.cv, f32[6,4,16,128]{3,2,1,0:T(8,128)S(1)} %get-tuple-element.41.cs, f32[3,4,16,128]{3,2,1,0:T(8,128)S(1)} %get-tuple-element.42.cm, f32[128,256]{1,0:T(8,128)S(1)} %collective-permute-done.13.refs_4_.xr, ...), custom_call_target="tpu_custom_call" | custom-call | tf_op jit(solution)/shard_map/pallas_call | solution.py:21
  (54 shorter events, 6.2 us)
Async XLA Ops:
  0.8 12.3 %copy-start = (f32[3,12,24,256]{3,2,1,0:T(8,128)S(1)}, f32[3,12,24,256]{3,2,1,0:T(8,128)}, u32[]{:S(2)}) copy-start(f32[3,12,24,256]{3,2,1,0:T(8,128)} %refs_2_.11) | copy-start | bytes 2654212
  0.8 12.3 %copy-start.1 = (f32[6,12,24,256]{3,2,1,0:T(8,128)S(1)}, f32[6,12,24,256]{3,2,1,0:T(8,128)}, u32[]{:S(2)}) copy-start(f32[6,12,24,256]{3,2,1,0:T(8,128)} %refs_0_.3) | copy-start | bytes 5308420
  0.8 12.3 %copy-start.3 = (f32[6,4,16,128]{3,2,1,0:T(8,128)S(1)}, f32[6,4,16,128]{3,2,1,0:T(8,128)}, u32[]{:S(2)}) copy-start(f32[6,4,16,128]{3,2,1,0:T(8,128)} %cs.5) | copy-start | bytes 589828
  3.1 9.3 %collective-permute-start.1 = (f32[528,256]{1,0:T(8,128)S(1)}, f32[528,256]{1,0:T(8,128)S(1)}, u32[]{:S(2)}, u32[]{:S(2)}) collective-permute-start(f32[528,256]{1,0:T(8,128)S(1)} %get-tuple-element.37), channel_id=1, source_target_pairs={{0,15},{1,0},{2,1},{3,2},{4,3},{5,4},{6,5},{7,6},{8,7},{9,8},{10,9... | collective-permute-start | bytes 1622024 | tf_op jit(solution)/shard_map/ppermute | solution.py:32
  3.9 6.6 %collective-permute-start = (f32[408,256]{1,0:T(8,128)S(1)}, f32[408,256]{1,0:T(8,128)S(1)}, u32[]{:S(2)}, u32[]{:S(2)}) collective-permute-start(f32[408,256]{1,0:T(8,128)S(1)} %get-tuple-element.36), channel_id=1, source_target_pairs={{0,1},{1,2},{2,3},{3,4},{4,5},{5,6},{6,7},{7,8},{8,9},{9,10},{10,1... | collective-permute-start | bytes 1253384 | tf_op jit(solution)/shard_map/ppermute | solution.py:32
  6.4 21.2 %copy-start.2 = (f32[3,12,24,256]{3,2,1,0:T(8,128)S(1)}, f32[3,12,24,256]{3,2,1,0:T(8,128)}, u32[]{:S(2)}) copy-start(f32[3,12,24,256]{3,2,1,0:T(8,128)} %refs_0_.2) | copy-start | bytes 2654212
  6.4 2.1 %collective-permute-start.9 = (f32[24,128]{1,0:T(8,128)S(1)}, f32[24,128]{1,0:T(8,128)S(1)}, u32[]{:S(2)}, u32[]{:S(2)}) collective-permute-start(f32[24,128]{1,0:T(8,128)S(1)} %shard_map.185), channel_id=1, source_target_pairs={{5,3},{10,8},{21,19},{26,24},{37,35},{42,40},{53,51},{58,56},{69,6... | collective-permute-start | bytes 36872 | tf_op jit(solution)/shard_map/ppermute | solution.py:611
  7.2 2.0 %collective-permute-start.8 = (f32[24,128]{1,0:T(8,128)S(1)}, f32[24,128]{1,0:T(8,128)S(1)}, u32[]{:S(2)}, u32[]{:S(2)}) collective-permute-start(f32[24,128]{1,0:T(8,128)S(1)} %shard_map.185), channel_id=1, source_target_pairs={{5,1},{10,6},{21,17},{26,22},{37,33},{42,38},{53,49},{58,54},{69,6... | collective-permute-start | bytes 36872 | tf_op jit(solution)/shard_map/ppermute | solution.py:611
  7.9 5.5 %collective-permute-start.7 = (f32[24,128]{1,0:T(8,128)S(1)}, f32[24,128]{1,0:T(8,128)S(1)}, u32[]{:S(2)}, u32[]{:S(2)}) collective-permute-start(f32[24,128]{1,0:T(8,128)S(1)} %shard_map.185), channel_id=1, source_target_pairs={{5,15},{10,4},{21,31},{26,20},{37,47},{42,36},{53,63},{58,52},{69,... | collective-permute-start | bytes 36872 | tf_op jit(solution)/shard_map/ppermute | solution.py:611
  8.6 5.3 %collective-permute-start.6 = (f32[24,128]{1,0:T(8,128)S(1)}, f32[24,128]{1,0:T(8,128)S(1)}, u32[]{:S(2)}, u32[]{:S(2)}) collective-permute-start(f32[24,128]{1,0:T(8,128)S(1)} %shard_map.185), channel_id=1, source_target_pairs={{5,13},{10,2},{21,29},{26,18},{37,45},{42,34},{53,61},{58,50},{69,... | collective-permute-start | bytes 36872 | tf_op jit(solution)/shard_map/ppermute | solution.py:611
  9.3 4.6 %collective-permute-start.5 = (f32[24,128]{1,0:T(8,128)S(1)}, f32[24,128]{1,0:T(8,128)S(1)}, u32[]{:S(2)}, u32[]{:S(2)}) collective-permute-start(f32[24,128]{1,0:T(8,128)S(1)} %shard_map.185), channel_id=1, source_target_pairs={{5,11},{10,0},{21,27},{26,16},{37,43},{42,32},{53,59},{58,48},{69,... | collective-permute-start | bytes 36872 | tf_op jit(solution)/shard_map/ppermute | solution.py:611
  10.5 15.9 %collective-permute-start.4 = (f32[24,128]{1,0:T(8,128)S(1)}, f32[24,128]{1,0:T(8,128)S(1)}, u32[]{:S(2)}, u32[]{:S(2)}) collective-permute-start(f32[24,128]{1,0:T(8,128)S(1)} %shard_map.185), channel_id=1, source_target_pairs={{5,9},{10,14},{21,25},{26,30},{37,41},{42,46},{53,57},{58,62},{69,... | collective-permute-start | bytes 36872 | tf_op jit(solution)/shard_map/ppermute | solution.py:611
  12.4 14.0 %collective-permute-start.3 = (f32[24,128]{1,0:T(8,128)S(1)}, f32[24,128]{1,0:T(8,128)S(1)}, u32[]{:S(2)}, u32[]{:S(2)}) collective-permute-start(f32[24,128]{1,0:T(8,128)S(1)} %shard_map.185), channel_id=1, source_target_pairs={{5,7},{10,12},{21,23},{26,28},{37,39},{42,44},{53,55},{58,60},{69,... | collective-permute-start | bytes 36872 | tf_op jit(solution)/shard_map/ppermute | solution.py:611
  13.4 14.2 %collective-permute-start.2 = (f32[208,256]{1,0:T(8,128)S(1)}, f32[208,256]{1,0:T(8,128)S(1)}, u32[]{:S(2)}, u32[]{:S(2)}) collective-permute-start(f32[208,256]{1,0:T(8,128)S(1)} %get-tuple-element.39), channel_id=1, source_target_pairs={{0,16},{16,32},{32,48},{48,64},{64,80},{80,96},{96,112},{112,0},{1... | collective-permute-start | bytes 638984 | tf_op jit(solution)/shard_map/ppermute | solution.py:32
  26.4 1.3 %collective-permute-start.10 = (f32[24,128]{1,0:T(8,128)S(1)}, f32[24,128]{1,0:T(8,128)S(1)}, u32[]{:S(2)}, u32[]{:S(2)}) collective-permute-start(f32[24,128]{1,0:T(8,128)S(1)} %add_add_fusion.1.bounds_a.refs_5_), channel_id=1, source_target_pairs={{0,1},{1,0},{2,3},{3,2},{4,5},{5,4},{6,7},{7,6},{8,9},{9,8},{10,11... | collective-permute-start | bytes 36872 | tf_op jit(solution)/shard_map/ppermute | solution.py:604
  27.7 3.9 %copy-start.4 = (f32[3,4,16,128]{3,2,1,0:T(8,128)S(1)}, f32[3,4,16,128]{3,2,1,0:T(8,128)}, u32[]{:S(2)}) copy-start(f32[3,4,16,128]{3,2,1,0:T(8,128)} %cv.5) | copy-start | bytes 294916
  27.7 3.9 %copy-start.5 = (f32[3,4,16,128]{3,2,1,0:T(8,128)S(1)}, f32[3,4,16,128]{3,2,1,0:T(8,128)}, u32[]{:S(2)}) copy-start(f32[3,4,16,128]{3,2,1,0:T(8,128)} %cm.3) | copy-start | bytes 294916
  27.7 3.9 %copy-start.6 = (s32[2,4,128]{2,1,0:T(4,128)S(1)}, s32[2,4,128]{2,1,0:T(4,128)}, u32[]{:S(2)}) copy-start(s32[2,4,128]{2,1,0:T(4,128)} %rows_ref.3) | copy-start | bytes 12292
  27.9 6.4 %collective-permute-start.11 = (f32[96,256]{1,0:T(8,128)S(1)}, f32[96,256]{1,0:T(8,128)S(1)}, u32[]{:S(2)}, u32[]{:S(2)}) collective-permute-start(f32[96,256]{1,0:T(8,128)S(1)} %get-tuple-element.44), channel_id=1, source_target_pairs={{0,112},{16,0},{32,16},{48,32},{64,48},{80,64},{96,80},{112,96},{1... | collective-permute-start | bytes 294920 | tf_op jit(solution)/shard_map/ppermute | solution.py:32
  28.0 6.3 %collective-permute-start.12 = (f32[96,256]{1,0:T(8,128)S(1)}, f32[96,256]{1,0:T(8,128)S(1)}, u32[]{:S(2)}, u32[]{:S(2)}) collective-permute-start(f32[96,256]{1,0:T(8,128)S(1)} %get-tuple-element.46), channel_id=1, source_target_pairs={{0,16},{16,32},{32,48},{48,64},{64,80},{80,96},{96,112},{112,0},{1... | collective-permute-start | bytes 294920 | tf_op jit(solution)/shard_map/ppermute | solution.py:32
  35.0 6.1 %collective-permute-start.13 = (f32[128,256]{1,0:T(8,128)S(1)}, f32[128,256]{1,0:T(8,128)S(1)}, u32[]{:S(2)}, u32[]{:S(2)}) collective-permute-start(f32[128,256]{1,0:T(8,128)S(1)} %get-tuple-element.50), channel_id=1, source_target_pairs={{0,112},{16,0},{32,16},{48,32},{64,48},{80,64},{96,80},{112,96},{1... | collective-permute-start | bytes 393224 | tf_op jit(solution)/shard_map/ppermute | solution.py:32
  35.3 5.3 %collective-permute-start.14 = (f32[96,256]{1,0:T(8,128)S(1)}, f32[96,256]{1,0:T(8,128)S(1)}, u32[]{:S(2)}, u32[]{:S(2)}) collective-permute-start(f32[96,256]{1,0:T(8,128)S(1)} %get-tuple-element.54), channel_id=1, source_target_pairs={{0,16},{16,32},{32,48},{48,64},{64,80},{80,96},{96,112},{112,0},{1... | collective-permute-start | bytes 294920 | tf_op jit(solution)/shard_map/ppermute | solution.py:32
  42.9 4.0 %collective-permute-start.15 = (f32[24,128]{1,0:T(8,128)S(1)}, f32[24,128]{1,0:T(8,128)S(1)}, u32[]{:S(2)}, u32[]{:S(2)}) collective-permute-start(f32[24,128]{1,0:T(8,128)S(1)} %shard_map.194), channel_id=1, source_target_pairs={{0,1},{1,0},{2,3},{3,2},{4,5},{5,4},{6,7},{7,6},{8,9},{9,8},{10,11... | collective-permute-start | bytes 36872 | tf_op jit(solution)/shard_map/ppermute | solution.py:604
  46.9 3.3 %collective-permute-start.22 = (f32[24,128]{1,0:T(8,128)S(1)}, f32[24,128]{1,0:T(8,128)S(1)}, u32[]{:S(2)}, u32[]{:S(2)}) collective-permute-start(f32[24,128]{1,0:T(8,128)S(1)} %add.52), channel_id=1, source_target_pairs={{3,5},{8,10},{19,21},{24,26},{35,37},{40,42},{51,53},{56,58},{67,6... | collective-permute-start | bytes 36872 | tf_op jit(solution)/shard_map/ppermute | solution.py:611
  47.6 9.8 %collective-permute-start.21 = (f32[24,128]{1,0:T(8,128)S(1)}, f32[24,128]{1,0:T(8,128)S(1)}, u32[]{:S(2)}, u32[]{:S(2)}) collective-permute-start(f32[24,128]{1,0:T(8,128)S(1)} %add.52), channel_id=1, source_target_pairs={{1,5},{6,10},{17,21},{22,26},{33,37},{38,42},{49,53},{54,58},{65,6... | collective-permute-start | bytes 36872 | tf_op jit(solution)/shard_map/ppermute | solution.py:611
  48.2 9.8 %collective-permute-start.20 = (f32[24,128]{1,0:T(8,128)S(1)}, f32[24,128]{1,0:T(8,128)S(1)}, u32[]{:S(2)}, u32[]{:S(2)}) collective-permute-start(f32[24,128]{1,0:T(8,128)S(1)} %add.52), channel_id=1, source_target_pairs={{15,5},{4,10},{31,21},{20,26},{47,37},{36,42},{63,53},{52,58},{79,... | collective-permute-start | bytes 36872 | tf_op jit(solution)/shard_map/ppermute | solution.py:611
  48.9 9.2 %collective-permute-start.19 = (f32[24,128]{1,0:T(8,128)S(1)}, f32[24,128]{1,0:T(8,128)S(1)}, u32[]{:S(2)}, u32[]{:S(2)}) collective-permute-start(f32[24,128]{1,0:T(8,128)S(1)} %add.52), channel_id=1, source_target_pairs={{13,5},{2,10},{29,21},{18,26},{45,37},{34,42},{61,53},{50,58},{77,... | collective-permute-start | bytes 36872 | tf_op jit(solution)/shard_map/ppermute | solution.py:611
  49.6 8.6 %collective-permute-start.18 = (f32[24,128]{1,0:T(8,128)S(1)}, f32[24,128]{1,0:T(8,128)S(1)}, u32[]{:S(2)}, u32[]{:S(2)}) collective-permute-start(f32[24,128]{1,0:T(8,128)S(1)} %add.52), channel_id=1, source_target_pairs={{11,5},{0,10},{27,21},{16,26},{43,37},{32,42},{59,53},{48,58},{75,... | collective-permute-start | bytes 36872 | tf_op jit(solution)/shard_map/ppermute | solution.py:611
  50.3 7.9 %collective-permute-start.17 = (f32[24,128]{1,0:T(8,128)S(1)}, f32[24,128]{1,0:T(8,128)S(1)}, u32[]{:S(2)}, u32[]{:S(2)}) collective-permute-start(f32[24,128]{1,0:T(8,128)S(1)} %add.52), channel_id=1, source_target_pairs={{9,5},{14,10},{25,21},{30,26},{41,37},{46,42},{57,53},{62,58},{73,... | collective-permute-start | bytes 36872 | tf_op jit(solution)/shard_map/ppermute | solution.py:611
  57.4 0.8 %collective-permute-start.16 = (f32[24,128]{1,0:T(8,128)S(1)}, f32[24,128]{1,0:T(8,128)S(1)}, u32[]{:S(2)}, u32[]{:S(2)}) collective-permute-start(f32[24,128]{1,0:T(8,128)S(1)} %add.52), channel_id=1, source_target_pairs={{7,5},{12,10},{23,21},{28,26},{39,37},{44,42},{55,53},{60,58},{71,... | collective-permute-start | bytes 36872 | tf_op jit(solution)/shard_map/ppermute | solution.py:611
  58.0 5.4 %collective-permute-start.24 = (f32[72,256]{1,0:T(8,128)S(1)}, f32[72,256]{1,0:T(8,128)S(1)}, u32[]{:S(2)}, u32[]{:S(2)}) collective-permute-start(f32[72,256]{1,0:T(8,128)S(1)} %shard_map.193), channel_id=1, source_target_pairs={{0,112},{16,0},{32,16},{48,32},{64,48},{80,64},{96,80},{112,96},{1... | collective-permute-start | bytes 221192 | tf_op jit(solution)/shard_map/ppermute | solution.py:32
  58.2 7.4 %collective-permute-start.23 = (f32[24,128]{1,0:T(8,128)S(1)}, f32[24,128]{1,0:T(8,128)S(1)}, u32[]{:S(2)}, u32[]{:S(2)}) collective-permute-start(f32[24,128]{1,0:T(8,128)S(1)} %add_add_fusion.rest), channel_id=1, source_target_pairs={{0,112},{16,0},{32,16},{48,32},{64,48},{80,64},{96,80},{112,96},{1... | collective-permute-start | bytes 36872 | tf_op jit(solution)/shard_map/ppermute | solution.py:32

commit v6 on v5

--- a/solution.py
+++ b/solution.py
@@ -696,8 +696,6 @@
             [VMEM] * (8 + len(to_send) * (step < 2)), *near, *(to_send if step < 2 else ()),
         )
         sends = list(sends)
-        if step == 2:
-            sends[0], *to_send = lax.optimization_barrier((sends[0], *to_send))
         moved = [ring(send, "gx", way) for send, way in zip(sends, (-1, 1))]
         (new,) = call(fine_velocity_kernel, [(3, nx, 32, ny)], [VMEM] * 8, *args)
         return (new, moved, *to_send) if step == 2 else (new, moved)
@@ -721,6 +719,7 @@
     (share,) = call(share_kernel, [shares], [VMEM] * 7, velocity, stress, fine_material, behind, *bounds, flags)
     share = share + swap(share, "gy", 1)
     velocity, (xr,), share = velocity_half(2, behind, share)
+    share, velocity = lax.optimization_barrier((share, velocity))
     parts = apart(share, False)
     restricted = share + sum(parts[1:], parts[0])
     restricted_next = ring(restricted, "gx", -1)

time: 67.2 us -> 67 us (level)
    ppermute x9, waiting for transfers between devices: 6.08 us -> 6.85 us  [ring(): lax.ppermute(value, axis, [(i, (i + steps) % count) for i in range(count)])]
where the time goes in v6:
time: 67 us; the launch traced here: 66.6 us
  starting transfers between devices  31.7 us (47%)
  waiting for transfers between devices  20.6 us (31%)
  Pallas kernels  13 us (19%)
  between operations  1.06 us (2%)
    ppermute x14, starting transfers between devices, apart(): lax.ppermute(value, 'gy', [pair if out else pair[::-1] for pair in pairs])  16.4 us
    ppermute x14, waiting for transfers between devices, apart(): lax.ppermute(value, 'gy', [pair if out else pair[::-1] for pair in pairs])  12.5 us
    ppermute x9, starting transfers between devices, ring(): lax.ppermute(value, axis, [(i, (i + steps) % count) for i in range(count)])  12.1 us
    pallas_call x13, Pallas kernels, call(): pl.pallas_call(kernel, out_shape=tuple((jax.ShapeDtypeStruct(shape, F32)...  7.55 us
    ppermute x9, waiting for transfers between devices, ring(): lax.ppermute(value, axis, [(i, (i + steps) % count) for i in range(count)])  6.85 us
    ppermute x2, starting transfers between devices, swap(): return lax.ppermute(value, axis, [(i, i ^ bit) for i in range(count)])  3.21 us
    pallas_call x1, Pallas kernels, body(): pl.pallas_call(pack_kernel, out_shape=[jax.ShapeDtypeStruct(shape, F32) f...  2.3 us
    pallas_call x1, Pallas kernels, body(): pl.pallas_call(lambda *refs: fine_stress_kernel(2, *refs), out_shape=[jax...  2.21 us
  transfers between devices with their start and end apart: 25, of which 8 were waited for; matrix products, arithmetic and copies ran while one was open for 0% of the time, Pallas kernels for 11%

profile of v6, /device:TPU:31, one launch (start us, length us, event | category | flops | bytes accessed | tf_op | source)
XLA Modules:
  0.0 66.6 jit_solution(5619760405182213259)
XLA Ops:
  0.8 2.3 %shard_map.182 = (f32[408,256]{1,0:T(8,128)S(1)}, f32[528,256]{1,0:T(8,128)S(1)}, f32[24,128]{1,0:T(8,128)S(1)}) custom-call(f32[3,12,24,256]{3,2,1,0:T(8,128)} %refs_0_.2, f32[6,12,24,256]{3,2,1,0:T(8,128)} %refs_0_.3, f32[3,12,24,256]{3,2,1,0:T(8,128)} %refs_2_.11, f32[6,4,16,128]{3,2,1,0:T(8,128)} %cs.5, f32[3,4,16,128]{3,2,1,0:T(8,128)} %cv.5, ...), custom_call_target="tpu_custom_call" | custom-call | tf_op jit(solution)/shard_map/pallas_call | solution.py:643
  3.1 0.7 %collective-permute-start.1 = (f32[528,256]{1,0:T(8,128)S(1)}, f32[528,256]{1,0:T(8,128)S(1)}, u32[]{:S(2)}, u32[]{:S(2)}) collective-permute-start(f32[528,256]{1,0:T(8,128)S(1)} %get-tuple-element.37), channel_id=1, source_target_pairs={{0,15},{1,0},{2,1},{3,2},{4,3},{5,4},{6,5},{7,6},{8,7},{9,8},{10,9... | collective-permute-start | bytes 1622024 | tf_op jit(solution)/shard_map/ppermute | solution.py:32
  3.9 1.6 %collective-permute-start = (f32[408,256]{1,0:T(8,128)S(1)}, f32[408,256]{1,0:T(8,128)S(1)}, u32[]{:S(2)}, u32[]{:S(2)}) collective-permute-start(f32[408,256]{1,0:T(8,128)S(1)} %get-tuple-element.36), channel_id=1, source_target_pairs={{0,1},{1,2},{2,3},{3,4},{4,5},{5,6},{6,7},{7,8},{8,9},{9,10},{10,1... | collective-permute-start | bytes 1253384 | tf_op jit(solution)/shard_map/ppermute | solution.py:32
  5.5 1.0 %shard_map.185 = f32[24,128]{1,0:T(8,128)S(1)} custom-call(f32[3,4,16,128]{3,2,1,0:T(8,128)} %cv.5, s32[2,4,128]{2,1,0:T(4,128)} %rows_ref.3, f32[8,256]{1,0:T(8,128)S(1)} %broadcast_in_dim.2._.flags.refs_7_, f32[24,128]{1,0:T(8,128)S(1)} %get-tuple-element.38.raw._), custom_call_target="tpu_custom_call" | custom-call | tf_op jit(solution)/shard_map/pallas_call | solution.py:658
  6.4 0.8 %collective-permute-start.9 = (f32[24,128]{1,0:T(8,128)S(1)}, f32[24,128]{1,0:T(8,128)S(1)}, u32[]{:S(2)}, u32[]{:S(2)}) collective-permute-start(f32[24,128]{1,0:T(8,128)S(1)} %shard_map.185), channel_id=1, source_target_pairs={{5,3},{10,8},{21,19},{26,24},{37,35},{42,40},{53,51},{58,56},{69,6... | collective-permute-start | bytes 36872 | tf_op jit(solution)/shard_map/ppermute | solution.py:611
  7.2 0.7 collective-permute-start.8
  7.9 0.7 collective-permute-start.7
  8.6 0.7 collective-permute-start.6
  9.3 0.7 collective-permute-start.5
  10.5 1.3 %collective-permute-start.4 = (f32[24,128]{1,0:T(8,128)S(1)}, f32[24,128]{1,0:T(8,128)S(1)}, u32[]{:S(2)}, u32[]{:S(2)}) collective-permute-start(f32[24,128]{1,0:T(8,128)S(1)} %shard_map.185), channel_id=1, source_target_pairs={{5,9},{10,14},{21,25},{26,30},{37,41},{42,46},{53,57},{58,62},{69,... | collective-permute-start | bytes 36872 | tf_op jit(solution)/shard_map/ppermute | solution.py:611
  11.7 0.7 %collective-permute-done.1.from_above.above = f32[528,256]{1,0:T(8,128)S(1)} collective-permute-done((f32[528,256]{1,0:T(8,128)S(1)}, f32[528,256]{1,0:T(8,128)S(1)}, u32[]{:S(2)}, u32[]{:S(2)}) %collective-permute-start.1) | collective-permute-done | bytes 540704 | tf_op jit(solution)/shard_map/ppermute | solution.py:32
  13.9 12.5 %collective-permute-done.4 = f32[24,128]{1,0:T(8,128)S(1)} collective-permute-done((f32[24,128]{1,0:T(8,128)S(1)}, f32[24,128]{1,0:T(8,128)S(1)}, u32[]{:S(2)}, u32[]{:S(2)}) %collective-permute-start.4) | collective-permute-done | bytes 12320 | tf_op jit(solution)/shard_map/ppermute | solution.py:611
  26.5 1.2 %collective-permute-done.10.bounds_b.refs_6_ = f32[24,128]{1,0:T(8,128)S(1)} collective-permute-done((f32[24,128]{1,0:T(8,128)S(1)}, f32[24,128]{1,0:T(8,128)S(1)}, u32[]{:S(2)}, u32[]{:S(2)}) %collective-permute-start.10) | collective-permute-done | bytes 12320 | tf_op jit(solution)/shard_map/ppermute | solution.py:604
  28.0 3.6 %collective-permute-start.12 = (f32[96,256]{1,0:T(8,128)S(1)}, f32[96,256]{1,0:T(8,128)S(1)}, u32[]{:S(2)}, u32[]{:S(2)}) collective-permute-start(f32[96,256]{1,0:T(8,128)S(1)} %get-tuple-element.46), channel_id=1, source_target_pairs={{0,16},{16,32},{32,48},{48,64},{64,80},{80,96},{96,112},{112,0},{1... | collective-permute-start | bytes 294920 | tf_op jit(solution)/shard_map/ppermute | solution.py:32
  31.7 0.8 %shard_map.186.v.refs_0_.refs_1_ = f32[3,12,32,256]{3,2,1,0:T(8,128)S(1)} custom-call(f32[3,12,24,256]{3,2,1,0:T(8,128)S(1)} %copy-done.2, f32[6,12,24,256]{3,2,1,0:T(8,128)S(1)} %copy-done.1, f32[3,12,24,256]{3,2,1,0:T(8,128)S(1)} %copy-done, f32[12,12,8,256]{3,2,1,0:T(8,128)S(1)} %get-tuple-element.43.rim.refs_3_, ...), custom_call_target="tpu_custom_call" | custom-call | tf_op jit(solution)/shard_map/pallas_call | solution.py:21
  32.5 1.8 %collective-permute-done.11.xr.refs_4_ = f32[96,256]{1,0:T(8,128)S(1)} collective-permute-done((f32[96,256]{1,0:T(8,128)S(1)}, f32[96,256]{1,0:T(8,128)S(1)}, u32[]{:S(2)}, u32[]{:S(2)}) %collective-permute-start.11) | collective-permute-done | bytes 98336 | tf_op jit(solution)/shard_map/ppermute | solution.py:32
  35.3 3.4 %collective-permute-start.14 = (f32[96,256]{1,0:T(8,128)S(1)}, f32[96,256]{1,0:T(8,128)S(1)}, u32[]{:S(2)}, u32[]{:S(2)}) collective-permute-start(f32[96,256]{1,0:T(8,128)S(1)} %get-tuple-element.54), channel_id=1, source_target_pairs={{0,16},{16,32},{32,48},{48,64},{64,80},{80,96},{96,112},{112,0},{1... | collective-permute-start | bytes 294920 | tf_op jit(solution)/shard_map/ppermute | solution.py:32
  38.6 1.1 %shard_map.190 = (f32[6,12,32,256]{3,2,1,0:T(8,128)S(1)}, f32[32,128]{1,0:T(8,128)S(1)}) custom-call(f32[6,12,24,256]{3,2,1,0:T(8,128)S(1)} %copy-done.1, f32[3,12,32,256]{3,2,1,0:T(8,128)S(1)} %shard_map.186.v.refs_0_.refs_1_, f32[3,12,24,256]{3,2,1,0:T(8,128)S(1)} %copy-done, f32[12,12,8,256]{3,2,1,0:T(8,128)S(1)} %get-tuple-element.43.rim.refs_3_, ...), custom_call_target="tpu_custom_call" | custom-call | tf_op jit(solution)/shard_map/pallas_call | solution.py:21
  39.8 0.8 %shard_map.191.refs_1_.v.refs_0_ = f32[3,12,32,256]{3,2,1,0:T(8,128)S(1)} custom-call(f32[3,12,32,256]{3,2,1,0:T(8,128)S(1)} %shard_map.186.v.refs_0_.refs_1_, f32[6,12,32,256]{3,2,1,0:T(8,128)S(1)} %get-tuple-element.52.s.refs_0_, f32[3,12,24,256]{3,2,1,0:T(8,128)S(1)} %copy-done, f32[12,12,8,256]{3,2,1,0:T(8,128)S(1)} %get-tuple-element.43.rim.refs_3_, ...), custom_call_target="tpu_custom_call" | custom-call | tf_op jit(solution)/shard_map/pallas_call | solution.py:21
  41.1 1.3 %shard_map.192 = (f32[6,12,32,256]{3,2,1,0:T(8,128)S(1)}, f32[32,128]{1,0:T(8,128)S(1)}, f32[96,256]{1,0:T(8,128)S(1)}) custom-call(f32[6,12,32,256]{3,2,1,0:T(8,128)S(1)} %get-tuple-element.52.s.refs_0_, f32[3,12,32,256]{3,2,1,0:T(8,128)S(1)} %shard_map.191.refs_1_.v.refs_0_, f32[3,12,24,256]{3,2,1,0:T(8,128)S(1)} %copy-done, ...), custom_call_target="tpu_custom_call" | custom-call | tf_op jit(solution)/shard_map/pallas_call | solution.py:21
  42.9 3.1 %collective-permute-start.15 = (f32[24,128]{1,0:T(8,128)S(1)}, f32[24,128]{1,0:T(8,128)S(1)}, u32[]{:S(2)}, u32[]{:S(2)}) collective-permute-start(f32[24,128]{1,0:T(8,128)S(1)} %shard_map.193), channel_id=1, source_target_pairs={{0,1},{1,0},{2,3},{3,2},{4,5},{5,4},{6,7},{7,6},{8,9},{9,8},{10,11... | collective-permute-start | bytes 36872 | tf_op jit(solution)/shard_map/ppermute | solution.py:604
  46.1 0.8 %shard_map.194.refs_1_ = f32[3,12,32,256]{3,2,1,0:T(8,128)S(1)} custom-call(f32[3,12,32,256]{3,2,1,0:T(8,128)S(1)} %shard_map.191.refs_1_.v.refs_0_, f32[6,12,32,256]{3,2,1,0:T(8,128)S(1)} %get-tuple-element.56.s.refs_1_.refs_0_, f32[3,12,24,256]{3,2,1,0:T(8,128)S(1)} %copy-done, f32[12,12,8,256]{3,2,1,0:T(8,128)S(1)} %get-tuple-element.43.rim.refs_3_, ...), custom_call_target="tpu_custom_call" | custom-call | tf_op jit(solution)/shard_map/pallas_call | solution.py:21
  47.6 0.7 collective-permute-start.21
  48.2 0.7 collective-permute-start.20
  48.9 0.7 collective-permute-start.19
  49.6 0.7 collective-permute-start.18
  50.3 7.1 %collective-permute-start.17 = (f32[24,128]{1,0:T(8,128)S(1)}, f32[24,128]{1,0:T(8,128)S(1)}, u32[]{:S(2)}, u32[]{:S(2)}) collective-permute-start(f32[24,128]{1,0:T(8,128)S(1)} %add.52), channel_id=1, source_target_pairs={{9,5},{14,10},{25,21},{30,26},{41,37},{46,42},{57,53},{62,58},{73,... | collective-permute-start | bytes 36872 | tf_op jit(solution)/shard_map/ppermute | solution.py:611
  57.4 0.7 collective-permute-start.16
  58.3 1.9 %collective-permute-start.23 = (f32[24,128]{1,0:T(8,128)S(1)}, f32[24,128]{1,0:T(8,128)S(1)}, u32[]{:S(2)}, u32[]{:S(2)}) collective-permute-start(f32[24,128]{1,0:T(8,128)S(1)} %add_add_fusion.rest), channel_id=1, source_target_pairs={{0,112},{16,0},{32,16},{48,32},{64,48},{80,64},{96,80},{112,96},{1... | collective-permute-start | bytes 36872 | tf_op jit(solution)/shard_map/ppermute | solution.py:32
  60.3 3.3 %collective-permute-done.24.refs_4_ = f32[72,256]{1,0:T(8,128)S(1)} collective-permute-done((f32[72,256]{1,0:T(8,128)S(1)}, f32[72,256]{1,0:T(8,128)S(1)}, u32[]{:S(2)}, u32[]{:S(2)}) %collective-permute-start.24) | collective-permute-done | bytes 73760 | tf_op jit(solution)/shard_map/ppermute | solution.py:32
  63.6 2.2 %shard_map.196 = (f32[6,12,24,256]{3,2,1,0:T(8,128)}, f32[3,12,24,256]{3,2,1,0:T(8,128)}, f32[12,24]{1,0:T(8,128)}, f32[8,128]{1,0:T(8,128)S(1)}) custom-call(f32[6,12,32,256]{3,2,1,0:T(8,128)S(1)} %get-tuple-element.56.s.refs_1_.refs_0_, f32[3,12,32,256]{3,2,1,0:T(8,128)S(1)} %shard_map.194.refs_1_, f32[3,12,24,256]{3,2,1,0:T(8,128)S(1)} %copy-done, ...), custom_call_target="tpu_custom_call" | custom-call | tf_op jit(solution)/shard_map/pallas_call | solution.py:726
  65.8 0.8 %shard_map.197 = (f32[3,4,16,128]{3,2,1,0:T(8,128)}, f32[6,4,16,128]{3,2,1,0:T(8,128)}) custom-call(f32[3,4,16,128]{3,2,1,0:T(8,128)S(1)} %get-tuple-element.40.cv, f32[6,4,16,128]{3,2,1,0:T(8,128)S(1)} %get-tuple-element.41.cs, f32[3,4,16,128]{3,2,1,0:T(8,128)S(1)} %get-tuple-element.42.cm, f32[128,256]{1,0:T(8,128)S(1)} %collective-permute-done.13.refs_4_.xr, ...), custom_call_target="tpu_custom_call" | custom-call | tf_op jit(solution)/shard_map/pallas_call | solution.py:21
  (54 shorter events, 5.6 us)
Async XLA Ops:
  0.8 12.3 %copy-start = (f32[3,12,24,256]{3,2,1,0:T(8,128)S(1)}, f32[3,12,24,256]{3,2,1,0:T(8,128)}, u32[]{:S(2)}) copy-start(f32[3,12,24,256]{3,2,1,0:T(8,128)} %refs_2_.11) | copy-start | bytes 2654212
  0.8 12.3 %copy-start.1 = (f32[6,12,24,256]{3,2,1,0:T(8,128)S(1)}, f32[6,12,24,256]{3,2,1,0:T(8,128)}, u32[]{:S(2)}) copy-start(f32[6,12,24,256]{3,2,1,0:T(8,128)} %refs_0_.3) | copy-start | bytes 5308420
  0.8 12.3 %copy-start.3 = (f32[6,4,16,128]{3,2,1,0:T(8,128)S(1)}, f32[6,4,16,128]{3,2,1,0:T(8,128)}, u32[]{:S(2)}) copy-start(f32[6,4,16,128]{3,2,1,0:T(8,128)} %cs.5) | copy-start | bytes 589828
  3.1 9.3 %collective-permute-start.1 = (f32[528,256]{1,0:T(8,128)S(1)}, f32[528,256]{1,0:T(8,128)S(1)}, u32[]{:S(2)}, u32[]{:S(2)}) collective-permute-start(f32[528,256]{1,0:T(8,128)S(1)} %get-tuple-element.37), channel_id=1, source_target_pairs={{0,15},{1,0},{2,1},{3,2},{4,3},{5,4},{6,5},{7,6},{8,7},{9,8},{10,9... | collective-permute-start | bytes 1622024 | tf_op jit(solution)/shard_map/ppermute | solution.py:32
  3.9 6.6 %collective-permute-start = (f32[408,256]{1,0:T(8,128)S(1)}, f32[408,256]{1,0:T(8,128)S(1)}, u32[]{:S(2)}, u32[]{:S(2)}) collective-permute-start(f32[408,256]{1,0:T(8,128)S(1)} %get-tuple-element.36), channel_id=1, source_target_pairs={{0,1},{1,2},{2,3},{3,4},{4,5},{5,6},{6,7},{7,8},{8,9},{9,10},{10,1... | collective-permute-start | bytes 1253384 | tf_op jit(solution)/shard_map/ppermute | solution.py:32
  6.4 21.2 %copy-start.2 = (f32[3,12,24,256]{3,2,1,0:T(8,128)S(1)}, f32[3,12,24,256]{3,2,1,0:T(8,128)}, u32[]{:S(2)}) copy-start(f32[3,12,24,256]{3,2,1,0:T(8,128)} %refs_0_.2) | copy-start | bytes 2654212
  6.4 2.1 %collective-permute-start.9 = (f32[24,128]{1,0:T(8,128)S(1)}, f32[24,128]{1,0:T(8,128)S(1)}, u32[]{:S(2)}, u32[]{:S(2)}) collective-permute-start(f32[24,128]{1,0:T(8,128)S(1)} %shard_map.185), channel_id=1, source_target_pairs={{5,3},{10,8},{21,19},{26,24},{37,35},{42,40},{53,51},{58,56},{69,6... | collective-permute-start | bytes 36872 | tf_op jit(solution)/shard_map/ppermute | solution.py:611
  7.2 2.0 %collective-permute-start.8 = (f32[24,128]{1,0:T(8,128)S(1)}, f32[24,128]{1,0:T(8,128)S(1)}, u32[]{:S(2)}, u32[]{:S(2)}) collective-permute-start(f32[24,128]{1,0:T(8,128)S(1)} %shard_map.185), channel_id=1, source_target_pairs={{5,1},{10,6},{21,17},{26,22},{37,33},{42,38},{53,49},{58,54},{69,6... | collective-permute-start | bytes 36872 | tf_op jit(solution)/shard_map/ppermute | solution.py:611
  7.9 5.5 %collective-permute-start.7 = (f32[24,128]{1,0:T(8,128)S(1)}, f32[24,128]{1,0:T(8,128)S(1)}, u32[]{:S(2)}, u32[]{:S(2)}) collective-permute-start(f32[24,128]{1,0:T(8,128)S(1)} %shard_map.185), channel_id=1, source_target_pairs={{5,15},{10,4},{21,31},{26,20},{37,47},{42,36},{53,63},{58,52},{69,... | collective-permute-start | bytes 36872 | tf_op jit(solution)/shard_map/ppermute | solution.py:611
  8.6 5.3 %collective-permute-start.6 = (f32[24,128]{1,0:T(8,128)S(1)}, f32[24,128]{1,0:T(8,128)S(1)}, u32[]{:S(2)}, u32[]{:S(2)}) collective-permute-start(f32[24,128]{1,0:T(8,128)S(1)} %shard_map.185), channel_id=1, source_target_pairs={{5,13},{10,2},{21,29},{26,18},{37,45},{42,34},{53,61},{58,50},{69,... | collective-permute-start | bytes 36872 | tf_op jit(solution)/shard_map/ppermute | solution.py:611
  9.3 4.6 %collective-permute-start.5 = (f32[24,128]{1,0:T(8,128)S(1)}, f32[24,128]{1,0:T(8,128)S(1)}, u32[]{:S(2)}, u32[]{:S(2)}) collective-permute-start(f32[24,128]{1,0:T(8,128)S(1)} %shard_map.185), channel_id=1, source_target_pairs={{5,11},{10,0},{21,27},{26,16},{37,43},{42,32},{53,59},{58,48},{69,... | collective-permute-start | bytes 36872 | tf_op jit(solution)/shard_map/ppermute | solution.py:611
  10.5 15.9 %collective-permute-start.4 = (f32[24,128]{1,0:T(8,128)S(1)}, f32[24,128]{1,0:T(8,128)S(1)}, u32[]{:S(2)}, u32[]{:S(2)}) collective-permute-start(f32[24,128]{1,0:T(8,128)S(1)} %shard_map.185), channel_id=1, source_target_pairs={{5,9},{10,14},{21,25},{26,30},{37,41},{42,46},{53,57},{58,62},{69,... | collective-permute-start | bytes 36872 | tf_op jit(solution)/shard_map/ppermute | solution.py:611
  12.4 14.0 %collective-permute-start.3 = (f32[24,128]{1,0:T(8,128)S(1)}, f32[24,128]{1,0:T(8,128)S(1)}, u32[]{:S(2)}, u32[]{:S(2)}) collective-permute-start(f32[24,128]{1,0:T(8,128)S(1)} %shard_map.185), channel_id=1, source_target_pairs={{5,7},{10,12},{21,23},{26,28},{37,39},{42,44},{53,55},{58,60},{69,... | collective-permute-start | bytes 36872 | tf_op jit(solution)/shard_map/ppermute | solution.py:611
  13.4 14.2 %collective-permute-start.2 = (f32[208,256]{1,0:T(8,128)S(1)}, f32[208,256]{1,0:T(8,128)S(1)}, u32[]{:S(2)}, u32[]{:S(2)}) collective-permute-start(f32[208,256]{1,0:T(8,128)S(1)} %get-tuple-element.39), channel_id=1, source_target_pairs={{0,16},{16,32},{32,48},{48,64},{64,80},{80,96},{96,112},{112,0},{1... | collective-permute-start | bytes 638984 | tf_op jit(solution)/shard_map/ppermute | solution.py:32
  26.4 1.3 %collective-permute-start.10 = (f32[24,128]{1,0:T(8,128)S(1)}, f32[24,128]{1,0:T(8,128)S(1)}, u32[]{:S(2)}, u32[]{:S(2)}) collective-permute-start(f32[24,128]{1,0:T(8,128)S(1)} %add_add_fusion.1.bounds_a.refs_5_), channel_id=1, source_target_pairs={{0,1},{1,0},{2,3},{3,2},{4,5},{5,4},{6,7},{7,6},{8,9},{9,8},{10,11... | collective-permute-start | bytes 36872 | tf_op jit(solution)/shard_map/ppermute | solution.py:604
  27.7 3.9 %copy-start.4 = (f32[3,4,16,128]{3,2,1,0:T(8,128)S(1)}, f32[3,4,16,128]{3,2,1,0:T(8,128)}, u32[]{:S(2)}) copy-start(f32[3,4,16,128]{3,2,1,0:T(8,128)} %cv.5) | copy-start | bytes 294916
  27.7 3.9 %copy-start.5 = (f32[3,4,16,128]{3,2,1,0:T(8,128)S(1)}, f32[3,4,16,128]{3,2,1,0:T(8,128)}, u32[]{:S(2)}) copy-start(f32[3,4,16,128]{3,2,1,0:T(8,128)} %cm.3) | copy-start | bytes 294916
  27.7 3.9 %copy-start.6 = (s32[2,4,128]{2,1,0:T(4,128)S(1)}, s32[2,4,128]{2,1,0:T(4,128)}, u32[]{:S(2)}) copy-start(s32[2,4,128]{2,1,0:T(4,128)} %rows_ref.3) | copy-start | bytes 12292
  27.9 6.4 %collective-permute-start.11 = (f32[96,256]{1,0:T(8,128)S(1)}, f32[96,256]{1,0:T(8,128)S(1)}, u32[]{:S(2)}, u32[]{:S(2)}) collective-permute-start(f32[96,256]{1,0:T(8,128)S(1)} %get-tuple-element.44), channel_id=1, source_target_pairs={{0,112},{16,0},{32,16},{48,32},{64,48},{80,64},{96,80},{112,96},{1... | collective-permute-start | bytes 294920 | tf_op jit(solution)/shard_map/ppermute | solution.py:32
  28.0 6.3 %collective-permute-start.12 = (f32[96,256]{1,0:T(8,128)S(1)}, f32[96,256]{1,0:T(8,128)S(1)}, u32[]{:S(2)}, u32[]{:S(2)}) collective-permute-start(f32[96,256]{1,0:T(8,128)S(1)} %get-tuple-element.46), channel_id=1, source_target_pairs={{0,16},{16,32},{32,48},{48,64},{64,80},{80,96},{96,112},{112,0},{1... | collective-permute-start | bytes 294920 | tf_op jit(solution)/shard_map/ppermute | solution.py:32
  35.0 6.1 %collective-permute-start.13 = (f32[128,256]{1,0:T(8,128)S(1)}, f32[128,256]{1,0:T(8,128)S(1)}, u32[]{:S(2)}, u32[]{:S(2)}) collective-permute-start(f32[128,256]{1,0:T(8,128)S(1)} %get-tuple-element.50), channel_id=1, source_target_pairs={{0,112},{16,0},{32,16},{48,32},{64,48},{80,64},{96,80},{112,96},{1... | collective-permute-start | bytes 393224 | tf_op jit(solution)/shard_map/ppermute | solution.py:32
  35.3 5.3 %collective-permute-start.14 = (f32[96,256]{1,0:T(8,128)S(1)}, f32[96,256]{1,0:T(8,128)S(1)}, u32[]{:S(2)}, u32[]{:S(2)}) collective-permute-start(f32[96,256]{1,0:T(8,128)S(1)} %get-tuple-element.54), channel_id=1, source_target_pairs={{0,16},{16,32},{32,48},{48,64},{64,80},{80,96},{96,112},{112,0},{1... | collective-permute-start | bytes 294920 | tf_op jit(solution)/shard_map/ppermute | solution.py:32
  42.9 4.0 %collective-permute-start.15 = (f32[24,128]{1,0:T(8,128)S(1)}, f32[24,128]{1,0:T(8,128)S(1)}, u32[]{:S(2)}, u32[]{:S(2)}) collective-permute-start(f32[24,128]{1,0:T(8,128)S(1)} %shard_map.193), channel_id=1, source_target_pairs={{0,1},{1,0},{2,3},{3,2},{4,5},{5,4},{6,7},{7,6},{8,9},{9,8},{10,11... | collective-permute-start | bytes 36872 | tf_op jit(solution)/shard_map/ppermute | solution.py:604
  46.9 3.3 %collective-permute-start.22 = (f32[24,128]{1,0:T(8,128)S(1)}, f32[24,128]{1,0:T(8,128)S(1)}, u32[]{:S(2)}, u32[]{:S(2)}) collective-permute-start(f32[24,128]{1,0:T(8,128)S(1)} %add.52), channel_id=1, source_target_pairs={{3,5},{8,10},{19,21},{24,26},{35,37},{40,42},{51,53},{56,58},{67,6... | collective-permute-start | bytes 36872 | tf_op jit(solution)/shard_map/ppermute | solution.py:611
  47.6 9.8 %collective-permute-start.21 = (f32[24,128]{1,0:T(8,128)S(1)}, f32[24,128]{1,0:T(8,128)S(1)}, u32[]{:S(2)}, u32[]{:S(2)}) collective-permute-start(f32[24,128]{1,0:T(8,128)S(1)} %add.52), channel_id=1, source_target_pairs={{1,5},{6,10},{17,21},{22,26},{33,37},{38,42},{49,53},{54,58},{65,6... | collective-permute-start | bytes 36872 | tf_op jit(solution)/shard_map/ppermute | solution.py:611
  48.2 10.0 %collective-permute-start.20 = (f32[24,128]{1,0:T(8,128)S(1)}, f32[24,128]{1,0:T(8,128)S(1)}, u32[]{:S(2)}, u32[]{:S(2)}) collective-permute-start(f32[24,128]{1,0:T(8,128)S(1)} %add.52), channel_id=1, source_target_pairs={{15,5},{4,10},{31,21},{20,26},{47,37},{36,42},{63,53},{52,58},{79,... | collective-permute-start | bytes 36872 | tf_op jit(solution)/shard_map/ppermute | solution.py:611
  48.9 9.4 %collective-permute-start.19 = (f32[24,128]{1,0:T(8,128)S(1)}, f32[24,128]{1,0:T(8,128)S(1)}, u32[]{:S(2)}, u32[]{:S(2)}) collective-permute-start(f32[24,128]{1,0:T(8,128)S(1)} %add.52), channel_id=1, source_target_pairs={{13,5},{2,10},{29,21},{18,26},{45,37},{34,42},{61,53},{50,58},{77,... | collective-permute-start | bytes 36872 | tf_op jit(solution)/shard_map/ppermute | solution.py:611
  49.6 8.7 %collective-permute-start.18 = (f32[24,128]{1,0:T(8,128)S(1)}, f32[24,128]{1,0:T(8,128)S(1)}, u32[]{:S(2)}, u32[]{:S(2)}) collective-permute-start(f32[24,128]{1,0:T(8,128)S(1)} %add.52), channel_id=1, source_target_pairs={{11,5},{0,10},{27,21},{16,26},{43,37},{32,42},{59,53},{48,58},{75,... | collective-permute-start | bytes 36872 | tf_op jit(solution)/shard_map/ppermute | solution.py:611
  50.3 8.1 %collective-permute-start.17 = (f32[24,128]{1,0:T(8,128)S(1)}, f32[24,128]{1,0:T(8,128)S(1)}, u32[]{:S(2)}, u32[]{:S(2)}) collective-permute-start(f32[24,128]{1,0:T(8,128)S(1)} %add.52), channel_id=1, source_target_pairs={{9,5},{14,10},{25,21},{30,26},{41,37},{46,42},{57,53},{62,58},{73,... | collective-permute-start | bytes 36872 | tf_op jit(solution)/shard_map/ppermute | solution.py:611
  57.4 1.0 %collective-permute-start.16 = (f32[24,128]{1,0:T(8,128)S(1)}, f32[24,128]{1,0:T(8,128)S(1)}, u32[]{:S(2)}, u32[]{:S(2)}) collective-permute-start(f32[24,128]{1,0:T(8,128)S(1)} %add.52), channel_id=1, source_target_pairs={{7,5},{12,10},{23,21},{28,26},{39,37},{44,42},{55,53},{60,58},{71,... | collective-permute-start | bytes 36872 | tf_op jit(solution)/shard_map/ppermute | solution.py:611
  58.2 5.4 %collective-permute-start.24 = (f32[72,256]{1,0:T(8,128)S(1)}, f32[72,256]{1,0:T(8,128)S(1)}, u32[]{:S(2)}, u32[]{:S(2)}) collective-permute-start(f32[72,256]{1,0:T(8,128)S(1)} %shard_map.195), channel_id=1, source_target_pairs={{0,112},{16,0},{32,16},{48,32},{64,48},{80,64},{96,80},{112,96},{1... | collective-permute-start | bytes 221192 | tf_op jit(solution)/shard_map/ppermute | solution.py:32
  58.3 7.5 %collective-permute-start.23 = (f32[24,128]{1,0:T(8,128)S(1)}, f32[24,128]{1,0:T(8,128)S(1)}, u32[]{:S(2)}, u32[]{:S(2)}) collective-permute-start(f32[24,128]{1,0:T(8,128)S(1)} %add_add_fusion.rest), channel_id=1, source_target_pairs={{0,112},{16,0},{32,16},{48,32},{64,48},{80,64},{96,80},{112,96},{1... | collective-permute-start | bytes 36872 | tf_op jit(solution)/shard_map/ppermute | solution.py:32
